TPU v7x, 512 devices: a whole 4x4x16 slice. The times are simulated.
512 devices in a mesh: row: 8 (over y, x_hi), col: 16 (over z), occ: 4 (over x_lo, core).
Axes of the slice: x: 4 (x_hi: 2, x_lo: 2; x = x_hi * 2 + x_lo), y: 4, z: 16, core: 2. Of those that a mesh axis runs over, the one named last changes fastest.
Arguments:
- amplitudes: float32 [512, 3, 512], P(('row', 'col'), None, 'occ'), may hold values from -24 to 24
- integrals: float32 [3, 512, 512, 512], P(None, 'occ', ('row', 'col')), may hold values from -0.4375 to 0.4375
- orbital_irrep: int32 [512], replicated, may hold values from 0 to 7
- slab_irrep: int32 [3], replicated, may hold values from 0 to 7
- pair_irrep: int32 [512], replicated, may hold values from 0 to 7
Outputs:
- residual: float32 [512, 512, 512], P('occ', ('row', 'col'))
Inputs may be any that keep to these rules, and one draw needn't show every extreme that they name: `orbital_irrep`: labels of the 8 irreps. `slab_irrep`: labels of the 8 irreps. `pair_irrep`: labels of the 8 irreps.
All inputs are finite; a program needn't handle non-finite values.
Results may differ from a plain program's by a relative error of at most 0.00007.
Values sent between devices are 32-bit elements; how exact they have to be, the bound alone decides.
No kernel may reach another device: no remote copies, remote signals or barrier semaphores. Data moves between devices by JAX's collectives and lax.ppermute only.
A program may use at most 128 MiB of HBM per device.

v0:
```python
import jax
import jax.numpy as jnp
from jax import lax
from jax.sharding import PartitionSpec as P


def on_device(amplitudes, integrals, orbital_irrep, slab_irrep, pair_irrep):
    slab_count, local_depth, local_rows, orbitals = integrals.shape
    pair_count = pair_irrep.shape[0]
    groups = lax.axis_size("occ")
    quarter = pair_count // groups
    row_offset = lax.axis_index(("row", "col")) * local_rows
    depth_offset = lax.axis_index("occ") * local_depth
    pair_offset = lax.axis_index("occ") * quarter
    own_labels = lax.dynamic_slice_in_dim(pair_irrep, pair_offset, quarter, 0)
    gathered = lax.all_gather(amplitudes, ("row", "col"), axis=0, tiled=True)
    depth_labels = lax.dynamic_slice_in_dim(orbital_irrep, depth_offset, local_depth, 0)
    allowed = jnp.bitwise_xor(slab_irrep[:, None], depth_labels[None, :])
    flat_panel = integrals.reshape(slab_count * local_depth, local_rows * orbitals)
    masked = jnp.where(allowed[None, :, :] == pair_irrep[:, None, None], gathered, 0.0)
    flat_ladder = lax.psum_scatter(
        jnp.dot(
            masked.reshape(quarter * lax.axis_size("occ"), slab_count * local_depth),
            flat_panel,
            precision=lax.Precision.HIGHEST,
            preferred_element_type=jnp.float32,
        ),
        "occ",
        scatter_dimension=0,
        tiled=True,
    )
    row_labels = lax.dynamic_slice_in_dim(orbital_irrep, row_offset, local_rows, 0)
    block_labels = jnp.bitwise_xor(row_labels[:, None], orbital_irrep[None, :])
    ladder = flat_ladder.reshape(quarter, local_rows, orbitals)
    ladder = jnp.where(block_labels[None, :, :] == own_labels[:, None, None], ladder, 0.0)
    pairs_last = jnp.transpose(ladder, (1, 2, 0))
    mirrored = lax.all_to_all(pairs_last, ("row", "col"), split_axis=1, concat_axis=0, tiled=True)
    swapped = jnp.transpose(mirrored, (2, 1, 0))
    return ladder - swapped


def solution(mesh):
    placed = (P(("row", "col"), None, "occ"), P(None, "occ", ("row", "col"), None), P(), P(), P())
    return jax.shard_map(
        on_device,
        mesh=mesh,
        in_specs=placed,
        out_specs=P("occ", ("row", "col"), None),
        check_vma=False,
    )
```

profile of v0, /device:TPU:64, one launch (start us, length us, event | category | flops | bytes accessed | tf_op | source)
XLA Modules:
  0.0 515.5 jit_solution(13527111317932373883)
XLA Ops:
  6.5 0.0 reduce-scatter.2.cloned.1.call-start
  6.5 0.7 copy.11
  7.2 359.6 %all_gather.3 = f32[512,3,128]{2,1,0:T(4,128)S(1)} all-gather(f32[4,3,128]{2,1,0:T(4,128)S(1)} %copy.11), channel_id=1, replica_groups=mesh['row'=8,'col'=16,'occ'=4] {'row','col'}, dimensions={0}, use_global_device_ids=true | all-gather | bytes 792576 | tf_op jit(solution)/shard_map/all_gather | solution.py:16
  366.9 1.2 copy.12
  368.1 0.0 copy-start.1
  368.1 0.0 copy-start.2
  368.1 0.0 copy-start
  368.1 3.3 copy.19
  371.4 0.0 copy-done.1
  371.4 0.1 dynamic_slice.11
  371.5 0.0 copy-done.2
  371.5 0.1 broadcast_xor_fusion.1
  371.6 0.0 copy-done
  371.6 1.2 compare_select_fusion.1
  372.8 8.4 %fusion.2 = f32[512,2048]{1,0:T(8,128)} fusion(f32[512,384]{0,1:T(8,128)S(1)} %bitcast.18, f32[384,2048]{1,0:T(8,128)S(1)} %bitcast.15), kind=kOutput, calls=%fused_computation.6 | convolution fusion | flops 4831838208 | bytes 8126464 | tf_op jit(solution)/shard_map/dot_general | solution.py:22
  381.2 0.0 reduce-scatter.2.cloned.1.call-update
  381.3 0.1 dynamic_slice.10
  381.3 0.1 dynamic_slice.9
  381.4 0.1 broadcast_xor_fusion
  381.5 45.9 %reduce-scatter.2.cloned.1.call-done = f32[128,2048]{1,0:T(8,128)} async-done(((f32[512,2048]{1,0:T(8,128)}), f32[128,2048]{1,0:T(8,128)}) %reduce-scatter.2.cloned.1.call-update) | async-done | bytes 1048592 | tf_op jit(solution)/shard_map/reduce_scatter | solution.py:21
  427.4 1.5 copy.18
  428.9 0.3 fusion.1
  429.3 0.7 copy.14
  430.0 76.2 %all_to_all.18 = f32[4,512,128]{2,0,1:T(4,128)S(1)} all-to-all(f32[4,512,128]{2,0,1:T(4,128)S(1)} %copy.14), channel_id=1, replica_groups=mesh['row'=8,'col'=16,'occ'=4] {'row','col'}, dimensions={1} | all-to-all | bytes 2097152 | tf_op jit(solution)/shard_map/all_to_all | solution.py:37
  506.2 0.1 copy.15
  506.3 0.7 copy.16
  506.9 0.3 fusion
  507.3 1.4 copy.17
Async XLA Ops:
  6.5 420.9 %reduce-scatter.2.cloned.1.call-start = ((), (), s32[]{:S(2)}) async-start(), calls=%async_computation.2 | async-start | bytes 5242880 | tf_op jit(solution)/shard_map/reduce_scatter | solution.py:21
  368.1 3.4 copy-start.1
  368.1 3.4 copy-start.2
  368.1 3.5 copy-start
Sparse Core Ops, SparseCore 0:
  381.4 45.9 reduce-scatter.1
where the time goes:
time: 516 us
  blocking collectives  436 us (84%)
  waiting for transfers between devices  45.9 us (9%)
  between operations  13.5 us (3%)
  local copies, waits for them, and re-layouts  9.81 us (2%)
  matrix products  8.41 us (2%)
    all_gather x1, blocking collectives, on_device(): gathered = lax.all_gather(amplitudes, ('row', 'col'), axis=0, tiled=True)  360 us
    all_to_all x1, blocking collectives, on_device(): lax.all_to_all(pairs_last, ('row', 'col'), split_axis=1, concat_axis=0, t...  76.2 us
    reduce_scatter x1, waiting for transfers between devices, on_device(): lax.psum_scatter(jnp.dot(masked.reshape(quarter * lax.axis_size('occ'), s...  45.9 us
  transfers between devices with their start and end apart: 1, of which 1 were waited for; matrix products, arithmetic and copies ran while one was open for 0% of the time, Pallas kernels for 0%

commit v1 on v0

v1 whole, which is shorter than its diff:
```python
import functools

import jax
import jax.numpy as jnp
import numpy as np
from jax import lax
from jax.experimental import pallas as pl
from jax.experimental.pallas import tpu as pltpu
from jax.sharding import Mesh
from jax.sharding import PartitionSpec as P

SLOTS = 32
LANES = 128
VMEM = pl.BlockSpec(memory_space=pltpu.VMEM)
SMEM = pl.BlockSpec(memory_space=pltpu.SMEM)


def split(x):
    high = x.astype(jnp.bfloat16)
    return high, (x - high.astype(jnp.float32)).astype(jnp.bfloat16)


def dot(x, y):
    return jnp.dot(x, y, preferred_element_type=jnp.float32)


def column_of(row):
    return jnp.transpose(jnp.broadcast_to(row, (LANES, LANES)))


def ladder_kernel(place, slab, orbital_s, orbital, pair, gathered, integrals, keep, send, high_t, low_t):
    block, occ, core, shift = place[0], place[1], place[2], place[3]
    depth_row = orbital[pl.ds(occ, 1), :]
    depth_rows = [depth_row ^ slab[c] for c in range(3)]
    before = lax.broadcasted_iota(jnp.int32, (LANES, LANES), 0) < lax.broadcasted_iota(jnp.int32, (LANES, LANES), 1)
    slot = lax.broadcasted_iota(jnp.int32, (SLOTS, LANES), 0) + shift
    for half in range(2):
        for x in range(2):
            quarter = 2 * x + (core ^ half)
            row = pair[pl.ds(quarter, 1), :]
            column = column_of(row)
            rank = jnp.sum(jnp.where((column == row) & before, 1, 0), axis=0, keepdims=True)
            pick = jnp.where(slot == rank, 1.0, 0.0).astype(jnp.bfloat16)
            at = (half * 2 + x) * SLOTS
            for c in range(3):
                part = gathered[pl.ds(pl.multiple_of(quarter * LANES, LANES), LANES), c * LANES : (c + 1) * LANES]
                high, low = split(jnp.where(column == depth_rows[c], part, 0.0))
                high_t[at : at + SLOTS, c * LANES : (c + 1) * LANES] = dot(pick, high).astype(jnp.bfloat16)
                low_t[at : at + SLOTS, c * LANES : (c + 1) * LANES] = dot(pick, low).astype(jnp.bfloat16)
    depth_columns = jnp.concatenate([column_of(r) for r in depth_rows], axis=0)
    t_high, t_low = high_t[...], low_t[...]
    for y in range(4):
        lanes = orbital[y : y + 1, :]
        for i in range(4):
            panel = integrals[pl.ds(y * 4 + i, 3 * LANES, stride=16), :]
            label = lanes ^ orbital_s[block * 4 + i]
            v_high, v_low = split(jnp.where(depth_columns == label, panel, 0.0))
            total = dot(t_high, v_high) + dot(t_high, v_low) + dot(t_low, v_high)
            for half, out in ((0, keep), (1, send)):
                for x in range(2):
                    at = (half * 2 + x) * SLOTS
                    out[pl.ds((x * 4 + y) * 4 * SLOTS + i, SLOTS, stride=4), :] = total[at : at + SLOTS]


def turn_kernel(arrived, out):
    size = 4 * SLOTS
    for i in range(4):
        rows = []
        for y in range(4):
            rows.append(
                arrived[pl.ds(y * size + i, SLOTS, stride=4), :] + arrived[pl.ds((4 + y) * size + i, SLOTS, stride=4), :]
            )
        out[pl.ds(i, LANES, stride=4), :] = jnp.transpose(jnp.concatenate(rows, axis=0))


def spread_kernel(first, place, slots, labels, orbital_s, orbital, summed, other, swapped, *rest):
    out, turned, packed = rest[-3:]
    block, x, shift = place[0], place[4], place[3]
    size = 4 * SLOTS
    for j in range(4):
        for s in range(32):
            turned[j * LANES + s * 4 : j * LANES + s * 4 + 4, :] = swapped[s * 16 + j * 4 : s * 16 + j * 4 + 4, :]
    for j in range(4):
        mirrored = jnp.transpose(turned[j * LANES : (j + 1) * LANES, :])
        for y in range(4):
            own = summed[pl.ds(x * 4 * size + y * size + j, SLOTS, stride=4), :]
            own = own + other[pl.ds(y * size + j, SLOTS, stride=4), :]
            packed[pl.ds(y * 4 + j, SLOTS, stride=16), :] = own - mirrored[y * SLOTS : (y + 1) * SLOTS]
    rows = []
    for y in range(4):
        for j in range(4):
            rows.append(orbital[y : y + 1, :] ^ orbital_s[block * 4 + j])
    entry = jnp.concatenate(rows, axis=0)

    def step(p, carry):
        slot = slots[p] - shift
        inside = (slot >= 0) & (slot < SLOTS)
        spot = pl.multiple_of(jnp.clip(slot, 0, SLOTS - 1) * 16, 16)
        values = packed[pl.ds(spot, 16), :]
        where = pl.ds(pl.multiple_of(p * 16, 16), 16)
        if first:
            out[where, :] = jnp.where((entry == labels[p]) & inside, values, 0.0)
        else:

            @pl.when(inside)
            def _():
                out[where, :] = jnp.where(entry == labels[p], values, 0.0)

        return carry

    if not first:
        out[...] = rest[0][...]
    lax.fori_loop(0, LANES, step, 0, unroll=4)


def on_device(amplitudes, integrals, orbital_irrep, slab_irrep, pair_irrep):
    y, xh, z = lax.axis_index("y"), lax.axis_index("xh"), lax.axis_index("z")
    x, core = lax.axis_index("xl"), lax.axis_index("core")
    block, occ = (y * 2 + xh) * 16 + z, x * 2 + core
    params = pltpu.CompilerParams(vmem_limit_bytes=40 * 1024 * 1024)

    mine = amplitudes.reshape(4, 384)
    near = lax.all_to_all(jnp.broadcast_to(mine[None], (16, 4, 384)), "z", 0, 0, tiled=True)
    near = jnp.broadcast_to(near.reshape(1, 64, 384), (8, 64, 384))
    gathered = lax.all_to_all(near, ("y", "xh"), 0, 0, tiled=True).reshape(512, 384)

    panel = integrals.reshape(3, LANES, 4, 4, LANES).transpose(0, 1, 3, 2, 4).reshape(3 * LANES * 16, LANES)
    orbital = orbital_irrep.reshape(4, LANES)
    pair = pair_irrep.reshape(4, LANES)
    same = pair[:, :, None] == pair[:, None, :]
    earlier = jnp.arange(LANES)[:, None] < jnp.arange(LANES)[None, :]
    ranks = jnp.sum(same & earlier[None], axis=1, dtype=jnp.int32)
    rounds = jnp.max(ranks) // SLOTS + 1
    slots = lax.dynamic_slice_in_dim(ranks, occ, 1, 0)[0]
    labels = lax.dynamic_slice_in_dim(pair, occ, 1, 0)[0]

    def one_round(turn, previous):
        place = jnp.stack([block, occ, core, turn * SLOTS, x]).astype(jnp.int32)
        keep, send = pl.pallas_call(
            ladder_kernel,
            out_shape=[jax.ShapeDtypeStruct((8 * 4 * SLOTS, LANES), jnp.float32)] * 2,
            in_specs=[SMEM] * 3 + [VMEM] * 4,
            out_specs=[VMEM] * 2,
            scratch_shapes=[pltpu.VMEM((4 * SLOTS, 384), jnp.bfloat16)] * 2,
            compiler_params=params,
            name="ladder",
        )(place, slab_irrep, orbital_irrep, orbital, pair, gathered, panel)
        arrived = lax.ppermute(send, "core", [(0, 1), (1, 0)])
        summed = keep + arrived
        half = 16 * SLOTS
        other = lax.ppermute(lax.dynamic_slice_in_dim(summed, (1 - x) * half, half, 0), "xl", [(0, 1), (1, 0)])
        columns = lax.all_to_all(summed, ("xl", "y"), 0, 0, tiled=True)
        turned = pl.pallas_call(
            turn_kernel,
            out_shape=jax.ShapeDtypeStruct((512, LANES), jnp.float32),
            in_specs=[VMEM],
            out_specs=VMEM,
            compiler_params=params,
            name="turn",
        )(columns)
        swapped = lax.all_to_all(turned, ("xh", "z"), 0, 0, tiled=True)
        first = previous is None
        operands = [place, slots, labels, orbital_irrep, orbital, summed, other, swapped]
        operands += [] if first else [previous]
        return pl.pallas_call(
            functools.partial(spread_kernel, first),
            out_shape=jax.ShapeDtypeStruct((LANES * 16, LANES), jnp.float32),
            in_specs=[SMEM] * 4 + [VMEM] * (len(operands) - 4),
            out_specs=VMEM,
            scratch_shapes=[pltpu.VMEM((512, LANES), jnp.float32), pltpu.VMEM((16 * SLOTS, LANES), jnp.float32)],
            compiler_params=params,
            name="spread",
        )(*operands)

    filled = one_round(jnp.int32(0), None)
    _, filled = lax.while_loop(
        lambda state: state[0] < rounds,
        lambda state: (state[0] + 1, one_round(state[0], state[1])),
        (jnp.int32(1), filled),
    )
    return filled.reshape(LANES, 4, 4, LANES).transpose(0, 2, 1, 3).reshape(LANES, 4, 512)


def solution(mesh):
    devices = np.asarray(mesh.devices).reshape(4, 2, 16, 2, 2)
    fine = Mesh(devices, ("y", "xh", "z", "xl", "core"))
    blocks, groups = ("y", "xh", "z"), ("xl", "core")
    placed = (P(blocks, None, groups), P(None, groups, blocks, None), P(), P(), P())
    return jax.shard_map(
        on_device,
        mesh=fine,
        in_specs=placed,
        out_specs=P(groups, blocks, None),
        check_vma=False,
    )
```

time: 516 us -> 104 us (0.20)
  the two profiles are of different devices: /device:TPU:64 before, /device:TPU:2 now
where the time goes in v1:
time: 104 us; the launch traced here: 103 us
  blocking collectives  41.6 us (40%)
  waiting for transfers between devices  30.3 us (29%)
  starting transfers between devices  17 us (16%)
  Pallas kernels  7.36 us (7%)
  local copies, waits for them, and re-layouts  3.65 us (4%)
  between operations  2.39 us (2%)
    all_to_all x1, blocking collectives, on_device(): lax.all_to_all(jnp.broadcast_to(mine[None], (16, 4, 384)), 'z', 0, 0, til...  28.6 us
    all_to_all x1, blocking collectives, one_round(): columns = lax.all_to_all(summed, ('xl', 'y'), 0, 0, tiled=True)  13 us
    all_to_all x1, waiting for transfers between devices, one_round(): swapped = lax.all_to_all(turned, ('xh', 'z'), 0, 0, tiled=True)  12.8 us
    all_to_all x1, waiting for transfers between devices, on_device(): lax.all_to_all(near, ('y', 'xh'), 0, 0, tiled=True).reshape(512, 384)  12.5 us
    all_to_all x1, starting transfers between devices, on_device(): lax.all_to_all(near, ('y', 'xh'), 0, 0, tiled=True).reshape(512, 384)  6.03 us
    all_to_all x1, starting transfers between devices, one_round(): swapped = lax.all_to_all(turned, ('xh', 'z'), 0, 0, tiled=True)  5.3 us
    pallas_call x1, Pallas kernels, one_round(): pl.pallas_call(ladder_kernel, out_shape=[jax.ShapeDtypeStruct((8 * 4 * SL...  5.04 us
    ppermute x1, starting transfers between devices, one_round(): lax.ppermute(lax.dynamic_slice_in_dim(summed, (1 - x) * half, half, 0), '...  3.78 us
  transfers between devices with their start and end apart: 4, of which 4 were waited for; matrix products, arithmetic and copies ran while one was open for 1% of the time, Pallas kernels for 0%

profile of v1, /device:TPU:2, one launch (start us, length us, event | category | flops | bytes accessed | tf_op | source)
XLA Modules:
  0.0 103.2 jit_solution(3075552557948281468)
XLA Ops:
  0.0 0.7 broadcast_in_dim.18
  0.7 28.6 %all_to_all.52 = f32[16,4,384]{2,1,0:T(4,128)S(1)} all-to-all(f32[16,4,384]{2,1,0:T(4,128)S(1)} %broadcast_in_dim.18), channel_id=1, replica_groups=mesh['y'=4,'xh'=2,'z'=16,'xl'=2,'core'=2] {'z'}, dimensions={0} | all-to-all | bytes 196608 | tf_op jit(solution)/shard_map/all_to_all | solution.py:123
  29.3 0.9 broadcast_in_dim.20
  30.2 6.0 %all-to-all-start.3 = ((f32[8,64,384]{2,1,0:T(8,128)}), f32[8,64,384]{2,1,0:T(8,128)}, u32[]{:S(2)}, u32[]{:S(2)}) async-start(f32[8,64,384]{2,1,0:T(8,128)} %broadcast_in_dim.20), calls=%async_computation.3 | async-start | bytes 1572864 | tf_op jit(solution)/shard_map/all_to_all | solution.py:125
  36.3 0.1 stack.47.place
  36.4 12.5 %all-to-all-done.3 = f32[8,64,384]{2,1,0:T(8,128)} async-done(((f32[8,64,384]{2,1,0:T(8,128)}), f32[8,64,384]{2,1,0:T(8,128)}, u32[]{:S(2)}, u32[]{:S(2)}) %all-to-all-start.3) | async-done | bytes 786464 | tf_op jit(solution)/shard_map/all_to_all | solution.py:125
  48.8 5.0 %ladder.4 = (f32[1024,128]{1,0:T(8,128)S(1)}, f32[1024,128]{1,0:T(8,128)S(1)}) custom-call(s32[5]{0:T(128)S(1)} %stack.47.place, s32[3]{0:T(128)} %slab.1, s32[512]{0:T(512)} %orbital_s.3, s32[4,128]{1,0:T(4,128)} %bitcast.62, s32[4,128]{1,0:T(4,128)} %bitcast.68, f32[512,384]{1,0:T(8,128)} %bitcast.18.gathered, f32[6144,128]{1,0:T(8,128)} %bitcast.58), custom_call_target="tpu_custom_call" | custom-call | tf_op jit(solution)/shard_map/ladder/pallas_call | solution.py:139
  53.9 0.0 copy-start.1
  53.9 0.0 copy-start
  53.9 1.9 %collective-permute-start.2 = (f32[1024,128]{1,0:T(8,128)S(1)}, f32[1024,128]{1,0:T(8,128)S(1)}, u32[]{:S(2)}, u32[]{:S(2)}) collective-permute-start(f32[1024,128]{1,0:T(8,128)S(1)} %get-tuple-element.183), channel_id=1, source_target_pairs={{0,1},{1,0},{2,3},{3,2},{4,5},{5,4},{6,7},{7,6},{8,9},{9,8},{10,11... | collective-permute-start | bytes 1572872 | tf_op jit(solution)/shard_map/ppermute | solution.py:148
  55.8 1.9 %collective-permute-done.2 = f32[1024,128]{1,0:T(8,128)S(1)} collective-permute-done((f32[1024,128]{1,0:T(8,128)S(1)}, f32[1024,128]{1,0:T(8,128)S(1)}, u32[]{:S(2)}, u32[]{:S(2)}) %collective-permute-start.2) | collective-permute-done | bytes 524320 | tf_op jit(solution)/shard_map/ppermute | solution.py:148
  57.7 0.0 copy-start.2
  57.7 0.1 add.38.summed
  57.8 13.0 %all_to_all.53 = f32[8,128,128]{2,1,0:T(8,128)S(1)} all-to-all(f32[8,128,128]{2,1,0:T(8,128)S(1)} %bitcast.55), channel_id=1, replica_groups=mesh['y'=4,'xh'=2,'z'=16,'xl'=2,'core'=2] {'xl','y'}, dimensions={0} | all-to-all | bytes 1048576 | tf_op jit(solution)/shard_map/all_to_all | solution.py:152
  70.8 0.8 turn.4
  71.6 5.3 %all-to-all-start.5 = ((f32[32,16,128]{2,1,0:T(8,128)}), f32[32,16,128]{2,1,0:T(8,128)S(1)}, u32[]{:S(2)}, u32[]{:S(2)}) async-start(f32[32,16,128]{2,1,0:T(8,128)} %bitcast.24), calls=%async_computation.5 | async-start | bytes 524288 | tf_op jit(solution)/shard_map/all_to_all | solution.py:161
  77.0 3.8 %collective-permute-start.3 = (f32[512,128]{1,0:T(8,128)S(1)}, f32[512,128]{1,0:T(8,128)S(1)}, u32[]{:S(2)}, u32[]{:S(2)}) collective-permute-start(f32[512,128]{1,0:T(8,128)S(1)} %constant_dynamic-slice_fusion.1), channel_id=1, source_target_pairs={{0,2},{2,0},{1,3},{3,1},{4,6},{6,4},{5,7},{7,5},{8,10},{10,8},{9,1... | collective-permute-start | bytes 786440 | tf_op jit(solution)/shard_map/ppermute | solution.py:151
  80.8 0.0 copy-done.1
  80.8 0.1 convert_reduce_fusion
  80.9 0.6 reduce_max.9
  83.9 3.1 %collective-permute-done.3.other = f32[512,128]{1,0:T(8,128)S(1)} collective-permute-done((f32[512,128]{1,0:T(8,128)S(1)}, f32[512,128]{1,0:T(8,128)S(1)}, u32[]{:S(2)}, u32[]{:S(2)}) %collective-permute-start.3) | collective-permute-done | bytes 262176 | tf_op jit(solution)/shard_map/ppermute | solution.py:151
  87.0 12.8 %all-to-all-done.5 = f32[32,16,128]{2,1,0:T(8,128)S(1)} async-done(((f32[32,16,128]{2,1,0:T(8,128)}), f32[32,16,128]{2,1,0:T(8,128)S(1)}, u32[]{:S(2)}, u32[]{:S(2)}) %all-to-all-start.5) | async-done | bytes 262176 | tf_op jit(solution)/shard_map/all_to_all | solution.py:161
  99.8 0.0 copy-done
  99.8 1.5 %spread.4 = f32[2048,128]{1,0:T(8,128)S(1)} custom-call(s32[5]{0:T(128)S(1)} %stack.47.place, s32[128]{0:T(128)S(1)} %get-tuple-element.335.slots, s32[128]{0:T(128)S(1)} %get-tuple-element.336.labels, s32[512]{0:T(512)S(1)} %copy-done, s32[4,128]{1,0:T(4,128)S(1)} %bitcast.63, f32[1024,128]{1,0:T(8,128)S(1)} %add.38.summed, ...), custom_call_target="tpu_custom_call" | custom-call | tf_op jit(solution)/shard_map/spread/pallas_call | solution.py:165
  101.3 0.0 copy-done.2
  101.3 0.3 copy.11
  101.6 1.6 %reshape.57 = f32[128,4,512]{2,1,0:T(4,128)} reshape(f32[128,4,4,128]{3,2,1,0:T(4,128)S(1)} %bitcast.61) | data formatting | bytes 2097152 | tf_op jit(solution)/shard_map/reshape | solution.py:181
  (5 shorter events, 0.1 us)
Async XLA Ops:
  30.2 18.6 %all-to-all-start.3 = ((f32[8,64,384]{2,1,0:T(8,128)}), f32[8,64,384]{2,1,0:T(8,128)}, u32[]{:S(2)}, u32[]{:S(2)}) async-start(f32[8,64,384]{2,1,0:T(8,128)} %broadcast_in_dim.20), calls=%async_computation.3 | async-start | bytes 1572864 | tf_op jit(solution)/shard_map/all_to_all | solution.py:125
  53.9 26.9 %copy-start.1 = (s32[512]{0:T(512)S(1)}, s32[512]{0:T(512)}, u32[]{:S(2)}) copy-start(s32[512]{0:T(512)} %param.11) | copy-start | bytes 6148
  53.9 45.9 %copy-start = (s32[512]{0:T(512)S(1)}, s32[512]{0:T(512)}, u32[]{:S(2)}) copy-start(s32[512]{0:T(512)} %orbital_s.3) | copy-start | bytes 6148
  53.9 3.8 %collective-permute-start.2 = (f32[1024,128]{1,0:T(8,128)S(1)}, f32[1024,128]{1,0:T(8,128)S(1)}, u32[]{:S(2)}, u32[]{:S(2)}) collective-permute-start(f32[1024,128]{1,0:T(8,128)S(1)} %get-tuple-element.183), channel_id=1, source_target_pairs={{0,1},{1,0},{2,3},{3,2},{4,5},{5,4},{6,7},{7,6},{8,9},{9,8},{10,11... | collective-permute-start | bytes 1572872 | tf_op jit(solution)/shard_map/ppermute | solution.py:148
  57.7 43.6 %copy-start.2 = (s32[3]{0:T(128)S(1)}, s32[3]{0:T(128)}, u32[]{:S(2)}) copy-start(s32[3]{0:T(128)} %slab.1) | copy-start | bytes 40
  71.6 28.2 %all-to-all-start.5 = ((f32[32,16,128]{2,1,0:T(8,128)}), f32[32,16,128]{2,1,0:T(8,128)S(1)}, u32[]{:S(2)}, u32[]{:S(2)}) async-start(f32[32,16,128]{2,1,0:T(8,128)} %bitcast.24), calls=%async_computation.5 | async-start | bytes 524288 | tf_op jit(solution)/shard_map/all_to_all | solution.py:161
  77.0 10.0 %collective-permute-start.3 = (f32[512,128]{1,0:T(8,128)S(1)}, f32[512,128]{1,0:T(8,128)S(1)}, u32[]{:S(2)}, u32[]{:S(2)}) collective-permute-start(f32[512,128]{1,0:T(8,128)S(1)} %constant_dynamic-slice_fusion.1), channel_id=1, source_target_pairs={{0,2},{2,0},{1,3},{3,1},{4,6},{6,4},{5,7},{7,5},{8,10},{10,8},{9,1... | collective-permute-start | bytes 786440 | tf_op jit(solution)/shard_map/ppermute | solution.py:151

commit v2 on v1

v2 whole, which is shorter than its diff:
```python
import functools

import jax
import jax.numpy as jnp
import numpy as np
from jax import lax
from jax.experimental import pallas as pl
from jax.experimental.pallas import tpu as pltpu
from jax.sharding import Mesh
from jax.sharding import PartitionSpec as P

SLOTS = 32
LANES = 128
VMEM = pl.BlockSpec(memory_space=pltpu.VMEM)
SMEM = pl.BlockSpec(memory_space=pltpu.SMEM)


def split(x):
    high = x.astype(jnp.bfloat16)
    return high, (x - high.astype(jnp.float32)).astype(jnp.bfloat16)


def dot(x, y):
    return jnp.dot(x, y, preferred_element_type=jnp.float32)


def column_of(row):
    return jnp.transpose(jnp.broadcast_to(row, (LANES, LANES)))


def prepare_kernel(place, slab, orbital_s, orbital, pair, integrals, high, low, columns):
    block, occ = place[0], place[1]
    depth_row = orbital[pl.ds(occ, 1), :]
    depth = jnp.concatenate([column_of(depth_row ^ slab[c]) for c in range(3)], axis=0)
    for y in range(4):
        lanes = orbital[y : y + 1, :]
        for i in range(4):
            panel = integrals[pl.ds(y * 4 + i, 3 * LANES, stride=16), :]
            label = lanes ^ orbital_s[block * 4 + i]
            at = (y * 4 + i) * LANES
            high[:, at : at + LANES], low[:, at : at + LANES] = split(jnp.where(depth == label, panel, 0.0))
    for q in range(4):
        columns[q * LANES : (q + 1) * LANES, :] = column_of(pair[q : q + 1, :])


def ladder_kernel(place, slab, orbital, ranks, columns, gathered, v_high, v_low, keep, send, both_t):
    occ, core, shift = place[1], place[2], place[3]
    depth_row = orbital[pl.ds(occ, 1), :]
    depth_rows = [depth_row ^ slab[c] for c in range(3)]
    slot = lax.broadcasted_iota(jnp.int32, (SLOTS, LANES), 0) + shift
    for half in range(2):
        for x in range(2):
            quarter = 2 * x + (core ^ half)
            pick = jnp.where(slot == ranks[pl.ds(quarter, 1), :], 1.0, 0.0).astype(jnp.bfloat16)
            pairs = pl.ds(pl.multiple_of(quarter * LANES, LANES), LANES)
            column = columns[pairs, :]
            at = (half * 2 + x) * SLOTS
            for c in range(3):
                lanes = slice(c * LANES, (c + 1) * LANES)
                high, low = split(jnp.where(column == depth_rows[c], gathered[pairs, lanes], 0.0))
                both_t[at : at + SLOTS, lanes] = dot(pick, high).astype(jnp.bfloat16)
                both_t[LANES + at : LANES + at + SLOTS, lanes] = dot(pick, low).astype(jnp.bfloat16)
    near = lax.broadcasted_iota(jnp.int32, (LANES, LANES), 1) < 64
    for y in range(4):
        panel = slice(y * 512, (y + 1) * 512)
        parts = dot(both_t[...], v_high[:, panel])
        total = parts[:LANES] + parts[LANES:] + dot(both_t[:LANES, :], v_low[:, panel])
        for m in range(2):
            even, odd = total[:, 2 * m * LANES : (2 * m + 1) * LANES], total[:, (2 * m + 1) * LANES : (2 * m + 2) * LANES]
            cut = (
                jnp.where(near, even, pltpu.roll(odd, 64, 1)),
                jnp.where(near, pltpu.roll(even, 64, 1), odd),
            )
            for half, out in ((0, keep), (1, send)):
                for x in range(2):
                    at = (half * 2 + x) * SLOTS
                    for h in range(2):
                        to = (((x * 4 + y) * 2 + h) * 2 + m) * SLOTS
                        out[to : to + SLOTS, :] = cut[h][at : at + SLOTS]


def turn_kernel(arrived, out, turned):
    for h in range(2):
        for m in range(2):
            rows = []
            for y in range(4):
                at = ((y * 2 + h) * 2 + m) * SLOTS
                rows.append(arrived[at : at + SLOTS, :] + arrived[512 + at : 512 + at + SLOTS, :])
            turned[...] = jnp.transpose(jnp.concatenate(rows, axis=0))
            for e in range(2):
                for j in range(4):
                    out[pl.ds(j * 8 + h * 4 + 2 * m + e, 16, stride=32), :] = turned[pl.ds(e * 64 + j, 16, stride=4), :]


def spread_kernel(first, place, slots, labels, orbital_s, orbital, summed, other, swapped, *rest):
    out, turned, packed = rest[-3:]
    block, x, shift = place[0], place[4], place[3]
    for j in range(4):
        for h in range(2):
            for i in range(4):
                rows = swapped[pl.ds(j * 8 + h * 4 + i, 16, stride=32), :]
                turned[pl.ds(j * LANES + h * 64 + i, 16, stride=4), :] = rows
    mirrored = [jnp.transpose(turned[j * LANES : (j + 1) * LANES, :]) for j in range(4)]
    near = lax.broadcasted_iota(jnp.int32, (SLOTS, LANES), 1) < 64
    for y in range(4):
        for m in range(2):
            cut = []
            for h in range(2):
                at = ((y * 2 + h) * 2 + m) * SLOTS
                cut.append(summed[pl.ds(pl.multiple_of(x * 512 + at, SLOTS), SLOTS), :] + other[at : at + SLOTS, :])
            own = (
                jnp.where(near, cut[0], pltpu.roll(cut[1], 64, 1)),
                jnp.where(near, pltpu.roll(cut[0], 64, 1), cut[1]),
            )
            for e in range(2):
                j = 2 * m + e
                packed[pl.ds(y * 4 + j, SLOTS, stride=16), :] = own[e] - mirrored[j][y * SLOTS : (y + 1) * SLOTS]
    entries = []
    for y in range(4):
        entries.append(jnp.concatenate([orbital[y : y + 1, :] ^ orbital_s[block * 4 + j] for j in range(4)], axis=0))

    def step(p, carry):
        slot = slots[p] - shift
        inside = (slot >= 0) & (slot < SLOTS)
        spot = pl.multiple_of(jnp.clip(slot, 0, SLOTS - 1) * 16, 16)

        def store(wanted):
            for y in range(4):
                values = packed[pl.ds(spot + y * 4, 4), :]
                out[p, :, y * LANES : (y + 1) * LANES] = jnp.where(entries[y] == wanted, values, 0.0)

        if first:
            store(jnp.where(inside, labels[p], -1))
        else:
            pl.when(inside)(lambda: store(labels[p]))
        return carry

    if not first:
        out[...] = rest[0][...]
    lax.fori_loop(0, LANES, step, 0, unroll=4)


def on_device(amplitudes, integrals, orbital_irrep, slab_irrep, pair_irrep):
    y, xh, z = lax.axis_index("y"), lax.axis_index("xh"), lax.axis_index("z")
    x, core = lax.axis_index("xl"), lax.axis_index("core")
    block, occ = (y * 2 + xh) * 16 + z, x * 2 + core
    params = pltpu.CompilerParams(vmem_limit_bytes=40 * 1024 * 1024)

    mine = amplitudes.reshape(4, 384)
    near = lax.all_to_all(jnp.broadcast_to(mine[None], (16, 4, 384)), "z", 0, 0, tiled=True)
    near = jnp.broadcast_to(near.reshape(1, 64, 384), (8, 64, 384))
    gathered = lax.all_to_all(near, ("y", "xh"), 0, 0, tiled=True).reshape(512, 384)

    panel = integrals.reshape(3, LANES, 4, 4, LANES).transpose(0, 1, 3, 2, 4).reshape(3 * LANES * 16, LANES)
    orbital = orbital_irrep.reshape(4, LANES)
    pair = pair_irrep.reshape(4, LANES)
    same = pair[:, :, None] == pair[:, None, :]
    earlier = jnp.arange(LANES)[:, None] < jnp.arange(LANES)[None, :]
    ranks = jnp.sum(same & earlier[None], axis=1, dtype=jnp.int32)
    rounds = jnp.max(ranks) // SLOTS + 1
    slots = lax.dynamic_slice_in_dim(ranks, occ, 1, 0)[0]
    labels = lax.dynamic_slice_in_dim(pair, occ, 1, 0)[0]

    base = jnp.stack([block, occ, core, 0, x]).astype(jnp.int32)
    v_high, v_low, columns = pl.pallas_call(
        prepare_kernel,
        out_shape=[jax.ShapeDtypeStruct((384, 2048), jnp.bfloat16)] * 2 + [jax.ShapeDtypeStruct((512, LANES), jnp.int32)],
        in_specs=[SMEM] * 3 + [VMEM] * 3,
        out_specs=[VMEM] * 3,
        compiler_params=params,
        cost_estimate=pl.CostEstimate(flops=8_000_000, bytes_accessed=7_000_000, transcendentals=0),
        name="prepare",
    )(base, slab_irrep, orbital_irrep, orbital, pair, panel)

    def one_round(turn, previous):
        place = jnp.stack([block, occ, core, turn * SLOTS, x]).astype(jnp.int32)
        keep, send = pl.pallas_call(
            ladder_kernel,
            out_shape=[jax.ShapeDtypeStruct((1024, LANES), jnp.float32)] * 2,
            in_specs=[SMEM] * 2 + [VMEM] * 6,
            out_specs=[VMEM] * 2,
            scratch_shapes=[pltpu.VMEM((2 * LANES, 384), jnp.bfloat16)],
            compiler_params=params,
            name="ladder",
        )(place, slab_irrep, orbital, ranks, columns, gathered, v_high, v_low)
        arrived = lax.ppermute(send, "core", [(0, 1), (1, 0)])
        summed = keep + arrived
        other = lax.ppermute(lax.dynamic_slice_in_dim(summed, (1 - x) * 512, 512, 0), "xl", [(0, 1), (1, 0)])
        traded = lax.all_to_all(summed.reshape(16, 64, LANES), ("xl", "y", "xh"), 0, 0, tiled=True).reshape(1024, LANES)
        traded, other = lax.optimization_barrier((traded, other))
        turned = pl.pallas_call(
            turn_kernel,
            out_shape=jax.ShapeDtypeStruct((512, LANES), jnp.float32),
            in_specs=[VMEM],
            out_specs=VMEM,
            scratch_shapes=[pltpu.VMEM((LANES, LANES), jnp.float32)],
            compiler_params=params,
            name="turn",
        )(traded)
        swapped = lax.all_to_all(turned.reshape(16, 32, LANES), "z", 0, 0, tiled=True).reshape(512, LANES)
        first = previous is None
        operands = [place, slots, labels, orbital_irrep, orbital, summed, other, swapped]
        operands += [] if first else [previous]
        return pl.pallas_call(
            functools.partial(spread_kernel, first),
            out_shape=jax.ShapeDtypeStruct((LANES, 4, 512), jnp.float32),
            in_specs=[SMEM] * 4 + [VMEM] * (len(operands) - 4),
            out_specs=VMEM,
            scratch_shapes=[pltpu.VMEM((512, LANES), jnp.float32), pltpu.VMEM((16 * SLOTS, LANES), jnp.float32)],
            compiler_params=params,
            name="spread",
        )(*operands)

    filled = one_round(jnp.int32(0), None)
    _, filled = lax.while_loop(
        lambda state: state[0] < rounds,
        lambda state: (state[0] + 1, one_round(state[0], state[1])),
        (jnp.int32(1), filled),
    )
    return filled


def solution(mesh):
    devices = np.asarray(mesh.devices).reshape(4, 2, 16, 2, 2)
    fine = Mesh(devices, ("y", "xh", "z", "xl", "core"))
    blocks, groups = ("y", "xh", "z"), ("xl", "core")
    placed = (P(blocks, None, groups), P(None, groups, blocks, None), P(), P(), P())
    return jax.shard_map(
        on_device,
        mesh=fine,
        in_specs=placed,
        out_specs=P(groups, blocks, None),
        check_vma=False,
    )
```

time: 104 us -> 103 us (level)
  the two profiles are of different devices: /device:TPU:2 before, /device:TPU:8 now
where the time goes in v2:
time: 103 us; the launch traced here: 102 us
  waiting for transfers between devices  32.5 us (32%)
  blocking collectives  28.6 us (28%)
  starting transfers between devices  23.3 us (23%)
  Pallas kernels  8.69 us (8%)
  local copies, waits for them, and re-layouts  4.71 us (5%)
  between operations  2.39 us (2%)
  other arithmetic  1.67 us (2%)
    all_to_all x1, blocking collectives, on_device(): lax.all_to_all(jnp.broadcast_to(mine[None], (16, 4, 384)), 'z', 0, 0, til...  28.6 us
    all_to_all x1, waiting for transfers between devices, one_round(): lax.all_to_all(turned.reshape(16, 32, LANES), 'z', 0, 0, tiled=True)  15.4 us
    ppermute x1, waiting for transfers between devices, one_round(): lax.ppermute(lax.dynamic_slice_in_dim(summed, (1 - x) * 512, 512, 0), 'xl...  9.22 us
    all_to_all x1, starting transfers between devices, on_device(): lax.all_to_all(near, ('y', 'xh'), 0, 0, tiled=True).reshape(512, 384)  7.38 us
    all_to_all x1, waiting for transfers between devices, on_device(): lax.all_to_all(near, ('y', 'xh'), 0, 0, tiled=True).reshape(512, 384)  6.03 us
    all_to_all x1, starting transfers between devices, one_round(): lax.all_to_all(summed.reshape(16, 64, LANES), ('xl', 'y', 'xh'), 0, 0, ti...  5.58 us
    all_to_all x1, starting transfers between devices, one_round(): lax.all_to_all(turned.reshape(16, 32, LANES), 'z', 0, 0, tiled=True)  5.03 us
    ppermute x1, starting transfers between devices, one_round(): lax.ppermute(lax.dynamic_slice_in_dim(summed, (1 - x) * 512, 512, 0), 'xl...  3.43 us
  transfers between devices with their start and end apart: 5, of which 4 were waited for; matrix products, arithmetic and copies ran while one was open for 2% of the time, Pallas kernels for 2%

profile of v2, /device:TPU:8, one launch (start us, length us, event | category | flops | bytes accessed | tf_op | source)
XLA Modules:
  0.0 101.9 jit_solution(17128863949828976206)
XLA Ops:
  0.0 0.0 copy-start.3
  0.0 0.0 copy-start.4
  0.0 0.0 copy-start.1
  0.0 0.7 broadcast_in_dim.18
  0.8 28.6 %all_to_all.36 = f32[16,4,384]{2,1,0:T(4,128)S(1)} all-to-all(f32[16,4,384]{2,1,0:T(4,128)S(1)} %broadcast_in_dim.18), channel_id=1, replica_groups=mesh['y'=4,'xh'=2,'z'=16,'xl'=2,'core'=2] {'z'}, dimensions={0} | all-to-all | bytes 196608 | tf_op jit(solution)/shard_map/all_to_all | solution.py:150
  29.3 0.9 broadcast_in_dim.20
  30.3 7.4 %all-to-all-start.3 = ((f32[8,64,384]{2,1,0:T(8,128)}), f32[8,64,384]{2,1,0:T(8,128)}, u32[]{:S(2)}, u32[]{:S(2)}) async-start(f32[8,64,384]{2,1,0:T(8,128)} %broadcast_in_dim.20), calls=%async_computation.3 | async-start | bytes 1572864 | tf_op jit(solution)/shard_map/all_to_all | solution.py:152
  37.7 0.1 stack.52.place
  37.7 0.0 copy-done.3
  37.7 0.0 copy-done.4
  37.7 0.0 copy-done.1
  37.8 0.0 copy-start
  37.8 1.9 %copy-done = f32[3,128,4,512]{3,2,1,0:T(4,128)S(1)} copy-done((f32[3,128,4,512]{3,2,1,0:T(4,128)S(1)}, f32[3,128,4,512]{3,2,1,0:T(4,128)}, u32[]{:S(2)}) %copy-start) | copy-done | bytes 3145752
  39.6 2.1 %prepare.1 = (bf16[384,2048]{1,0:T(8,128)(2,1)S(1)}, bf16[384,2048]{1,0:T(8,128)(2,1)S(1)}, s32[512,128]{1,0:T(8,128)S(1)}) custom-call(s32[5]{0:T(128)S(1)} %stack.52.place, s32[3]{0:T(128)S(1)} %copy-done.4, s32[512]{0:T(512)S(1)} %copy-done.3, s32[4,128]{1,0:T(4,128)S(1)} %bitcast.56, s32[4,128]{1,0:T(4,128)S(1)} %bitcast.53, f32[6144,128]{1,0:T(8,128)S(1)} %bitcast.50), custom_call_target="tpu_custom_call" | custom-call | flops 8000000 | bytes 7000000 | tf_op jit(solution)/shard_map/prepare/pallas_call | solution.py:165
  41.7 0.0 copy-start.2
  41.8 0.1 convert_reduce_fusion.ranks
  41.9 6.0 %all-to-all-done.3 = f32[8,64,384]{2,1,0:T(8,128)} async-done(((f32[8,64,384]{2,1,0:T(8,128)}), f32[8,64,384]{2,1,0:T(8,128)}, u32[]{:S(2)}, u32[]{:S(2)}) %all-to-all-start.3) | async-done | bytes 786464 | tf_op jit(solution)/shard_map/all_to_all | solution.py:152
  48.0 2.5 %ladder.4 = (f32[1024,128]{1,0:T(8,128)S(1)}, f32[1024,128]{1,0:T(8,128)S(1)}) custom-call(s32[5]{0:T(128)S(1)} %stack.52.place, s32[3]{0:T(128)S(1)} %copy-done.4, s32[4,128]{1,0:T(4,128)S(1)} %bitcast.57, s32[4,128]{1,0:T(4,128)S(1)} %convert_reduce_fusion.ranks, s32[512,128]{1,0:T(8,128)S(1)} %get-tuple-element.383.columns, f32[512,384]{1,0:T(8,128)} %bitcast.21.gathered, ...), custom_call_target="tpu_custom_call" | custom-call | tf_op jit(solution)/shard_map/ladder/pallas_call | solution.py:177
  50.5 0.0 copy-done.2
  50.5 1.9 %collective-permute-start.2 = (f32[1024,128]{1,0:T(8,128)S(1)}, f32[1024,128]{1,0:T(8,128)S(1)}, u32[]{:S(2)}, u32[]{:S(2)}) collective-permute-start(f32[1024,128]{1,0:T(8,128)S(1)} %get-tuple-element.213), channel_id=1, source_target_pairs={{0,1},{1,0},{2,3},{3,2},{4,5},{5,4},{6,7},{7,6},{8,9},{9,8},{10,11... | collective-permute-start | bytes 1572872 | tf_op jit(solution)/shard_map/ppermute | solution.py:186
  52.4 1.9 %collective-permute-done.2 = f32[1024,128]{1,0:T(8,128)S(1)} collective-permute-done((f32[1024,128]{1,0:T(8,128)S(1)}, f32[1024,128]{1,0:T(8,128)S(1)}, u32[]{:S(2)}, u32[]{:S(2)}) %collective-permute-start.2) | collective-permute-done | bytes 524320 | tf_op jit(solution)/shard_map/ppermute | solution.py:186
  54.3 0.9 add.38.summed
  55.2 5.6 %all-to-all-start.4 = ((f32[16,64,128]{2,1,0:T(8,128)}), f32[16,64,128]{2,1,0:T(8,128)S(1)}, u32[]{:S(2)}, u32[]{:S(2)}) async-start(f32[16,64,128]{2,1,0:T(8,128)} %bitcast.22), calls=%async_computation.4 | async-start | bytes 1048576 | tf_op jit(solution)/shard_map/all_to_all | solution.py:189
  60.7 1.0 constant_dynamic-slice_fusion.1
  61.7 3.4 %collective-permute-start.3 = (f32[512,128]{1,0:T(8,128)S(1)}, f32[512,128]{1,0:T(8,128)S(1)}, u32[]{:S(2)}, u32[]{:S(2)}) collective-permute-start(f32[512,128]{1,0:T(8,128)S(1)} %constant_dynamic-slice_fusion.1), channel_id=1, source_target_pairs={{0,2},{2,0},{1,3},{3,1},{4,6},{6,4},{5,7},{7,5},{8,10},{10,8},{9,1... | collective-permute-start | bytes 786440 | tf_op jit(solution)/shard_map/ppermute | solution.py:188
  65.2 9.2 %collective-permute-done.3.other = f32[512,128]{1,0:T(8,128)S(1)} collective-permute-done((f32[512,128]{1,0:T(8,128)S(1)}, f32[512,128]{1,0:T(8,128)S(1)}, u32[]{:S(2)}, u32[]{:S(2)}) %collective-permute-start.3) | collective-permute-done | bytes 262176 | tf_op jit(solution)/shard_map/ppermute | solution.py:188
  74.4 0.0 all-to-all-done.4
  74.4 1.0 turn.4
  75.4 5.0 %all-to-all-start.5 = ((f32[16,32,128]{2,1,0:T(8,128)}), f32[16,32,128]{2,1,0:T(8,128)S(1)}, u32[]{:S(2)}, u32[]{:S(2)}) async-start(f32[16,32,128]{2,1,0:T(8,128)} %bitcast.24), calls=%async_computation.5 | async-start | bytes 524288 | tf_op jit(solution)/shard_map/all_to_all | solution.py:200
  80.4 0.6 reduce_max.9
  83.3 15.4 %all-to-all-done.5 = f32[16,32,128]{2,1,0:T(8,128)S(1)} async-done(((f32[16,32,128]{2,1,0:T(8,128)}), f32[16,32,128]{2,1,0:T(8,128)S(1)}, u32[]{:S(2)}, u32[]{:S(2)}) %all-to-all-start.5) | async-done | bytes 262176 | tf_op jit(solution)/shard_map/all_to_all | solution.py:200
  98.8 3.1 %spread.4 = f32[128,4,512]{2,1,0:T(4,128)} custom-call(s32[5]{0:T(128)S(1)} %stack.52.place, s32[128]{0:T(128)S(1)} %get-tuple-element.388.slots, s32[128]{0:T(128)S(1)} %get-tuple-element.389.labels, s32[512]{0:T(512)S(1)} %copy-done.3, s32[4,128]{1,0:T(4,128)S(1)} %bitcast.58, f32[1024,128]{1,0:T(8,128)} %add.38.summed, ...), custom_call_target="tpu_custom_call" | custom-call | tf_op jit(solution)/shard_map/spread/pallas_call | solution.py:204
  (4 shorter events, 0.1 us)
Async XLA Ops:
  0.0 37.7 %copy-start.3 = (s32[512]{0:T(512)S(1)}, s32[512]{0:T(512)}, u32[]{:S(2)}) copy-start(s32[512]{0:T(512)} %orbital_s.3) | copy-start | bytes 6148
  0.0 37.7 %copy-start.4 = (s32[3]{0:T(128)S(1)}, s32[3]{0:T(128)}, u32[]{:S(2)}) copy-start(s32[3]{0:T(128)} %slab.3) | copy-start | bytes 40
  0.0 37.7 %copy-start.1 = (s32[512]{0:T(512)S(1)}, s32[512]{0:T(512)}, u32[]{:S(2)}) copy-start(s32[512]{0:T(512)} %param.11) | copy-start | bytes 6148
  30.3 17.7 %all-to-all-start.3 = ((f32[8,64,384]{2,1,0:T(8,128)}), f32[8,64,384]{2,1,0:T(8,128)}, u32[]{:S(2)}, u32[]{:S(2)}) async-start(f32[8,64,384]{2,1,0:T(8,128)} %broadcast_in_dim.20), calls=%async_computation.3 | async-start | bytes 1572864 | tf_op jit(solution)/shard_map/all_to_all | solution.py:152
  37.8 1.9 %copy-start = (f32[3,128,4,512]{3,2,1,0:T(4,128)S(1)}, f32[3,128,4,512]{3,2,1,0:T(4,128)}, u32[]{:S(2)}) copy-start(f32[3,128,4,512]{3,2,1,0:T(4,128)} %param.8) | copy-start | bytes 9437188
  41.7 8.7 %copy-start.2 = (bf16[384,2048]{1,0:T(8,128)(2,1)}, bf16[384,2048]{1,0:T(8,128)(2,1)S(1)}, u32[]{:S(2)}) copy-start(bf16[384,2048]{1,0:T(8,128)(2,1)S(1)} %get-tuple-element.386.v_low) | copy-start | bytes 4718596
  50.5 3.8 %collective-permute-start.2 = (f32[1024,128]{1,0:T(8,128)S(1)}, f32[1024,128]{1,0:T(8,128)S(1)}, u32[]{:S(2)}, u32[]{:S(2)}) collective-permute-start(f32[1024,128]{1,0:T(8,128)S(1)} %get-tuple-element.213), channel_id=1, source_target_pairs={{0,1},{1,0},{2,3},{3,2},{4,5},{5,4},{6,7},{7,6},{8,9},{9,8},{10,11... | collective-permute-start | bytes 1572872 | tf_op jit(solution)/shard_map/ppermute | solution.py:186
  55.2 19.2 %all-to-all-start.4 = ((f32[16,64,128]{2,1,0:T(8,128)}), f32[16,64,128]{2,1,0:T(8,128)S(1)}, u32[]{:S(2)}, u32[]{:S(2)}) async-start(f32[16,64,128]{2,1,0:T(8,128)} %bitcast.22), calls=%async_computation.4 | async-start | bytes 1048576 | tf_op jit(solution)/shard_map/all_to_all | solution.py:189
  61.7 12.7 %collective-permute-start.3 = (f32[512,128]{1,0:T(8,128)S(1)}, f32[512,128]{1,0:T(8,128)S(1)}, u32[]{:S(2)}, u32[]{:S(2)}) collective-permute-start(f32[512,128]{1,0:T(8,128)S(1)} %constant_dynamic-slice_fusion.1), channel_id=1, source_target_pairs={{0,2},{2,0},{1,3},{3,1},{4,6},{6,4},{5,7},{7,5},{8,10},{10,8},{9,1... | collective-permute-start | bytes 786440 | tf_op jit(solution)/shard_map/ppermute | solution.py:188
  75.4 23.4 %all-to-all-start.5 = ((f32[16,32,128]{2,1,0:T(8,128)}), f32[16,32,128]{2,1,0:T(8,128)S(1)}, u32[]{:S(2)}, u32[]{:S(2)}) async-start(f32[16,32,128]{2,1,0:T(8,128)} %bitcast.24), calls=%async_computation.5 | async-start | bytes 524288 | tf_op jit(solution)/shard_map/all_to_all | solution.py:200

commit v3 on v2

v3 whole, which is shorter than its diff:
```python
import functools

import jax
import jax.numpy as jnp
import numpy as np
from jax import lax
from jax.experimental import pallas as pl
from jax.experimental.pallas import tpu as pltpu
from jax.sharding import Mesh
from jax.sharding import PartitionSpec as P

LANES = 128
GROUP = 64
SLOTS = 32
KEPT = 24
HALF = 16
DEPTH = 3 * LANES
VMEM = pl.BlockSpec(memory_space=pltpu.VMEM)
SMEM = pl.BlockSpec(memory_space=pltpu.SMEM)


def split(x):
    high = x.astype(jnp.bfloat16)
    return high, (x - high.astype(jnp.float32)).astype(jnp.bfloat16)


def dot(x, y):
    return jnp.dot(x, y, preferred_element_type=jnp.float32)


def iota(shape, dim):
    return lax.broadcasted_iota(jnp.int32, shape, dim)


def column_of(row):
    return jnp.transpose(jnp.broadcast_to(row, (LANES, LANES)))


def plan_kernel(turn, pair, sent, slots, targets, rounds):
    source, lane = iota((LANES, LANES), 0), iota((LANES, LANES), 1)
    near = source < GROUP
    mate = near == (lane < GROUP)
    later = iota((1, LANES), 1) >= GROUP
    ranks, firsts, starts = [], [], []
    most, total = 0, 0
    for q in range(4):
        row = pair[q : q + 1, :]
        column = column_of(row)
        same = column == row

        def count(where):
            return jnp.sum(jnp.where(where, 1, 0), axis=0, keepdims=True)

        ranks.append(count(same & mate & (source < lane)))
        firsts.append(count(same & near))
        most = jnp.maximum(most, jnp.max(count(same & mate)))
        total = jnp.maximum(total, jnp.max(count(same)))
        starts.append([count((column == (lane + t * LANES) // KEPT) & near) for t in range(2)])
    one = (most <= KEPT) & (total <= SLOTS)
    rounds[0] = jnp.where(one, 1, (most + HALF - 1) // HALF)
    shift = turn[0] * HALF
    for q in range(4):
        window = ranks[q] - shift
        window = jnp.where((window >= 0) & (window < HALF), window, -1)
        chosen = jnp.where(one, ranks[q], window)
        base = jnp.where(one, firsts[q], HALF)
        sent[q : q + 1, :] = chosen
        slots[q : q + 1, :] = jnp.where(chosen < 0, -1, chosen + jnp.where(later, base, 0))
        for t in range(2):
            spot = (iota((1, LANES), 1) + t * LANES) % KEPT
            start = jnp.where(one, starts[q][t], HALF)
            targets[q : q + 1, t * LANES : (t + 1) * LANES] = spot + start


def pack_kernel(place, slab, orbital, pair, sent, near, out, column):
    occ, quarter, later = place[1], place[5], place[6]
    depth_row = orbital[pl.ds(occ, 1), :]
    column[...] = column_of(pair[pl.ds(quarter, 1), :])
    mine = pl.ds(pl.multiple_of(later * GROUP, GROUP), GROUP)
    column = column[mine, :]
    chosen = sent[pl.ds(quarter, 1), :]
    chosen = jnp.where(later == 1, pltpu.roll(chosen, GROUP, 1), chosen)[:, :GROUP]
    pick = jnp.where(iota((KEPT, GROUP), 0) == chosen, 1.0, 0.0).astype(jnp.bfloat16)
    for c in range(3):
        lanes = slice(c * LANES, (c + 1) * LANES)
        high, low = split(jnp.where(column == depth_row ^ slab[c], near[:, lanes], 0.0))
        kept = dot(pick, high) + dot(pick, low)
        for to in range(8):
            out[to * KEPT : (to + 1) * KEPT, lanes] = kept


def prepare_kernel(place, slab, orbital_s, orbital, integrals, high, low):
    block, occ = place[0], place[1]
    depth_row = orbital[pl.ds(occ, 1), :]
    depth = jnp.concatenate([column_of(depth_row ^ slab[c]) for c in range(3)], axis=0)
    for y in range(4):
        lanes = orbital[y : y + 1, :]
        for i in range(4):
            panel = integrals[pl.ds(y * 4 + i, DEPTH, stride=16), :]
            label = lanes ^ orbital_s[block * 4 + i]
            at = (y * 4 + i) * LANES
            high[:, at : at + LANES], low[:, at : at + LANES] = split(jnp.where(depth == label, panel, 0.0))


def ladder_kernel(place, slab, orbital, targets, gathered, v_high, v_low, keep, send, both_t):
    occ, core = place[1], place[2]
    depth_row = orbital[pl.ds(occ, 1), :]
    depth_row = jnp.concatenate([depth_row ^ slab[c] for c in range(3)], axis=1)
    slot = iota((SLOTS, 8 * KEPT), 0)
    for half in range(2):
        for x in range(2):
            quarter = 2 * x + (core ^ half)
            pick = jnp.where(slot == targets[pl.ds(quarter, 1), : 8 * KEPT], 1.0, 0.0).astype(jnp.bfloat16)
            at = (half * 2 + x) * SLOTS
            first = gathered[pl.ds(pl.multiple_of(quarter * 2 * KEPT, 8), KEPT), :]
            second = gathered[pl.ds(pl.multiple_of(quarter * 2 * KEPT + KEPT, 8), KEPT), :]
            second = jnp.concatenate([jnp.where(depth_row == l, second, 0.0) for l in range(8)], axis=0)
            first = jnp.concatenate([first, jnp.zeros((SLOTS - KEPT, DEPTH), jnp.float32)], axis=0)
            for to, one, two in zip((at, LANES + at), split(first), split(second)):
                both_t[to : to + SLOTS, :] = (one.astype(jnp.float32) + dot(pick, two)).astype(jnp.bfloat16)
    near = iota((LANES, LANES), 1) < 64
    for y in range(4):
        panel = slice(y * 512, (y + 1) * 512)
        parts = dot(both_t[...], v_high[:, panel])
        total = parts[:LANES] + parts[LANES:] + dot(both_t[:LANES, :], v_low[:, panel])
        for m in range(2):
            even, odd = total[:, 2 * m * LANES : (2 * m + 1) * LANES], total[:, (2 * m + 1) * LANES : (2 * m + 2) * LANES]
            cut = (
                jnp.where(near, even, pltpu.roll(odd, 64, 1)),
                jnp.where(near, pltpu.roll(even, 64, 1), odd),
            )
            for half, out in ((0, keep), (1, send)):
                for x in range(2):
                    at = (half * 2 + x) * SLOTS
                    for h in range(2):
                        to = (((x * 4 + y) * 2 + h) * 2 + m) * SLOTS
                        out[to : to + SLOTS, :] = cut[h][at : at + SLOTS]


def add_kernel(place, keep, arrived, summed, other):
    x = place[4]
    summed[...] = keep[...] + arrived[...]
    other[...] = summed[pl.ds(pl.multiple_of((1 - x) * 512, 512), 512), :]


def turn_kernel(arrived, out, turned):
    for h in range(2):
        for m in range(2):
            rows = []
            for y in range(4):
                at = ((y * 2 + h) * 2 + m) * SLOTS
                rows.append(arrived[at : at + SLOTS, :] + arrived[512 + at : 512 + at + SLOTS, :])
            turned[...] = jnp.transpose(jnp.concatenate(rows, axis=0))
            for e in range(2):
                for j in range(4):
                    out[pl.ds(j * 8 + h * 4 + 2 * m + e, 16, stride=32), :] = turned[pl.ds(e * 64 + j, 16, stride=4), :]


def spread_kernel(first, place, slots, labels, orbital_s, orbital, summed, other, swapped, *rest):
    out, turned, packed = rest[-3:]
    block, x = place[0], place[4]
    for j in range(4):
        for h in range(2):
            for i in range(4):
                rows = swapped[pl.ds(j * 8 + h * 4 + i, 16, stride=32), :]
                turned[pl.ds(j * LANES + h * 64 + i, 16, stride=4), :] = rows
    mirrored = [jnp.transpose(turned[j * LANES : (j + 1) * LANES, :]) for j in range(4)]
    near = iota((SLOTS, LANES), 1) < 64
    for y in range(4):
        for m in range(2):
            cut = []
            for h in range(2):
                at = ((y * 2 + h) * 2 + m) * SLOTS
                cut.append(summed[pl.ds(pl.multiple_of(x * 512 + at, SLOTS), SLOTS), :] + other[at : at + SLOTS, :])
            own = (
                jnp.where(near, cut[0], pltpu.roll(cut[1], 64, 1)),
                jnp.where(near, pltpu.roll(cut[0], 64, 1), cut[1]),
            )
            for e in range(2):
                j = 2 * m + e
                packed[pl.ds(y * 4 + j, SLOTS, stride=16), :] = own[e] - mirrored[j][y * SLOTS : (y + 1) * SLOTS]
    rows = []
    for y in range(4):
        for j in range(4):
            rows.append(orbital[y : y + 1, :] ^ orbital_s[block * 4 + j])
    entry = jnp.concatenate(rows, axis=0)

    def step(p, carry):
        slot = slots[p]
        inside = slot >= 0
        values = packed[pl.ds(pl.multiple_of(jnp.maximum(slot, 0) * 16, 16), 16), :]
        where = pl.ds(pl.multiple_of(p * 16, 16), 16)
        if first:
            out[where, :] = jnp.where(entry == jnp.where(inside, labels[p], -1), values, 0.0)
        else:

            @pl.when(inside)
            def _():
                out[where, :] = jnp.where(entry == labels[p], values, 0.0)

        return carry

    if not first:
        out[...] = rest[0][...]
    lax.fori_loop(0, LANES, step, 0, unroll=8)


def call(kernel, name, scalars, out_shape, operands, scratch=(), cost=None, out_specs=None):
    return pl.pallas_call(
        kernel,
        out_shape=out_shape,
        in_specs=[SMEM] * scalars + [VMEM] * (len(operands) - scalars),
        out_specs=out_specs or jax.tree.map(lambda _: VMEM, out_shape),
        scratch_shapes=list(scratch),
        compiler_params=pltpu.CompilerParams(vmem_limit_bytes=40 * 1024 * 1024),
        cost_estimate=cost and pl.CostEstimate(flops=cost[0], bytes_accessed=cost[1], transcendentals=0),
        name=name,
    )(*operands)


def on_device(amplitudes, integrals, orbital_irrep, slab_irrep, pair_irrep):
    y, xh, z = lax.axis_index("y"), lax.axis_index("xh"), lax.axis_index("z")
    x, core = lax.axis_index("xl"), lax.axis_index("core")
    block, occ = (y * 2 + xh) * 16 + z, x * 2 + core
    place = jnp.stack([block, occ, core, 0, x, y, xh]).astype(jnp.int32)
    f32 = functools.partial(jax.ShapeDtypeStruct, dtype=jnp.float32)
    i32 = functools.partial(jax.ShapeDtypeStruct, dtype=jnp.int32)
    half = jax.ShapeDtypeStruct((DEPTH, 2048), jnp.bfloat16)

    mine = amplitudes.reshape(4, DEPTH)
    near = lax.all_to_all(jnp.broadcast_to(mine[None], (16, 4, DEPTH)), "z", 0, 0, tiled=True).reshape(GROUP, DEPTH)

    panel = integrals.reshape(3, LANES, 4, 4, LANES).transpose(0, 1, 3, 2, 4).reshape(DEPTH * 16, LANES)
    orbital = orbital_irrep.reshape(4, LANES)
    pair = pair_irrep.reshape(4, LANES)
    labels = lax.dynamic_slice_in_dim(pair, occ, 1, 0)[0]
    v_high, v_low = call(
        prepare_kernel,
        "prepare",
        3,
        [half, half],
        [place, slab_irrep, orbital_irrep, orbital, panel],
        cost=(8_000_000, 7_000_000),
    )

    def one_round(turn, previous):
        sent, slots, targets, rounds = call(
            plan_kernel,
            "plan",
            1,
            [i32((4, LANES)), i32((4, LANES)), i32((4, 2 * LANES)), i32((1,))],
            [turn.reshape(1), pair],
            out_specs=[VMEM, VMEM, VMEM, SMEM],
        )
        own_slots = lax.dynamic_slice_in_dim(slots, occ, 1, 0)[0]
        packed = call(
            pack_kernel,
            "pack",
            2,
            f32((8 * KEPT, DEPTH)),
            [place, slab_irrep, orbital, pair, sent, near],
            [pltpu.VMEM((LANES, LANES), jnp.int32)],
        )
        gathered = lax.all_to_all(packed.reshape(8, KEPT, DEPTH), ("y", "xh"), 0, 0, tiled=True).reshape(8 * KEPT, DEPTH)
        keep, send = call(
            ladder_kernel,
            "ladder",
            2,
            [f32((1024, LANES)), f32((1024, LANES))],
            [place, slab_irrep, orbital, targets, gathered, v_high, v_low],
            [pltpu.VMEM((2 * LANES, DEPTH), jnp.bfloat16)],
        )
        arrived = lax.ppermute(send, "core", [(0, 1), (1, 0)])
        summed, other = call(
            add_kernel, "add", 1, [f32((1024, LANES)), f32((512, LANES))], [place, keep, arrived]
        )
        other = lax.ppermute(other, "xl", [(0, 1), (1, 0)])
        traded = lax.all_to_all(summed.reshape(16, GROUP, LANES), ("xl", "y", "xh"), 0, 0, tiled=True)
        turned = call(
            turn_kernel,
            "turn",
            0,
            f32((512, LANES)),
            [traded.reshape(1024, LANES)],
            [pltpu.VMEM((LANES, LANES), jnp.float32)],
        )
        swapped = lax.all_to_all(turned.reshape(16, 32, LANES), "z", 0, 0, tiled=True).reshape(512, LANES)
        first = previous is None
        operands = [place, own_slots, labels, orbital_irrep, orbital, summed, other, swapped]
        if not first:
            operands.append(previous.reshape(LANES, 4, 4, LANES).transpose(0, 2, 1, 3).reshape(2048, LANES))
        filled = call(
            functools.partial(spread_kernel, first),
            "spread",
            4,
            f32((2048, LANES)),
            operands,
            [pltpu.VMEM((512, LANES), jnp.float32), pltpu.VMEM((16 * SLOTS, LANES), jnp.float32)],
        )
        return filled.reshape(LANES, 4, 4, LANES).transpose(0, 2, 1, 3).reshape(LANES, 4, 512), rounds[0]

    filled, rounds = one_round(jnp.int32(0), None)
    _, filled = lax.while_loop(
        lambda state: state[0] < rounds,
        lambda state: (state[0] + 1, one_round(state[0], state[1])[0]),
        (jnp.int32(1), filled),
    )
    return filled


def solution(mesh):
    devices = np.asarray(mesh.devices).reshape(4, 2, 16, 2, 2)
    fine = Mesh(devices, ("y", "xh", "z", "xl", "core"))
    blocks, groups = ("y", "xh", "z"), ("xl", "core")
    placed = (P(blocks, None, groups), P(None, groups, blocks, None), P(), P(), P())
    return jax.shard_map(
        on_device,
        mesh=fine,
        in_specs=placed,
        out_specs=P(groups, blocks, None),
        check_vma=False,
    )
```

time: 103 us -> 97.8 us (0.950)
  the two profiles are of different devices: /device:TPU:8 before, /device:TPU:32 now
where the time goes in v3:
time: 97.8 us; the launch traced here: 97.2 us
  starting transfers between devices  30.7 us (31%)
  waiting for transfers between devices  30 us (31%)
  blocking collectives  16.8 us (17%)
  Pallas kernels  14.8 us (15%)
  local copies, waits for them, and re-layouts  4.35 us (4%)
    all_to_all x1, blocking collectives, one_round(): lax.all_to_all(summed.reshape(16, GROUP, LANES), ('xl', 'y', 'xh'), 0, 0,...  16.8 us
    all_to_all x1, starting transfers between devices, on_device(): lax.all_to_all(jnp.broadcast_to(mine[None], (16, 4, DEPTH)), 'z', 0, 0, t...  15.2 us
    pallas_call x7, Pallas kernels, call(): pl.pallas_call(kernel, out_shape=out_shape, in_specs=[SMEM] * scalars + [...  14.8 us
    all_to_all x1, waiting for transfers between devices, on_device(): lax.all_to_all(jnp.broadcast_to(mine[None], (16, 4, DEPTH)), 'z', 0, 0, t...  11.3 us
    all_to_all x1, waiting for transfers between devices, one_round(): lax.all_to_all(turned.reshape(16, 32, LANES), 'z', 0, 0, tiled=True)  9.3 us
    all_to_all x1, starting transfers between devices, one_round(): lax.all_to_all(packed.reshape(8, KEPT, DEPTH), ('y', 'xh'), 0, 0, tiled=T...  6.94 us
    ppermute x1, waiting for transfers between devices, one_round(): other = lax.ppermute(other, 'xl', [(0, 1), (1, 0)])  5.74 us
    all_to_all x1, starting transfers between devices, one_round(): lax.all_to_all(turned.reshape(16, 32, LANES), 'z', 0, 0, tiled=True)  4.14 us
  transfers between devices with their start and end apart: 5, of which 5 were waited for; matrix products, arithmetic and copies ran while one was open for 0% of the time, Pallas kernels for 7%

profile of v3, /device:TPU:32, one launch (start us, length us, event | category | flops | bytes accessed | tf_op | source)
XLA Modules:
  0.0 97.2 jit_solution(7558286211514301144)
XLA Ops:
  0.0 1.3 %broadcast_in_dim.8 = f32[16,4,384]{2,1,0:T(4,128)} broadcast(f32[4,384]{1,0:T(4,128)} %bitcast.95), dimensions={1,2} | broadcast | bytes 104448 | tf_op jit(solution)/shard_map/broadcast_in_dim | solution.py:231
  1.3 15.2 %all-to-all-start.3 = ((f32[16,4,384]{2,1,0:T(4,128)}), f32[16,4,384]{2,1,0:T(4,128)S(1)}, u32[]{:S(2)}, u32[]{:S(2)}) async-start(f32[16,4,384]{2,1,0:T(4,128)} %broadcast_in_dim.8), calls=%async_computation.3 | async-start | bytes 196608 | tf_op jit(solution)/shard_map/all_to_all | solution.py:231
  16.6 1.6 %plan.4 = (s32[4,128]{1,0:T(4,128)S(1)}, s32[4,128]{1,0:T(4,128)S(1)}, s32[4,256]{1,0:T(4,128)S(1)}, s32[1]{0:T(128)}) custom-call(s32[1]{0:T(128)} %constant.43.clone.1.turn, s32[4,128]{1,0:T(4,128)} %bitcast.91), custom_call_target="tpu_custom_call" | custom-call | tf_op jit(solution)/shard_map/plan/pallas_call | solution.py:209
  18.1 0.1 stack.27.place
  18.2 11.3 %all-to-all-done.3 = f32[16,4,384]{2,1,0:T(4,128)S(1)} async-done(((f32[16,4,384]{2,1,0:T(4,128)}), f32[16,4,384]{2,1,0:T(4,128)S(1)}, u32[]{:S(2)}, u32[]{:S(2)}) %all-to-all-start.3) | async-done | bytes 98336 | tf_op jit(solution)/shard_map/all_to_all | solution.py:231
  29.6 1.7 %pack.4 = f32[192,384]{1,0:T(8,128)} custom-call(s32[7]{0:T(128)S(1)} %stack.27.place, s32[3]{0:T(128)} %slab.5, s32[4,128]{1,0:T(4,128)} %bitcast.82, s32[4,128]{1,0:T(4,128)} %bitcast.92, s32[4,128]{1,0:T(4,128)S(1)} %get-tuple-element.169.sent, f32[64,384]{1,0:T(8,128)S(1)} %reshape.87.near), custom_call_target="tpu_custom_call" | custom-call | tf_op jit(solution)/shard_map/pack/pallas_call | solution.py:209
  31.3 6.9 %all-to-all-start.4 = ((f32[8,24,384]{2,1,0:T(8,128)}), f32[8,24,384]{2,1,0:T(8,128)S(1)}, u32[]{:S(2)}, u32[]{:S(2)}) async-start(f32[8,24,384]{2,1,0:T(8,128)} %bitcast.29), calls=%async_computation.4 | async-start | bytes 589824 | tf_op jit(solution)/shard_map/all_to_all | solution.py:264
  38.2 0.0 copy-start
  38.2 1.9 %copy-done = f32[3,128,4,512]{3,2,1,0:T(4,128)S(1)} copy-done((f32[3,128,4,512]{3,2,1,0:T(4,128)S(1)}, f32[3,128,4,512]{3,2,1,0:T(4,128)}, u32[]{:S(2)}) %copy-start) | copy-done | bytes 3145752
  40.1 0.0 copy-start.2
  40.1 0.0 copy-start.4
  40.1 5.3 %prepare.1 = (bf16[384,2048]{1,0:T(8,128)(2,1)}, bf16[384,2048]{1,0:T(8,128)(2,1)}) custom-call(s32[7]{0:T(128)S(1)} %stack.27.place, s32[3]{0:T(128)} %slab.5, s32[512]{0:T(512)} %orbital_s.3, s32[4,128]{1,0:T(4,128)} %bitcast.83, f32[6144,128]{1,0:T(8,128)S(1)} %bitcast.74), custom_call_target="tpu_custom_call" | custom-call | flops 8000000 | bytes 7000000 | tf_op jit(solution)/shard_map/prepare/pallas_call | solution.py:209
  45.4 1.8 %all-to-all-done.4 = f32[8,24,384]{2,1,0:T(8,128)S(1)} async-done(((f32[8,24,384]{2,1,0:T(8,128)}), f32[8,24,384]{2,1,0:T(8,128)S(1)}, u32[]{:S(2)}, u32[]{:S(2)}) %all-to-all-start.4) | async-done | bytes 294944 | tf_op jit(solution)/shard_map/all_to_all | solution.py:264
  47.2 0.0 copy-done.2
  47.2 0.0 copy-done.4
  47.2 3.3 %ladder.4 = (f32[1024,128]{1,0:T(8,128)S(1)}, f32[1024,128]{1,0:T(8,128)S(1)}) custom-call(s32[7]{0:T(128)S(1)} %stack.27.place, s32[3]{0:T(128)S(1)} %copy-done.4, s32[4,128]{1,0:T(4,128)S(1)} %bitcast.84, s32[4,256]{1,0:T(4,128)S(1)} %get-tuple-element.168.targets, f32[192,384]{1,0:T(8,128)S(1)} %bitcast.77, bf16[384,2048]{1,0:T(8,128)(2,1)} %get-tuple-element.307.v_high, ...), custom_call_target="tpu_custom_call" | custom-call | tf_op jit(solution)/shard_map/ladder/pallas_call | solution.py:209
  50.5 1.9 %collective-permute-start.2 = (f32[1024,128]{1,0:T(8,128)S(1)}, f32[1024,128]{1,0:T(8,128)S(1)}, u32[]{:S(2)}, u32[]{:S(2)}) collective-permute-start(f32[1024,128]{1,0:T(8,128)S(1)} %get-tuple-element.173), channel_id=1, source_target_pairs={{0,1},{1,0},{2,3},{3,2},{4,5},{5,4},{6,7},{7,6},{8,9},{9,8},{10,11... | collective-permute-start | bytes 1572872 | tf_op jit(solution)/shard_map/ppermute | solution.py:273
  52.4 1.9 %collective-permute-done.2.arrived = f32[1024,128]{1,0:T(8,128)S(1)} collective-permute-done((f32[1024,128]{1,0:T(8,128)S(1)}, f32[1024,128]{1,0:T(8,128)S(1)}, u32[]{:S(2)}, u32[]{:S(2)}) %collective-permute-start.2) | collective-permute-done | bytes 524320 | tf_op jit(solution)/shard_map/ppermute | solution.py:273
  54.3 0.0 copy-start.3
  54.3 0.6 add.31
  54.9 16.8 %all_to_all.44 = f32[16,64,128]{2,1,0:T(8,128)S(1)} all-to-all(f32[16,64,128]{2,1,0:T(8,128)S(1)} %bitcast.76), channel_id=1, replica_groups=mesh['y'=4,'xh'=2,'z'=16,'xl'=2,'core'=2] {'xl','y','xh'}, dimensions={0} | all-to-all | bytes 1048576 | tf_op jit(solution)/shard_map/all_to_all | solution.py:278
  71.7 1.0 %turn.4 = f32[512,128]{1,0:T(8,128)} custom-call(f32[1024,128]{1,0:T(8,128)S(1)} %bitcast.75), custom_call_target="tpu_custom_call" | custom-call | tf_op jit(solution)/shard_map/turn/pallas_call | solution.py:209
  72.6 4.1 %all-to-all-start.6 = ((f32[16,32,128]{2,1,0:T(8,128)}), f32[16,32,128]{2,1,0:T(8,128)S(1)}, u32[]{:S(2)}, u32[]{:S(2)}) async-start(f32[16,32,128]{2,1,0:T(8,128)} %bitcast.36), calls=%async_computation.6 | async-start | bytes 524288 | tf_op jit(solution)/shard_map/all_to_all | solution.py:287
  76.8 2.5 %collective-permute-start.3 = (f32[512,128]{1,0:T(8,128)S(1)}, f32[512,128]{1,0:T(8,128)S(1)}, u32[]{:S(2)}, u32[]{:S(2)}) collective-permute-start(f32[512,128]{1,0:T(8,128)S(1)} %get-tuple-element.175), channel_id=1, source_target_pairs={{0,2},{2,0},{1,3},{3,1},{4,6},{6,4},{5,7},{7,5},{8,10},{10,8},{9,1... | collective-permute-start | bytes 786440 | tf_op jit(solution)/shard_map/ppermute | solution.py:277
  79.3 0.0 copy-done.3
  79.3 5.7 %collective-permute-done.3.other = f32[512,128]{1,0:T(8,128)S(1)} collective-permute-done((f32[512,128]{1,0:T(8,128)S(1)}, f32[512,128]{1,0:T(8,128)S(1)}, u32[]{:S(2)}, u32[]{:S(2)}) %collective-permute-start.3) | collective-permute-done | bytes 262176 | tf_op jit(solution)/shard_map/ppermute | solution.py:277
  85.0 9.3 %all-to-all-done.6 = f32[16,32,128]{2,1,0:T(8,128)S(1)} async-done(((f32[16,32,128]{2,1,0:T(8,128)}), f32[16,32,128]{2,1,0:T(8,128)S(1)}, u32[]{:S(2)}, u32[]{:S(2)}) %all-to-all-start.6) | async-done | bytes 262176 | tf_op jit(solution)/shard_map/all_to_all | solution.py:287
  94.3 1.3 %spread.4 = f32[2048,128]{1,0:T(8,128)S(1)} custom-call(s32[7]{0:T(128)S(1)} %stack.27.place, s32[128]{0:T(128)S(1)} %dynamic-slice_bitcast_fusion.2.slots, s32[128]{0:T(128)S(1)} %dynamic-slice_bitcast_fusion.1.labels, s32[512]{0:T(512)S(1)} %copy-done.2, s32[4,128]{1,0:T(4,128)S(1)} %bitcast.85, f32[1024,128]{1,0:T(8,128)S(1)} %get-tuple-element.174.summed, ...), custom_call_target="tpu_custom_call" | custom-call | tf_op jit(solution)/shard_map/spread/pallas_call | solution.py:209
  95.7 0.6 while.12
  96.3 0.0 copy-start.1
  96.3 1.0 copy-done.1
  (3 shorter events, 0.1 us)
Async XLA Ops:
  1.3 28.2 %all-to-all-start.3 = ((f32[16,4,384]{2,1,0:T(4,128)}), f32[16,4,384]{2,1,0:T(4,128)S(1)}, u32[]{:S(2)}, u32[]{:S(2)}) async-start(f32[16,4,384]{2,1,0:T(4,128)} %broadcast_in_dim.8), calls=%async_computation.3 | async-start | bytes 196608 | tf_op jit(solution)/shard_map/all_to_all | solution.py:231
  31.3 15.9 %all-to-all-start.4 = ((f32[8,24,384]{2,1,0:T(8,128)}), f32[8,24,384]{2,1,0:T(8,128)S(1)}, u32[]{:S(2)}, u32[]{:S(2)}) async-start(f32[8,24,384]{2,1,0:T(8,128)} %bitcast.29), calls=%async_computation.4 | async-start | bytes 589824 | tf_op jit(solution)/shard_map/all_to_all | solution.py:264
  38.2 1.9 %copy-start = (f32[3,128,4,512]{3,2,1,0:T(4,128)S(1)}, f32[3,128,4,512]{3,2,1,0:T(4,128)}, u32[]{:S(2)}) copy-start(f32[3,128,4,512]{3,2,1,0:T(4,128)} %param.8) | copy-start | bytes 9437188
  40.1 7.1 %copy-start.2 = (s32[512]{0:T(512)S(1)}, s32[512]{0:T(512)}, u32[]{:S(2)}) copy-start(s32[512]{0:T(512)} %orbital_s.3) | copy-start | bytes 6148
  40.1 7.1 %copy-start.4 = (s32[3]{0:T(128)S(1)}, s32[3]{0:T(128)}, u32[]{:S(2)}) copy-start(s32[3]{0:T(128)} %slab.5) | copy-start | bytes 40
  50.5 3.8 %collective-permute-start.2 = (f32[1024,128]{1,0:T(8,128)S(1)}, f32[1024,128]{1,0:T(8,128)S(1)}, u32[]{:S(2)}, u32[]{:S(2)}) collective-permute-start(f32[1024,128]{1,0:T(8,128)S(1)} %get-tuple-element.173), channel_id=1, source_target_pairs={{0,1},{1,0},{2,3},{3,2},{4,5},{5,4},{6,7},{7,6},{8,9},{9,8},{10,11... | collective-permute-start | bytes 1572872 | tf_op jit(solution)/shard_map/ppermute | solution.py:273
  54.3 25.0 %copy-start.3 = (s32[512]{0:T(512)S(1)}, s32[512]{0:T(512)}, u32[]{:S(2)}) copy-start(s32[512]{0:T(512)} %param.11) | copy-start | bytes 6148
  72.6 21.7 %all-to-all-start.6 = ((f32[16,32,128]{2,1,0:T(8,128)}), f32[16,32,128]{2,1,0:T(8,128)S(1)}, u32[]{:S(2)}, u32[]{:S(2)}) async-start(f32[16,32,128]{2,1,0:T(8,128)} %bitcast.36), calls=%async_computation.6 | async-start | bytes 524288 | tf_op jit(solution)/shard_map/all_to_all | solution.py:287
  76.8 8.3 %collective-permute-start.3 = (f32[512,128]{1,0:T(8,128)S(1)}, f32[512,128]{1,0:T(8,128)S(1)}, u32[]{:S(2)}, u32[]{:S(2)}) collective-permute-start(f32[512,128]{1,0:T(8,128)S(1)} %get-tuple-element.175), channel_id=1, source_target_pairs={{0,2},{2,0},{1,3},{3,1},{4,6},{6,4},{5,7},{7,5},{8,10},{10,8},{9,1... | collective-permute-start | bytes 786440 | tf_op jit(solution)/shard_map/ppermute | solution.py:277
  96.3 1.0 %copy-start.1 = (f32[128,4,512]{2,1,0:T(4,128)}, f32[128,4,512]{2,1,0:T(4,128)S(1)}, u32[]{:S(2)}) copy-start(f32[128,4,512]{2,1,0:T(4,128)S(1)} %get-tuple-element.351) | copy-start | bytes 3145732

commit v4 on v3

--- a/solution.py
+++ b/solution.py
@@ -17,6 +17,7 @@
 DEPTH = 3 * LANES
 VMEM = pl.BlockSpec(memory_space=pltpu.VMEM)
 SMEM = pl.BlockSpec(memory_space=pltpu.SMEM)
+ANY = pl.BlockSpec(memory_space=pl.ANY)
 
 
 def split(x):
@@ -36,7 +37,7 @@
     return jnp.transpose(jnp.broadcast_to(row, (LANES, LANES)))
 
 
-def plan_kernel(turn, pair, sent, slots, targets, rounds):
+def plan_kernel(turn, place, pair, sent, slots, targets, mates, rounds, column_s):
     source, lane = iota((LANES, LANES), 0), iota((LANES, LANES), 1)
     near = source < GROUP
     mate = near == (lane < GROUP)
@@ -70,14 +71,14 @@
             spot = (iota((1, LANES), 1) + t * LANES) % KEPT
             start = jnp.where(one, starts[q][t], HALF)
             targets[q : q + 1, t * LANES : (t + 1) * LANES] = spot + start
-
-
-def pack_kernel(place, slab, orbital, pair, sent, near, out, column):
+    column_s[...] = column_of(pair[pl.ds(place[5], 1), :])
+    mates[...] = column_s[pl.ds(pl.multiple_of(place[6] * GROUP, GROUP), GROUP), :]
+
+
+def pack_kernel(place, slab, orbital, mates, sent, near, out):
     occ, quarter, later = place[1], place[5], place[6]
     depth_row = orbital[pl.ds(occ, 1), :]
-    column[...] = column_of(pair[pl.ds(quarter, 1), :])
-    mine = pl.ds(pl.multiple_of(later * GROUP, GROUP), GROUP)
-    column = column[mine, :]
+    column = mates[...]
     chosen = sent[pl.ds(quarter, 1), :]
     chosen = jnp.where(later == 1, pltpu.roll(chosen, GROUP, 1), chosen)[:, :GROUP]
     pick = jnp.where(iota((KEPT, GROUP), 0) == chosen, 1.0, 0.0).astype(jnp.bfloat16)
@@ -156,9 +157,11 @@
                     out[pl.ds(j * 8 + h * 4 + 2 * m + e, 16, stride=32), :] = turned[pl.ds(e * 64 + j, 16, stride=4), :]
 
 
-def spread_kernel(first, place, slots, labels, orbital_s, orbital, summed, other, swapped, *rest):
-    out, turned, packed = rest[-3:]
+def spread_kernel(
+    place, rounds, slots, labels, orbital_s, orbital, summed, other, swapped, previous, out, turned, packed, filled, done
+):
     block, x = place[0], place[4]
+    several = rounds[0] > 1
     for j in range(4):
         for h in range(2):
             for i in range(4):
@@ -185,34 +188,52 @@
             rows.append(orbital[y : y + 1, :] ^ orbital_s[block * 4 + j])
     entry = jnp.concatenate(rows, axis=0)
 
-    def step(p, carry):
-        slot = slots[p]
-        inside = slot >= 0
-        values = packed[pl.ds(pl.multiple_of(jnp.maximum(slot, 0) * 16, 16), 16), :]
-        where = pl.ds(pl.multiple_of(p * 16, 16), 16)
-        if first:
-            out[where, :] = jnp.where(entry == jnp.where(inside, labels[p], -1), values, 0.0)
-        else:
-
-            @pl.when(inside)
-            def _():
-                out[where, :] = jnp.where(entry == labels[p], values, 0.0)
-
-        return carry
-
-    if not first:
-        out[...] = rest[0][...]
-    lax.fori_loop(0, LANES, step, 0, unroll=8)
-
-
-def call(kernel, name, scalars, out_shape, operands, scratch=(), cost=None, out_specs=None):
+    def rows_of(p):
+        return pl.ds(pl.multiple_of(p * 16, 16), 16)
+
+    def store(p, slot):
+        values = packed[pl.ds(pl.multiple_of(slot * 16, 16), 16), :]
+        filled[rows_of(p), :] = jnp.where(entry == labels[p], values, 0.0)
+
+    def part_of(part):
+        return pltpu.make_async_copy(filled.at[pl.ds(part * 512, 512), :], out.at[pl.ds(part * 512, 512), :], done.at[part])
+
+    @pl.when(several)
+    def _():
+        copy = pltpu.make_async_copy(previous, filled, done.at[0])
+        copy.start()
+        copy.wait()
+
+        def step(p, carry):
+            pl.when(slots[p] >= 0)(lambda: store(p, slots[p]))
+            return carry
+
+        lax.fori_loop(0, LANES, step, 0)
+        for part in range(4):
+            part_of(part).start()
+
+    @pl.when(jnp.logical_not(several))
+    def _():
+        def step(p, carry):
+            store(p, slots[p])
+            return carry
+
+        for part in range(4):
+            lax.fori_loop(part * 32, part * 32 + 32, step, 0, unroll=8)
+            part_of(part).start()
+
+    for part in range(4):
+        part_of(part).wait()
+
+
+def call(kernel, name, scalars, out_shape, operands, scratch=(), cost=None, out_specs=None, vmem=8, last=VMEM):
     return pl.pallas_call(
         kernel,
         out_shape=out_shape,
-        in_specs=[SMEM] * scalars + [VMEM] * (len(operands) - scalars),
+        in_specs=[SMEM] * scalars + [VMEM] * (len(operands) - scalars - 1) + [last],
         out_specs=out_specs or jax.tree.map(lambda _: VMEM, out_shape),
         scratch_shapes=list(scratch),
-        compiler_params=pltpu.CompilerParams(vmem_limit_bytes=40 * 1024 * 1024),
+        compiler_params=pltpu.CompilerParams(vmem_limit_bytes=vmem * 1024 * 1024),
         cost_estimate=cost and pl.CostEstimate(flops=cost[0], bytes_accessed=cost[1], transcendentals=0),
         name=name,
     )(*operands)
@@ -241,16 +262,19 @@
         [half, half],
         [place, slab_irrep, orbital_irrep, orbital, panel],
         cost=(8_000_000, 7_000_000),
+        vmem=16,
     )
-
-    def one_round(turn, previous):
-        sent, slots, targets, rounds = call(
+    near, v_high, v_low = lax.optimization_barrier((near, v_high, v_low))
+
+    def one_round(turn):
+        sent, slots, targets, mates, rounds = call(
             plan_kernel,
             "plan",
-            1,
-            [i32((4, LANES)), i32((4, LANES)), i32((4, 2 * LANES)), i32((1,))],
-            [turn.reshape(1), pair],
-            out_specs=[VMEM, VMEM, VMEM, SMEM],
+            2,
+            [i32((4, LANES)), i32((4, LANES)), i32((4, 2 * LANES)), i32((GROUP, LANES)), i32((1,))],
+            [turn.reshape(1), place, pair],
+            [pltpu.VMEM((LANES, LANES), jnp.int32)],
+            out_specs=[VMEM, VMEM, VMEM, VMEM, SMEM],
         )
         own_slots = lax.dynamic_slice_in_dim(slots, occ, 1, 0)[0]
         packed = call(
@@ -258,8 +282,7 @@
             "pack",
             2,
             f32((8 * KEPT, DEPTH)),
-            [place, slab_irrep, orbital, pair, sent, near],
-            [pltpu.VMEM((LANES, LANES), jnp.int32)],
+            [place, slab_irrep, orbital, mates, sent, near],
         )
         gathered = lax.all_to_all(packed.reshape(8, KEPT, DEPTH), ("y", "xh"), 0, 0, tiled=True).reshape(8 * KEPT, DEPTH)
         keep, send = call(
@@ -269,6 +292,7 @@
             [f32((1024, LANES)), f32((1024, LANES))],
             [place, slab_irrep, orbital, targets, gathered, v_high, v_low],
             [pltpu.VMEM((2 * LANES, DEPTH), jnp.bfloat16)],
+            vmem=16,
         )
         arrived = lax.ppermute(send, "core", [(0, 1), (1, 0)])
         summed, other = call(
@@ -285,27 +309,35 @@
             [pltpu.VMEM((LANES, LANES), jnp.float32)],
         )
         swapped = lax.all_to_all(turned.reshape(16, 32, LANES), "z", 0, 0, tiled=True).reshape(512, LANES)
-        first = previous is None
-        operands = [place, own_slots, labels, orbital_irrep, orbital, summed, other, swapped]
-        if not first:
-            operands.append(previous.reshape(LANES, 4, 4, LANES).transpose(0, 2, 1, 3).reshape(2048, LANES))
-        filled = call(
-            functools.partial(spread_kernel, first),
+        return rounds, own_slots, summed, other, swapped
+
+    def spread(previous, rounds, own_slots, summed, other, swapped):
+        return call(
+            spread_kernel,
             "spread",
-            4,
+            5,
             f32((2048, LANES)),
-            operands,
-            [pltpu.VMEM((512, LANES), jnp.float32), pltpu.VMEM((16 * SLOTS, LANES), jnp.float32)],
-        )
-        return filled.reshape(LANES, 4, 4, LANES).transpose(0, 2, 1, 3).reshape(LANES, 4, 512), rounds[0]
-
-    filled, rounds = one_round(jnp.int32(0), None)
-    _, filled = lax.while_loop(
-        lambda state: state[0] < rounds,
-        lambda state: (state[0] + 1, one_round(state[0], state[1])[0]),
-        (jnp.int32(1), filled),
+            [place, rounds, own_slots, labels, orbital_irrep, orbital, summed, other, swapped, previous],
+            [
+                pltpu.VMEM((512, LANES), jnp.float32),
+                pltpu.VMEM((16 * SLOTS, LANES), jnp.float32),
+                pltpu.VMEM((2048, LANES), jnp.float32),
+                pltpu.SemaphoreType.DMA((4,)),
+            ],
+            out_specs=ANY,
+            last=ANY,
+        )
+
+    rounds, own_slots, summed, other, swapped = one_round(jnp.int32(0))
+    empty = jnp.zeros((2048, LANES), jnp.float32)
+    empty, summed, other, swapped = lax.optimization_barrier((empty, summed, other, swapped))
+    _, previous = lax.while_loop(
+        lambda state: state[0] < rounds[0],
+        lambda state: (state[0] + 1, spread(state[1], *one_round(state[0]))),
+        (jnp.int32(1), empty),
     )
-    return filled
+    filled = spread(previous, rounds, own_slots, summed, other, swapped)
+    return filled.reshape(LANES, 4, 4, LANES).transpose(0, 2, 1, 3).reshape(LANES, 4, 512)
 
 
 def solution(mesh):

time: 97.8 us -> 99.9 us (1.021)
  blocking collectives: 16.8 us -> 30.1 us
  waiting for transfers between devices: 30 us -> 21 us
  starting transfers between devices: 30.7 us -> 27.7 us
    all_to_all x0 -> x1, blocking collectives: none -> 15.9 us  [one_round(): lax.all_to_all(packed.reshape(8, KEPT, DEPTH), ('y', 'xh'), 0, 0, tiled=T...]
    all_to_all x1, waiting for transfers between devices: 11.3 us -> 4.01 us  [on_device(): lax.all_to_all(jnp.broadcast_to(mine[None], (16, 4, DEPTH)), 'z', 0, 0, t...]
    all_to_all x1 -> x0, starting transfers between devices: 6.94 us -> none  [one_round(): lax.all_to_all(packed.reshape(8, KEPT, DEPTH), ('y', 'xh'), 0, 0, tiled=T...]
    all_to_all x1, starting transfers between devices: 4.14 us -> 8.02 us  [one_round(): lax.all_to_all(turned.reshape(16, 32, LANES), 'z', 0, 0, tiled=True)]
    all_to_all x1, blocking collectives: 16.8 us -> 14.2 us  [one_round(): lax.all_to_all(summed.reshape(16, GROUP, LANES), ('xl', 'y', 'xh'), 0, 0,...]
    all_to_all x1 -> x0, waiting for transfers between devices: 1.76 us -> none  [one_round(): lax.all_to_all(packed.reshape(8, KEPT, DEPTH), ('y', 'xh'), 0, 0, tiled=T...]
    broadcast_in_dim x0 -> x1, local copies, waits for them, and re-layouts: none -> 1.04 us  [on_device(): empty = jnp.zeros((2048, LANES), jnp.float32)]
    unnamed x10 -> x8, local copies, waits for them, and re-layouts: 2.86 us -> 1.9 us
  transfers between devices with their start and end apart: 5 -> 4, of which waited for: 5 -> 4; matrix products, arithmetic and copies ran while one was open for 0% -> 0% of each run, Pallas kernels for 7% -> 7%
where the time goes in v4:
time: 99.9 us; the launch traced here: 99.4 us
  blocking collectives  30.1 us (30%)
  starting transfers between devices  27.7 us (28%)
  waiting for transfers between devices  21 us (21%)
  Pallas kernels  15.3 us (15%)
  local copies, waits for them, and re-layouts  4.42 us (4%)
    all_to_all x1, blocking collectives, one_round(): lax.all_to_all(packed.reshape(8, KEPT, DEPTH), ('y', 'xh'), 0, 0, tiled=T...  15.9 us
    pallas_call x7, Pallas kernels, call(): pl.pallas_call(kernel, out_shape=out_shape, in_specs=[SMEM] * scalars + [...  15.3 us
    all_to_all x1, starting transfers between devices, on_device(): lax.all_to_all(jnp.broadcast_to(mine[None], (16, 4, DEPTH)), 'z', 0, 0, t...  15.2 us
    all_to_all x1, blocking collectives, one_round(): lax.all_to_all(summed.reshape(16, GROUP, LANES), ('xl', 'y', 'xh'), 0, 0,...  14.2 us
    all_to_all x1, waiting for transfers between devices, one_round(): lax.all_to_all(turned.reshape(16, 32, LANES), 'z', 0, 0, tiled=True)  9.46 us
    all_to_all x1, starting transfers between devices, one_round(): lax.all_to_all(turned.reshape(16, 32, LANES), 'z', 0, 0, tiled=True)  8.02 us
    ppermute x1, waiting for transfers between devices, one_round(): other = lax.ppermute(other, 'xl', [(0, 1), (1, 0)])  5.69 us
    all_to_all x1, waiting for transfers between devices, on_device(): lax.all_to_all(jnp.broadcast_to(mine[None], (16, 4, DEPTH)), 'z', 0, 0, t...  4.01 us
  transfers between devices with their start and end apart: 4, of which 4 were waited for; matrix products, arithmetic and copies ran while one was open for 0% of the time, Pallas kernels for 7%

profile of v4, /device:TPU:32, one launch (start us, length us, event | category | flops | bytes accessed | tf_op | source)
XLA Modules:
  0.0 99.4 jit_solution(16795866924014198616)
XLA Ops:
  0.0 1.3 %broadcast_in_dim.12 = f32[16,4,384]{2,1,0:T(4,128)} broadcast(f32[4,384]{1,0:T(4,128)} %bitcast.79), dimensions={1,2} | broadcast | bytes 104448 | tf_op jit(solution)/shard_map/broadcast_in_dim | solution.py:252
  1.3 15.2 %all-to-all-start.3 = ((f32[16,4,384]{2,1,0:T(4,128)}), f32[16,4,384]{2,1,0:T(4,128)S(1)}, u32[]{:S(2)}, u32[]{:S(2)}) async-start(f32[16,4,384]{2,1,0:T(4,128)} %broadcast_in_dim.12), calls=%async_computation.3 | async-start | bytes 196608 | tf_op jit(solution)/shard_map/all_to_all | solution.py:252
  16.6 0.1 stack.27.place
  16.6 1.7 %plan.4 = (s32[4,128]{1,0:T(4,128)S(1)}, s32[4,128]{1,0:T(4,128)S(1)}, s32[4,256]{1,0:T(4,128)S(1)}, s32[64,128]{1,0:T(8,128)S(1)}, s32[1]{0:T(128)}) custom-call(s32[1]{0:T(128)} %constant.43.clone.1.turn, s32[7]{0:T(128)S(1)} %stack.27.place, s32[4,128]{1,0:T(4,128)} %bitcast.76), custom_call_target="tpu_custom_call" | custom-call | tf_op jit(solution)/shard_map/plan/pallas_call | solution.py:230
  18.3 0.0 copy-start
  18.3 1.9 %copy-done = f32[3,128,4,512]{3,2,1,0:T(4,128)S(1)} copy-done((f32[3,128,4,512]{3,2,1,0:T(4,128)S(1)}, f32[3,128,4,512]{3,2,1,0:T(4,128)}, u32[]{:S(2)}) %copy-start) | copy-done | bytes 3145752
  20.2 0.0 copy-start.1
  20.2 0.0 copy-start.2
  20.2 5.3 %prepare.1 = (bf16[384,2048]{1,0:T(8,128)(2,1)}, bf16[384,2048]{1,0:T(8,128)(2,1)}) custom-call(s32[7]{0:T(128)S(1)} %stack.27.place, s32[3]{0:T(128)} %slab.5, s32[512]{0:T(512)} %orbital_s.3, s32[4,128]{1,0:T(4,128)} %bitcast.67, f32[6144,128]{1,0:T(8,128)S(1)} %bitcast.61), custom_call_target="tpu_custom_call" | custom-call | flops 8000000 | bytes 7000000 | tf_op jit(solution)/shard_map/prepare/pallas_call | solution.py:230
  25.5 4.0 %all-to-all-done.3 = f32[16,4,384]{2,1,0:T(4,128)S(1)} async-done(((f32[16,4,384]{2,1,0:T(4,128)}), f32[16,4,384]{2,1,0:T(4,128)S(1)}, u32[]{:S(2)}, u32[]{:S(2)}) %all-to-all-start.3) | async-done | bytes 98336 | tf_op jit(solution)/shard_map/all_to_all | solution.py:252
  29.6 0.0 copy-done.1
  29.6 0.0 copy-done.2
  29.6 0.8 pack.4
  30.4 15.9 %all_to_all.44 = f32[8,24,384]{2,1,0:T(8,128)S(1)} all-to-all(f32[8,24,384]{2,1,0:T(8,128)S(1)} %bitcast.64), channel_id=1, replica_groups=mesh['y'=4,'xh'=2,'z'=16,'xl'=2,'core'=2] {'y','xh'}, dimensions={0} | all-to-all | bytes 589824 | tf_op jit(solution)/shard_map/all_to_all | solution.py:287
  46.3 3.3 %ladder.4 = (f32[1024,128]{1,0:T(8,128)S(1)}, f32[1024,128]{1,0:T(8,128)S(1)}) custom-call(s32[7]{0:T(128)S(1)} %stack.27.place, s32[3]{0:T(128)S(1)} %copy-done.2, s32[4,128]{1,0:T(4,128)S(1)} %bitcast.69, s32[4,256]{1,0:T(4,128)S(1)} %get-tuple-element.178.targets, f32[192,384]{1,0:T(8,128)S(1)} %bitcast.65, bf16[384,2048]{1,0:T(8,128)(2,1)} %get-tuple-element.328.v_high, ...), custom_call_target="tpu_custom_call" | custom-call | tf_op jit(solution)/shard_map/ladder/pallas_call | solution.py:230
  49.6 1.9 %collective-permute-start.2 = (f32[1024,128]{1,0:T(8,128)S(1)}, f32[1024,128]{1,0:T(8,128)S(1)}, u32[]{:S(2)}, u32[]{:S(2)}) collective-permute-start(f32[1024,128]{1,0:T(8,128)S(1)} %get-tuple-element.187), channel_id=1, source_target_pairs={{0,1},{1,0},{2,3},{3,2},{4,5},{5,4},{6,7},{7,6},{8,9},{9,8},{10,11... | collective-permute-start | bytes 1572872 | tf_op jit(solution)/shard_map/ppermute | solution.py:297
  51.5 1.9 %collective-permute-done.2.arrived = f32[1024,128]{1,0:T(8,128)S(1)} collective-permute-done((f32[1024,128]{1,0:T(8,128)S(1)}, f32[1024,128]{1,0:T(8,128)S(1)}, u32[]{:S(2)}, u32[]{:S(2)}) %collective-permute-start.2) | collective-permute-done | bytes 524320 | tf_op jit(solution)/shard_map/ppermute | solution.py:297
  53.4 0.0 copy-start.3
  53.4 0.6 add.31
  54.0 14.2 %all_to_all.45 = f32[16,64,128]{2,1,0:T(8,128)S(1)} all-to-all(f32[16,64,128]{2,1,0:T(8,128)S(1)} %bitcast.63), channel_id=1, replica_groups=mesh['y'=4,'xh'=2,'z'=16,'xl'=2,'core'=2] {'xl','y','xh'}, dimensions={0} | all-to-all | bytes 1048576 | tf_op jit(solution)/shard_map/all_to_all | solution.py:302
  68.2 1.0 turn.4
  69.2 8.0 %all-to-all-start.6 = ((f32[16,32,128]{2,1,0:T(8,128)}), f32[16,32,128]{2,1,0:T(8,128)S(1)}, u32[]{:S(2)}, u32[]{:S(2)}) async-start(f32[16,32,128]{2,1,0:T(8,128)} %bitcast.27), calls=%async_computation.6 | async-start | bytes 524288 | tf_op jit(solution)/shard_map/all_to_all | solution.py:311
  77.2 2.5 %collective-permute-start.3 = (f32[512,128]{1,0:T(8,128)S(1)}, f32[512,128]{1,0:T(8,128)S(1)}, u32[]{:S(2)}, u32[]{:S(2)}) collective-permute-start(f32[512,128]{1,0:T(8,128)S(1)} %get-tuple-element.189), channel_id=1, source_target_pairs={{0,2},{2,0},{1,3},{3,1},{4,6},{6,4},{5,7},{7,5},{8,10},{10,8},{9,1... | collective-permute-start | bytes 786440 | tf_op jit(solution)/shard_map/ppermute | solution.py:301
  79.8 0.0 copy-done.3
  79.8 5.7 %collective-permute-done.3.other = f32[512,128]{1,0:T(8,128)S(1)} collective-permute-done((f32[512,128]{1,0:T(8,128)S(1)}, f32[512,128]{1,0:T(8,128)S(1)}, u32[]{:S(2)}, u32[]{:S(2)}) %collective-permute-start.3) | collective-permute-done | bytes 262176 | tf_op jit(solution)/shard_map/ppermute | solution.py:301
  85.5 9.5 %all-to-all-done.6 = f32[16,32,128]{2,1,0:T(8,128)S(1)} async-done(((f32[16,32,128]{2,1,0:T(8,128)}), f32[16,32,128]{2,1,0:T(8,128)S(1)}, u32[]{:S(2)}, u32[]{:S(2)}) %all-to-all-start.6) | async-done | bytes 262176 | tf_op jit(solution)/shard_map/all_to_all | solution.py:311
  95.0 1.0 %broadcast_in_dim.10 = f32[2048,128]{1,0:T(8,128)} broadcast(f32[]{:T(128)} %constant.46.clone.1), dimensions={} | broadcast | bytes 1048580 | tf_op jit(solution)/shard_map/broadcast_in_dim | solution.py:332
  96.0 0.7 while.12
  96.7 2.7 %spread.4 = f32[2048,128]{1,0:T(8,128)} custom-call(s32[7]{0:T(128)S(1)} %get-tuple-element.372, s32[1]{0:T(128)} %get-tuple-element.321.rounds, s32[128]{0:T(128)S(1)} %dynamic-slice_bitcast_fusion.2.slots, s32[128]{0:T(128)S(1)} %get-tuple-element.374, s32[512]{0:T(512)S(1)} %get-tuple-element.371, s32[4,128]{1,0:T(4,128)S(1)} %bitcast.75, ...), custom_call_target="tpu_custom_call" | custom-call | tf_op jit(solution)/shard_map/spread/pallas_call | solution.py:230
  (3 shorter events, 0.1 us)
Async XLA Ops:
  1.3 28.2 %all-to-all-start.3 = ((f32[16,4,384]{2,1,0:T(4,128)}), f32[16,4,384]{2,1,0:T(4,128)S(1)}, u32[]{:S(2)}, u32[]{:S(2)}) async-start(f32[16,4,384]{2,1,0:T(4,128)} %broadcast_in_dim.12), calls=%async_computation.3 | async-start | bytes 196608 | tf_op jit(solution)/shard_map/all_to_all | solution.py:252
  18.3 1.9 %copy-start = (f32[3,128,4,512]{3,2,1,0:T(4,128)S(1)}, f32[3,128,4,512]{3,2,1,0:T(4,128)}, u32[]{:S(2)}) copy-start(f32[3,128,4,512]{3,2,1,0:T(4,128)} %param.8) | copy-start | bytes 9437188
  20.2 9.4 %copy-start.1 = (s32[512]{0:T(512)S(1)}, s32[512]{0:T(512)}, u32[]{:S(2)}) copy-start(s32[512]{0:T(512)} %orbital_s.3) | copy-start | bytes 6148
  20.2 9.4 %copy-start.2 = (s32[3]{0:T(128)S(1)}, s32[3]{0:T(128)}, u32[]{:S(2)}) copy-start(s32[3]{0:T(128)} %slab.5) | copy-start | bytes 40
  49.6 3.8 %collective-permute-start.2 = (f32[1024,128]{1,0:T(8,128)S(1)}, f32[1024,128]{1,0:T(8,128)S(1)}, u32[]{:S(2)}, u32[]{:S(2)}) collective-permute-start(f32[1024,128]{1,0:T(8,128)S(1)} %get-tuple-element.187), channel_id=1, source_target_pairs={{0,1},{1,0},{2,3},{3,2},{4,5},{5,4},{6,7},{7,6},{8,9},{9,8},{10,11... | collective-permute-start | bytes 1572872 | tf_op jit(solution)/shard_map/ppermute | solution.py:297
  53.4 26.4 %copy-start.3 = (s32[512]{0:T(512)S(1)}, s32[512]{0:T(512)}, u32[]{:S(2)}) copy-start(s32[512]{0:T(512)} %param.11) | copy-start | bytes 6148
  69.2 25.7 %all-to-all-start.6 = ((f32[16,32,128]{2,1,0:T(8,128)}), f32[16,32,128]{2,1,0:T(8,128)S(1)}, u32[]{:S(2)}, u32[]{:S(2)}) async-start(f32[16,32,128]{2,1,0:T(8,128)} %bitcast.27), calls=%async_computation.6 | async-start | bytes 524288 | tf_op jit(solution)/shard_map/all_to_all | solution.py:311
  77.2 8.3 %collective-permute-start.3 = (f32[512,128]{1,0:T(8,128)S(1)}, f32[512,128]{1,0:T(8,128)S(1)}, u32[]{:S(2)}, u32[]{:S(2)}) collective-permute-start(f32[512,128]{1,0:T(8,128)S(1)} %get-tuple-element.189), channel_id=1, source_target_pairs={{0,2},{2,0},{1,3},{3,1},{4,6},{6,4},{5,7},{7,5},{8,10},{10,8},{9,1... | collective-permute-start | bytes 786440 | tf_op jit(solution)/shard_map/ppermute | solution.py:301

commit v5 on v4

--- a/solution.py
+++ b/solution.py
@@ -33,11 +33,15 @@
     return lax.broadcasted_iota(jnp.int32, shape, dim)
 
 
+def count(where):
+    return jnp.sum(jnp.where(where, 1, 0), axis=0, keepdims=True)
+
+
 def column_of(row):
     return jnp.transpose(jnp.broadcast_to(row, (LANES, LANES)))
 
 
-def plan_kernel(turn, place, pair, sent, slots, targets, mates, rounds, column_s):
+def plan_kernel(turn, pair, slots, targets, rounds):
     source, lane = iota((LANES, LANES), 0), iota((LANES, LANES), 1)
     near = source < GROUP
     mate = near == (lane < GROUP)
@@ -48,10 +52,6 @@
         row = pair[q : q + 1, :]
         column = column_of(row)
         same = column == row
-
-        def count(where):
-            return jnp.sum(jnp.where(where, 1, 0), axis=0, keepdims=True)
-
         ranks.append(count(same & mate & (source < lane)))
         firsts.append(count(same & near))
         most = jnp.maximum(most, jnp.max(count(same & mate)))
@@ -65,23 +65,25 @@
         window = jnp.where((window >= 0) & (window < HALF), window, -1)
         chosen = jnp.where(one, ranks[q], window)
         base = jnp.where(one, firsts[q], HALF)
-        sent[q : q + 1, :] = chosen
         slots[q : q + 1, :] = jnp.where(chosen < 0, -1, chosen + jnp.where(later, base, 0))
         for t in range(2):
             spot = (iota((1, LANES), 1) + t * LANES) % KEPT
-            start = jnp.where(one, starts[q][t], HALF)
-            targets[q : q + 1, t * LANES : (t + 1) * LANES] = spot + start
-    column_s[...] = column_of(pair[pl.ds(place[5], 1), :])
-    mates[...] = column_s[pl.ds(pl.multiple_of(place[6] * GROUP, GROUP), GROUP), :]
-
-
-def pack_kernel(place, slab, orbital, mates, sent, near, out):
+            split_up = jnp.where(spot < HALF, spot + HALF, -1)
+            targets[q : q + 1, t * LANES : (t + 1) * LANES] = jnp.where(one, spot + starts[q][t], split_up)
+
+
+def pack_kernel(turn, place, slab, orbital, pair, near, out, column_s):
     occ, quarter, later = place[1], place[5], place[6]
     depth_row = orbital[pl.ds(occ, 1), :]
-    column = mates[...]
-    chosen = sent[pl.ds(quarter, 1), :]
+    row = pair[pl.ds(quarter, 1), :]
+    column = column_of(row)
+    column_s[...] = column
+    source, lane = iota((LANES, LANES), 0), iota((LANES, LANES), 1)
+    mate = (source < GROUP) == (lane < GROUP)
+    chosen = count((column == row) & mate & (source < lane)) - turn[0] * HALF
     chosen = jnp.where(later == 1, pltpu.roll(chosen, GROUP, 1), chosen)[:, :GROUP]
     pick = jnp.where(iota((KEPT, GROUP), 0) == chosen, 1.0, 0.0).astype(jnp.bfloat16)
+    column = column_s[pl.ds(pl.multiple_of(later * GROUP, GROUP), GROUP), :]
     for c in range(3):
         lanes = slice(c * LANES, (c + 1) * LANES)
         high, low = split(jnp.where(column == depth_row ^ slab[c], near[:, lanes], 0.0))
@@ -103,11 +105,12 @@
             high[:, at : at + LANES], low[:, at : at + LANES] = split(jnp.where(depth == label, panel, 0.0))
 
 
-def ladder_kernel(place, slab, orbital, targets, gathered, v_high, v_low, keep, send, both_t):
+def ladder_kernel(place, slab, rounds, orbital, targets, gathered, v_high, v_low, keep, send, both_t):
     occ, core = place[1], place[2]
     depth_row = orbital[pl.ds(occ, 1), :]
     depth_row = jnp.concatenate([depth_row ^ slab[c] for c in range(3)], axis=1)
     slot = iota((SLOTS, 8 * KEPT), 0)
+    kept = jnp.where(rounds[0] > 1, HALF, KEPT)
     for half in range(2):
         for x in range(2):
             quarter = 2 * x + (core ^ half)
@@ -116,6 +119,7 @@
             first = gathered[pl.ds(pl.multiple_of(quarter * 2 * KEPT, 8), KEPT), :]
             second = gathered[pl.ds(pl.multiple_of(quarter * 2 * KEPT + KEPT, 8), KEPT), :]
             second = jnp.concatenate([jnp.where(depth_row == l, second, 0.0) for l in range(8)], axis=0)
+            first = jnp.where(iota((KEPT, DEPTH), 0) < kept, first, 0.0)
             first = jnp.concatenate([first, jnp.zeros((SLOTS - KEPT, DEPTH), jnp.float32)], axis=0)
             for to, one, two in zip((at, LANES + at), split(first), split(second)):
                 both_t[to : to + SLOTS, :] = (one.astype(jnp.float32) + dot(pick, two)).astype(jnp.bfloat16)
@@ -134,14 +138,16 @@
                 for x in range(2):
                     at = (half * 2 + x) * SLOTS
                     for h in range(2):
-                        to = (((x * 4 + y) * 2 + h) * 2 + m) * SLOTS
+                        to = (((y * 2 + h) * 2 + x) * 2 + m) * SLOTS
                         out[to : to + SLOTS, :] = cut[h][at : at + SLOTS]
 
 
 def add_kernel(place, keep, arrived, summed, other):
     x = place[4]
     summed[...] = keep[...] + arrived[...]
-    other[...] = summed[pl.ds(pl.multiple_of((1 - x) * 512, 512), 512), :]
+    for block in range(8):
+        rows = pl.ds(pl.multiple_of((block * 2 + 1 - x) * GROUP, GROUP), GROUP)
+        other[block * GROUP : (block + 1) * GROUP, :] = summed[rows, :]
 
 
 def turn_kernel(arrived, out, turned):
@@ -149,8 +155,8 @@
         for m in range(2):
             rows = []
             for y in range(4):
-                at = ((y * 2 + h) * 2 + m) * SLOTS
-                rows.append(arrived[at : at + SLOTS, :] + arrived[512 + at : 512 + at + SLOTS, :])
+                at = (y * 2 + h) * 2 * GROUP + m * SLOTS
+                rows.append(arrived[at : at + SLOTS, :] + arrived[GROUP + at : GROUP + at + SLOTS, :])
             turned[...] = jnp.transpose(jnp.concatenate(rows, axis=0))
             for e in range(2):
                 for j in range(4):
@@ -173,8 +179,9 @@
         for m in range(2):
             cut = []
             for h in range(2):
-                at = ((y * 2 + h) * 2 + m) * SLOTS
-                cut.append(summed[pl.ds(pl.multiple_of(x * 512 + at, SLOTS), SLOTS), :] + other[at : at + SLOTS, :])
+                at = (y * 2 + h) * GROUP + m * SLOTS
+                mine = ((y * 2 + h) * 2 + x) * GROUP + m * SLOTS
+                cut.append(summed[pl.ds(pl.multiple_of(mine, SLOTS), SLOTS), :] + other[at : at + SLOTS, :])
             own = (
                 jnp.where(near, cut[0], pltpu.roll(cut[1], 64, 1)),
                 jnp.where(near, pltpu.roll(cut[0], 64, 1), cut[1]),
@@ -255,42 +262,44 @@
     orbital = orbital_irrep.reshape(4, LANES)
     pair = pair_irrep.reshape(4, LANES)
     labels = lax.dynamic_slice_in_dim(pair, occ, 1, 0)[0]
-    v_high, v_low = call(
-        prepare_kernel,
-        "prepare",
-        3,
-        [half, half],
-        [place, slab_irrep, orbital_irrep, orbital, panel],
-        cost=(8_000_000, 7_000_000),
-        vmem=16,
-    )
-    near, v_high, v_low = lax.optimization_barrier((near, v_high, v_low))
-
-    def one_round(turn):
-        sent, slots, targets, mates, rounds = call(
-            plan_kernel,
-            "plan",
-            2,
-            [i32((4, LANES)), i32((4, LANES)), i32((4, 2 * LANES)), i32((GROUP, LANES)), i32((1,))],
-            [turn.reshape(1), place, pair],
-            [pltpu.VMEM((LANES, LANES), jnp.int32)],
-            out_specs=[VMEM, VMEM, VMEM, VMEM, SMEM],
-        )
-        own_slots = lax.dynamic_slice_in_dim(slots, occ, 1, 0)[0]
+
+    near, late_pair, late_place = lax.optimization_barrier((near, pair, place))
+
+    def one_round(turn, near):
+        turn = turn.reshape(1)
         packed = call(
             pack_kernel,
             "pack",
-            2,
+            3,
             f32((8 * KEPT, DEPTH)),
-            [place, slab_irrep, orbital, mates, sent, near],
+            [turn, place, slab_irrep, orbital, pair, near],
+            [pltpu.VMEM((LANES, LANES), jnp.int32)],
         )
         gathered = lax.all_to_all(packed.reshape(8, KEPT, DEPTH), ("y", "xh"), 0, 0, tiled=True).reshape(8 * KEPT, DEPTH)
+        slots, targets, rounds = call(
+            plan_kernel,
+            "plan",
+            1,
+            [i32((4, LANES)), i32((4, 2 * LANES)), i32((1,))],
+            [turn, late_pair],
+            out_specs=[VMEM, VMEM, SMEM],
+        )
+        v_high, v_low = call(
+            prepare_kernel,
+            "prepare",
+            3,
+            [half, half],
+            [late_place, slab_irrep, orbital_irrep, orbital, panel],
+            cost=(8_000_000, 7_000_000),
+            vmem=16,
+        )
+        own_slots = lax.dynamic_slice_in_dim(slots, occ, 1, 0)[0]
         keep, send = call(
             ladder_kernel,
             "ladder",
-            2,
+            3,
             [f32((1024, LANES)), f32((1024, LANES))],
-            [place, slab_irrep, orbital, targets, gathered, v_high, v_low],
+            [place, slab_irrep, rounds, orbital, targets, gathered, v_high, v_low],
             [pltpu.VMEM((2 * LANES, DEPTH), jnp.bfloat16)],
             vmem=16,
         )
@@ -299,7 +308,7 @@
             add_kernel, "add", 1, [f32((1024, LANES)), f32((512, LANES))], [place, keep, arrived]
         )
         other = lax.ppermute(other, "xl", [(0, 1), (1, 0)])
-        traded = lax.all_to_all(summed.reshape(16, GROUP, LANES), ("xl", "y", "xh"), 0, 0, tiled=True)
+        traded = lax.all_to_all(summed.reshape(16, GROUP, LANES), ("y", "xh", "xl"), 0, 0, tiled=True)
         turned = call(
             turn_kernel,
             "turn",
@@ -308,8 +317,12 @@
             [traded.reshape(1024, LANES)],
             [pltpu.VMEM((LANES, LANES), jnp.float32)],
         )
+        empty = jnp.zeros((2048, LANES), jnp.float32)
+        turned, other, summed, own_slots, rounds, empty = lax.optimization_barrier(
+            (turned, other, summed, own_slots, rounds, empty)
+        )
         swapped = lax.all_to_all(turned.reshape(16, 32, LANES), "z", 0, 0, tiled=True).reshape(512, LANES)
-        return rounds, own_slots, summed, other, swapped
+        return rounds, own_slots, summed, other, swapped, empty
 
     def spread(previous, rounds, own_slots, summed, other, swapped):
         return call(
@@ -328,12 +341,11 @@
             last=ANY,
         )
 
-    rounds, own_slots, summed, other, swapped = one_round(jnp.int32(0))
-    empty = jnp.zeros((2048, LANES), jnp.float32)
+    rounds, own_slots, summed, other, swapped, empty = one_round(jnp.int32(0), near)
     empty, summed, other, swapped = lax.optimization_barrier((empty, summed, other, swapped))
     _, previous = lax.while_loop(
         lambda state: state[0] < rounds[0],
-        lambda state: (state[0] + 1, spread(state[1], *one_round(state[0]))),
+        lambda state: (state[0] + 1, spread(state[1], *one_round(state[0], near)[:-1])),
         (jnp.int32(1), empty),
     )
     filled = spread(previous, rounds, own_slots, summed, other, swapped)

time: 99.9 us -> 104 us (1.041)
  blocking collectives: 30.1 us -> 0 us
  waiting for transfers between devices: 21 us -> 41.9 us
  starting transfers between devices: 27.7 us -> 39.2 us
  Pallas kernels: 15.3 us -> 18.2 us
    all_to_all x2 -> x0, blocking collectives: 30.1 us -> none  [the longest x1 15.9 us: one_round(): lax.all_to_all(packed.reshape(8, KEPT, DEPTH), ('y', 'xh'), 0, 0, tiled=T...]
    all_to_all x0 -> x2, starting transfers between devices: none -> 14.1 us  [the longest x1 7.15 us: one_round(): lax.all_to_all(summed.reshape(16, GROUP, LANES), ('y', 'xh', 'xl'), 0, 0,...]
    all_to_all x0 -> x2, waiting for transfers between devices: none -> 9.24 us  [the longest x1 9.07 us: one_round(): lax.all_to_all(summed.reshape(16, GROUP, LANES), ('y', 'xh', 'xl'), 0, 0,...]
    all_to_all x1, waiting for transfers between devices: 4.01 us -> 12.9 us  [on_device(): lax.all_to_all(jnp.broadcast_to(mine[None], (16, 4, DEPTH)), 'z', 0, 0, t...]
    all_to_all x1, waiting for transfers between devices: 9.46 us -> 17.9 us  [one_round(): lax.all_to_all(turned.reshape(16, 32, LANES), 'z', 0, 0, tiled=True)]
    ppermute x1, waiting for transfers between devices: 5.69 us -> 0.01 us  [one_round(): other = lax.ppermute(other, 'xl', [(0, 1), (1, 0)])]
    all_to_all x1, starting transfers between devices: 8.02 us -> 4.14 us  [one_round(): lax.all_to_all(turned.reshape(16, 32, LANES), 'z', 0, 0, tiled=True)]
    pallas_call x7, Pallas kernels: 15.3 us -> 18.2 us  [call(): pl.pallas_call(kernel, out_shape=out_shape, in_specs=[SMEM] * scalars + [...]
  transfers between devices with their start and end apart: 4 -> 6, of which waited for: 4 -> 5; matrix products, arithmetic and copies ran while one was open for 0% -> 0% of each run, Pallas kernels for 7% -> 8%
where the time goes in v5:
time: 104 us
  waiting for transfers between devices  41.9 us (40%)
  starting transfers between devices  39.2 us (38%)
  Pallas kernels  18.2 us (18%)
  local copies, waits for them, and re-layouts  3.45 us (3%)
    pallas_call x7, Pallas kernels, call(): pl.pallas_call(kernel, out_shape=out_shape, in_specs=[SMEM] * scalars + [...  18.2 us
    all_to_all x1, waiting for transfers between devices, one_round(): lax.all_to_all(turned.reshape(16, 32, LANES), 'z', 0, 0, tiled=True)  17.9 us
    all_to_all x1, starting transfers between devices, on_device(): lax.all_to_all(jnp.broadcast_to(mine[None], (16, 4, DEPTH)), 'z', 0, 0, t...  15.2 us
    all_to_all x1, waiting for transfers between devices, on_device(): lax.all_to_all(jnp.broadcast_to(mine[None], (16, 4, DEPTH)), 'z', 0, 0, t...  12.9 us
    all_to_all x1, waiting for transfers between devices, one_round(): lax.all_to_all(summed.reshape(16, GROUP, LANES), ('y', 'xh', 'xl'), 0, 0,...  9.07 us
    all_to_all x1, starting transfers between devices, one_round(): lax.all_to_all(summed.reshape(16, GROUP, LANES), ('y', 'xh', 'xl'), 0, 0,...  7.15 us
    all_to_all x1, starting transfers between devices, one_round(): lax.all_to_all(packed.reshape(8, KEPT, DEPTH), ('y', 'xh'), 0, 0, tiled=T...  6.93 us
    all_to_all x1, starting transfers between devices, one_round(): lax.all_to_all(turned.reshape(16, 32, LANES), 'z', 0, 0, tiled=True)  4.14 us
  transfers between devices with their start and end apart: 6, of which 5 were waited for; matrix products, arithmetic and copies ran while one was open for 0% of the time, Pallas kernels for 8%

profile of v5, /device:TPU:32, one launch (start us, length us, event | category | flops | bytes accessed | tf_op | source)
XLA Modules:
  0.0 103.5 jit_solution(8952235618519240455)
XLA Ops:
  0.0 1.3 %broadcast_in_dim.8 = f32[16,4,384]{2,1,0:T(4,128)} broadcast(f32[4,384]{1,0:T(4,128)} %bitcast.77), dimensions={1,2} | broadcast | bytes 104448 | tf_op jit(solution)/shard_map/broadcast_in_dim | solution.py:259
  1.3 15.2 %all-to-all-start.3 = ((f32[16,4,384]{2,1,0:T(4,128)}), f32[16,4,384]{2,1,0:T(4,128)S(1)}, u32[]{:S(2)}, u32[]{:S(2)}) async-start(f32[16,4,384]{2,1,0:T(4,128)} %broadcast_in_dim.8), calls=%async_computation.3 | async-start | bytes 196608 | tf_op jit(solution)/shard_map/all_to_all | solution.py:259
  16.6 0.1 stack.27.place
  16.6 12.9 %all-to-all-done.3 = f32[16,4,384]{2,1,0:T(4,128)S(1)} async-done(((f32[16,4,384]{2,1,0:T(4,128)}), f32[16,4,384]{2,1,0:T(4,128)S(1)}, u32[]{:S(2)}, u32[]{:S(2)}) %all-to-all-start.3) | async-done | bytes 98336 | tf_op jit(solution)/shard_map/all_to_all | solution.py:259
  29.6 1.8 %pack.6 = f32[192,384]{1,0:T(8,128)} custom-call(s32[1]{0:T(128)} %constant.48.clone.1.turn, s32[7]{0:T(128)S(1)} %stack.27.place, s32[3]{0:T(128)} %slab.5, s32[4,128]{1,0:T(4,128)} %bitcast.63, s32[4,128]{1,0:T(4,128)} %bitcast.72, f32[64,384]{1,0:T(8,128)S(1)} %reshape.73.near), custom_call_target="tpu_custom_call" | custom-call | tf_op jit(solution)/shard_map/pack/pallas_call | solution.py:237
  31.4 6.9 %all-to-all-start.4 = ((f32[8,24,384]{2,1,0:T(8,128)}), f32[8,24,384]{2,1,0:T(8,128)S(1)}, u32[]{:S(2)}, u32[]{:S(2)}) async-start(f32[8,24,384]{2,1,0:T(8,128)} %bitcast.18), calls=%async_computation.4 | async-start | bytes 589824 | tf_op jit(solution)/shard_map/all_to_all | solution.py:278
  38.3 1.6 %plan.6 = (s32[4,128]{1,0:T(4,128)S(1)}, s32[4,256]{1,0:T(4,128)S(1)}, s32[1]{0:T(128)}) custom-call(s32[1]{0:T(128)} %constant.48.clone.1.turn, s32[4,128]{1,0:T(4,128)} %bitcast.73), custom_call_target="tpu_custom_call" | custom-call | tf_op jit(solution)/shard_map/plan/pallas_call | solution.py:237
  39.9 0.0 copy-start
  39.9 1.9 %copy-done = f32[3,128,4,512]{3,2,1,0:T(4,128)S(1)} copy-done((f32[3,128,4,512]{3,2,1,0:T(4,128)S(1)}, f32[3,128,4,512]{3,2,1,0:T(4,128)}, u32[]{:S(2)}) %copy-start) | copy-done | bytes 3145752
  41.8 0.0 copy-start.1
  41.8 0.0 copy-start.3
  41.8 5.3 %prepare.4 = (bf16[384,2048]{1,0:T(8,128)(2,1)}, bf16[384,2048]{1,0:T(8,128)(2,1)}) custom-call(s32[7]{0:T(128)S(1)} %stack.27.place, s32[3]{0:T(128)} %slab.5, s32[512]{0:T(512)} %orbital_s.3, s32[4,128]{1,0:T(4,128)} %bitcast.64, f32[6144,128]{1,0:T(8,128)S(1)} %bitcast.59), custom_call_target="tpu_custom_call" | custom-call | flops 8000000 | bytes 7000000 | tf_op jit(solution)/shard_map/prepare/pallas_call | solution.py:237
  47.1 0.2 all-to-all-done.4
  47.2 0.0 copy-done.1
  47.3 0.0 copy-done.3
  47.3 4.0 %ladder.6 = (f32[1024,128]{1,0:T(8,128)S(1)}, f32[1024,128]{1,0:T(8,128)S(1)}) custom-call(s32[7]{0:T(128)S(1)} %stack.27.place, s32[3]{0:T(128)S(1)} %copy-done.3, s32[1]{0:T(128)} %get-tuple-element.526.rounds, s32[4,128]{1,0:T(4,128)S(1)} %bitcast.65, s32[4,256]{1,0:T(4,128)S(1)} %get-tuple-element.365.targets, f32[192,384]{1,0:T(8,128)S(1)} %bitcast.61, ...), custom_call_target="tpu_custom_call" | custom-call | tf_op jit(solution)/shard_map/ladder/pallas_call | solution.py:237
  51.3 1.9 %collective-permute-start.2 = (f32[1024,128]{1,0:T(8,128)S(1)}, f32[1024,128]{1,0:T(8,128)S(1)}, u32[]{:S(2)}, u32[]{:S(2)}) collective-permute-start(f32[1024,128]{1,0:T(8,128)S(1)} %get-tuple-element.371), channel_id=1, source_target_pairs={{0,1},{1,0},{2,3},{3,2},{4,5},{5,4},{6,7},{7,6},{8,9},{9,8},{10,11... | collective-permute-start | bytes 1572872 | tf_op jit(solution)/shard_map/ppermute | solution.py:306
  53.2 1.9 %collective-permute-done.2.arrived = f32[1024,128]{1,0:T(8,128)S(1)} collective-permute-done((f32[1024,128]{1,0:T(8,128)S(1)}, f32[1024,128]{1,0:T(8,128)S(1)}, u32[]{:S(2)}, u32[]{:S(2)}) %collective-permute-start.2) | collective-permute-done | bytes 524320 | tf_op jit(solution)/shard_map/ppermute | solution.py:306
  55.1 0.0 copy-start.2
  55.1 1.4 %add.35 = (f32[1024,128]{1,0:T(8,128)}, f32[512,128]{1,0:T(8,128)S(1)}) custom-call(s32[7]{0:T(128)S(1)} %stack.27.place, f32[1024,128]{1,0:T(8,128)S(1)} %get-tuple-element.370.keep, f32[1024,128]{1,0:T(8,128)S(1)} %collective-permute-done.2.arrived), custom_call_target="tpu_custom_call" | custom-call | tf_op jit(solution)/shard_map/add/pallas_call | solution.py:237
  56.5 7.2 %all-to-all-start.5 = ((f32[16,64,128]{2,1,0:T(8,128)}), f32[16,64,128]{2,1,0:T(8,128)S(1)}, u32[]{:S(2)}, u32[]{:S(2)}) async-start(f32[16,64,128]{2,1,0:T(8,128)} %bitcast.23), calls=%async_computation.5 | async-start | bytes 1048576 | tf_op jit(solution)/shard_map/all_to_all | solution.py:311
  63.6 3.8 %collective-permute-start.3 = (f32[512,128]{1,0:T(8,128)S(1)}, f32[512,128]{1,0:T(8,128)S(1)}, u32[]{:S(2)}, u32[]{:S(2)}) collective-permute-start(f32[512,128]{1,0:T(8,128)S(1)} %get-tuple-element.373), channel_id=1, source_target_pairs={{0,2},{2,0},{1,3},{3,1},{4,6},{6,4},{5,7},{7,5},{8,10},{10,8},{9,1... | collective-permute-start | bytes 786440 | tf_op jit(solution)/shard_map/ppermute | solution.py:310
  67.5 9.1 %all-to-all-done.5 = f32[16,64,128]{2,1,0:T(8,128)S(1)} async-done(((f32[16,64,128]{2,1,0:T(8,128)}), f32[16,64,128]{2,1,0:T(8,128)S(1)}, u32[]{:S(2)}, u32[]{:S(2)}) %all-to-all-start.5) | async-done | bytes 524320 | tf_op jit(solution)/shard_map/all_to_all | solution.py:311
  76.5 1.0 turn.6
  77.5 0.0 collective-permute-done.3.other
  77.5 4.1 %all-to-all-start.6 = ((f32[16,32,128]{2,1,0:T(8,128)}), f32[16,32,128]{2,1,0:T(8,128)S(1)}, u32[]{:S(2)}, u32[]{:S(2)}) async-start(f32[16,32,128]{2,1,0:T(8,128)} %bitcast.27), calls=%async_computation.6 | async-start | bytes 524288 | tf_op jit(solution)/shard_map/all_to_all | solution.py:324
  81.7 0.0 copy-done.2
  81.7 17.9 %all-to-all-done.6 = f32[16,32,128]{2,1,0:T(8,128)S(1)} async-done(((f32[16,32,128]{2,1,0:T(8,128)}), f32[16,32,128]{2,1,0:T(8,128)S(1)}, u32[]{:S(2)}, u32[]{:S(2)}) %all-to-all-start.6) | async-done | bytes 262176 | tf_op jit(solution)/shard_map/all_to_all | solution.py:324
  99.6 0.1 broadcast.4
  99.7 0.7 while.14
  100.4 3.2 %spread.6 = f32[2048,128]{1,0:T(8,128)} custom-call(s32[7]{0:T(128)S(1)} %get-tuple-element.585, s32[1]{0:T(128)} %get-tuple-element.526.rounds, s32[128]{0:T(128)S(1)} %dynamic-slice_bitcast_fusion.2.slots, s32[128]{0:T(128)S(1)} %get-tuple-element.586, s32[512]{0:T(512)S(1)} %get-tuple-element.583, s32[4,128]{1,0:T(4,128)S(1)} %bitcast.71, ...), custom_call_target="tpu_custom_call" | custom-call | tf_op jit(solution)/shard_map/spread/pallas_call | solution.py:237
  (3 shorter events, 0.1 us)
Async XLA Ops:
  1.3 28.2 %all-to-all-start.3 = ((f32[16,4,384]{2,1,0:T(4,128)}), f32[16,4,384]{2,1,0:T(4,128)S(1)}, u32[]{:S(2)}, u32[]{:S(2)}) async-start(f32[16,4,384]{2,1,0:T(4,128)} %broadcast_in_dim.8), calls=%async_computation.3 | async-start | bytes 196608 | tf_op jit(solution)/shard_map/all_to_all | solution.py:259
  31.4 15.9 %all-to-all-start.4 = ((f32[8,24,384]{2,1,0:T(8,128)}), f32[8,24,384]{2,1,0:T(8,128)S(1)}, u32[]{:S(2)}, u32[]{:S(2)}) async-start(f32[8,24,384]{2,1,0:T(8,128)} %bitcast.18), calls=%async_computation.4 | async-start | bytes 589824 | tf_op jit(solution)/shard_map/all_to_all | solution.py:278
  39.9 1.9 %copy-start = (f32[3,128,4,512]{3,2,1,0:T(4,128)S(1)}, f32[3,128,4,512]{3,2,1,0:T(4,128)}, u32[]{:S(2)}) copy-start(f32[3,128,4,512]{3,2,1,0:T(4,128)} %param.8) | copy-start | bytes 9437188
  41.8 5.5 %copy-start.1 = (s32[512]{0:T(512)S(1)}, s32[512]{0:T(512)}, u32[]{:S(2)}) copy-start(s32[512]{0:T(512)} %orbital_s.3) | copy-start | bytes 6148
  41.8 5.5 %copy-start.3 = (s32[3]{0:T(128)S(1)}, s32[3]{0:T(128)}, u32[]{:S(2)}) copy-start(s32[3]{0:T(128)} %slab.5) | copy-start | bytes 40
  51.3 3.8 %collective-permute-start.2 = (f32[1024,128]{1,0:T(8,128)S(1)}, f32[1024,128]{1,0:T(8,128)S(1)}, u32[]{:S(2)}, u32[]{:S(2)}) collective-permute-start(f32[1024,128]{1,0:T(8,128)S(1)} %get-tuple-element.371), channel_id=1, source_target_pairs={{0,1},{1,0},{2,3},{3,2},{4,5},{5,4},{6,7},{7,6},{8,9},{9,8},{10,11... | collective-permute-start | bytes 1572872 | tf_op jit(solution)/shard_map/ppermute | solution.py:306
  55.1 26.6 %copy-start.2 = (s32[512]{0:T(512)S(1)}, s32[512]{0:T(512)}, u32[]{:S(2)}) copy-start(s32[512]{0:T(512)} %param.11) | copy-start | bytes 6148
  56.5 20.1 %all-to-all-start.5 = ((f32[16,64,128]{2,1,0:T(8,128)}), f32[16,64,128]{2,1,0:T(8,128)S(1)}, u32[]{:S(2)}, u32[]{:S(2)}) async-start(f32[16,64,128]{2,1,0:T(8,128)} %bitcast.23), calls=%async_computation.5 | async-start | bytes 1048576 | tf_op jit(solution)/shard_map/all_to_all | solution.py:311
  63.6 13.9 %collective-permute-start.3 = (f32[512,128]{1,0:T(8,128)S(1)}, f32[512,128]{1,0:T(8,128)S(1)}, u32[]{:S(2)}, u32[]{:S(2)}) collective-permute-start(f32[512,128]{1,0:T(8,128)S(1)} %get-tuple-element.373), channel_id=1, source_target_pairs={{0,2},{2,0},{1,3},{3,1},{4,6},{6,4},{5,7},{7,5},{8,10},{10,8},{9,1... | collective-permute-start | bytes 786440 | tf_op jit(solution)/shard_map/ppermute | solution.py:310
  77.5 22.1 %all-to-all-start.6 = ((f32[16,32,128]{2,1,0:T(8,128)}), f32[16,32,128]{2,1,0:T(8,128)S(1)}, u32[]{:S(2)}, u32[]{:S(2)}) async-start(f32[16,32,128]{2,1,0:T(8,128)} %bitcast.27), calls=%async_computation.6 | async-start | bytes 524288 | tf_op jit(solution)/shard_map/all_to_all | solution.py:324

commit v6 on v4

v6 whole, which is shorter than its diff:
```python
import functools

import jax
import jax.numpy as jnp
import numpy as np
from jax import lax
from jax.experimental import pallas as pl
from jax.experimental.pallas import tpu as pltpu
from jax.sharding import Mesh
from jax.sharding import PartitionSpec as P

LANES = 128
GROUP = 64
SLOTS = 32
FEW = 24
KEPT = 24
HALF = 16
DEPTH = 3 * LANES
VMEM = pl.BlockSpec(memory_space=pltpu.VMEM)
SMEM = pl.BlockSpec(memory_space=pltpu.SMEM)
HBM = pl.BlockSpec(memory_space=pltpu.HBM)


def split(x):
    high = x.astype(jnp.bfloat16)
    return high, (x - high.astype(jnp.float32)).astype(jnp.bfloat16)


def dot(x, y):
    return jnp.dot(x, y, preferred_element_type=jnp.float32)


def iota(shape, dim):
    return lax.broadcasted_iota(jnp.int32, shape, dim)


def count(where):
    return jnp.sum(jnp.where(where, 1, 0), axis=0, keepdims=True)


def column_of(row):
    return jnp.transpose(jnp.broadcast_to(row, (LANES, LANES)))


def plan_kernel(turn, place, pair, sent, slots, targets, mates, rounds, column_s):
    source, lane = iota((LANES, LANES), 0), iota((LANES, LANES), 1)
    near = source < GROUP
    mate = near == (lane < GROUP)
    later = iota((1, LANES), 1) >= GROUP
    ranks, firsts, starts = [], [], []
    most, total = 0, 0
    for q in range(4):
        row = pair[q : q + 1, :]
        column = column_of(row)
        same = column == row

        ranks.append(count(same & mate & (source < lane)))
        firsts.append(count(same & near))
        most = jnp.maximum(most, jnp.max(count(same & mate)))
        total = jnp.maximum(total, jnp.max(count(same)))
        starts.append([count((column == (lane + t * LANES) // KEPT) & near) for t in range(2)])
    one = (most <= KEPT) & (total <= SLOTS)
    rounds[0] = jnp.where(one, 1, (most + HALF - 1) // HALF)
    rounds[1] = jnp.where(total <= FEW, 1, 0)
    shift = turn[0] * HALF
    for q in range(4):
        window = ranks[q] - shift
        window = jnp.where((window >= 0) & (window < HALF), window, -1)
        chosen = jnp.where(one, ranks[q], window)
        base = jnp.where(one, firsts[q], HALF)
        sent[q : q + 1, :] = chosen
        slots[q : q + 1, :] = jnp.where(chosen < 0, -1, chosen + jnp.where(later, base, 0))
        for t in range(2):
            spot = (iota((1, LANES), 1) + t * LANES) % KEPT
            start = jnp.where(one, starts[q][t], HALF)
            targets[q : q + 1, t * LANES : (t + 1) * LANES] = spot + start
    column_s[...] = column_of(pair[pl.ds(place[5], 1), :])
    mates[...] = column_s[pl.ds(pl.multiple_of(place[6] * GROUP, GROUP), GROUP), :]


def pack_kernel(place, slab, orbital, mates, sent, near, out):
    occ, quarter, later = place[1], place[5], place[6]
    depth_row = orbital[pl.ds(occ, 1), :]
    column = mates[...]
    chosen = sent[pl.ds(quarter, 1), :]
    chosen = jnp.where(later == 1, pltpu.roll(chosen, GROUP, 1), chosen)[:, :GROUP]
    pick = jnp.where(iota((KEPT, GROUP), 0) == chosen, 1.0, 0.0).astype(jnp.bfloat16)
    for c in range(3):
        lanes = slice(c * LANES, (c + 1) * LANES)
        high, low = split(jnp.where(column == depth_row ^ slab[c], near[:, lanes], 0.0))
        kept = dot(pick, high) + dot(pick, low)
        for to in range(8):
            out[to * KEPT : (to + 1) * KEPT, lanes] = kept


def prepare_kernel(place, slab, orbital_s, orbital, integrals, v_high, v_low, panels, high, low, done):
    block, occ = place[0], place[1]
    depth_row = orbital[pl.ds(occ, 1), :]

    def part_of(c):
        rows = pl.ds(c * LANES * 16, LANES * 16)
        return pltpu.make_async_copy(integrals.at[rows, :], panels.at[rows, :], done.at[c])

    def results_of(c):
        rows = pl.ds(c * LANES, LANES)
        yield pltpu.make_async_copy(high.at[rows, :], v_high.at[rows, :], done.at[3 + 2 * c])
        yield pltpu.make_async_copy(low.at[rows, :], v_low.at[rows, :], done.at[4 + 2 * c])

    for c in range(3):
        part_of(c).start()
    for c in range(3):
        depth = column_of(depth_row ^ slab[c])
        part_of(c).wait()
        for y in range(4):
            lanes = orbital[y : y + 1, :]
            for i in range(4):
                panel = panels[pl.ds(c * LANES * 16 + y * 4 + i, LANES, stride=16), :]
                label = lanes ^ orbital_s[block * 4 + i]
                parts = split(jnp.where(depth == label, panel, 0.0))
                columns = slice((y * 4 + i) * LANES, (y * 4 + i + 1) * LANES)
                high[c * LANES : (c + 1) * LANES, columns], low[c * LANES : (c + 1) * LANES, columns] = parts
        for copy in results_of(c):
            copy.start()
    for c in range(3):
        for copy in results_of(c):
            copy.wait()


def ladder_kernel(size, place, slab, orbital, targets, gathered, v_high, v_low, keep, send):
    occ, core = place[1], place[2]
    depth_row = orbital[pl.ds(occ, 1), :]
    depth_row = jnp.concatenate([depth_row ^ slab[c] for c in range(3)], axis=1)
    slot = iota((size, 8 * KEPT), 0)
    highs, lows = [], []
    for half in range(2):
        for x in range(2):
            quarter = 2 * x + (core ^ half)
            pick = jnp.where(slot == targets[pl.ds(quarter, 1), : 8 * KEPT], 1.0, 0.0).astype(jnp.bfloat16)
            first = gathered[pl.ds(pl.multiple_of(quarter * 2 * KEPT, 8), KEPT), :]
            second = gathered[pl.ds(pl.multiple_of(quarter * 2 * KEPT + KEPT, 8), KEPT), :]
            second = jnp.concatenate([jnp.where(depth_row == l, second, 0.0) for l in range(8)], axis=0)
            if size > KEPT:
                first = jnp.concatenate([first, jnp.zeros((size - KEPT, DEPTH), jnp.float32)], axis=0)
            for to, one, two in zip((highs, lows), split(first), split(second)):
                to.append(one.astype(jnp.float32) + dot(pick, two))
    t_both = jnp.concatenate(highs + lows, axis=0).astype(jnp.bfloat16)
    t_high = jnp.concatenate(highs, axis=0).astype(jnp.bfloat16)
    near = iota((4 * size, LANES), 1) < 64
    for y in range(4):
        panel = slice(y * 512, (y + 1) * 512)
        parts = dot(t_both, v_high[:, panel])
        total = parts[: 4 * size] + parts[4 * size :] + dot(t_high, v_low[:, panel])
        for m in range(2):
            even, odd = total[:, 2 * m * LANES : (2 * m + 1) * LANES], total[:, (2 * m + 1) * LANES : (2 * m + 2) * LANES]
            cut = (
                jnp.where(near, even, pltpu.roll(odd, 64, 1)),
                jnp.where(near, pltpu.roll(even, 64, 1), odd),
            )
            for half, out in ((0, keep), (1, send)):
                for x in range(2):
                    at = (half * 2 + x) * size
                    for h in range(2):
                        to = (((y * 2 + h) * 2 + x) * 2 + m) * size
                        out[to : to + size, :] = cut[h][at : at + size]


def add_kernel(size, place, keep, arrived, summed, other):
    x = place[4]
    summed[...] = keep[...] + arrived[...]
    for block in range(8):
        rows = pl.ds(pl.multiple_of((block * 2 + 1 - x) * 2 * size, 8), 2 * size)
        other[block * 2 * size : (block + 1) * 2 * size, :] = summed[rows, :]


def turn_kernel(size, arrived, out, turned):
    lane = iota((16, LANES), 1)
    for h in range(2):
        for m in range(2):
            rows = []
            for y in range(4):
                at = (y * 2 + h) * 4 * size + m * size
                rows.append(arrived[at : at + size, :] + arrived[2 * size + at : 2 * size + at + size, :])
            if size < SLOTS:
                rows.append(jnp.zeros((LANES - 4 * size, LANES), jnp.float32))
            turned[...] = jnp.transpose(jnp.concatenate(rows, axis=0))
            for e in range(2):
                parts = [turned[pl.ds(e * 64 + j, 16, stride=4), :] for j in range(4)]
                if size < SLOTS:
                    last = parts.pop()
                    parts = [jnp.where(lane < 96, part, pltpu.roll(last, 96 - 32 * u, 1)) for u, part in enumerate(parts)]
                for j, part in enumerate(parts):
                    out[pl.ds(j * 8 + h * 4 + 2 * m + e, 16, stride=size), :] = part


def spread_kernel(size, place, rounds, slots, labels, orbital_s, orbital, summed, other, swapped, *rest):
    *rest, turned, packed, filled, done = rest
    held, outs = (rest[:2], rest[2:]) if size == SLOTS else ((), rest)
    block, occ, x = place[0], place[1], place[4]
    lane = iota((16, LANES), 1)
    for h in range(2):
        for i in range(4):
            parts = [swapped[pl.ds(j * 8 + h * 4 + i, 16, stride=size), :] for j in range(size // 8)]
            if size < SLOTS:
                low = jnp.where(lane < 32, pltpu.roll(parts[0], 32, 1), pltpu.roll(parts[1], 64, 1))
                parts.append(jnp.where(lane < 64, low, pltpu.roll(parts[2], 96, 1)))
            for j, part in enumerate(parts):
                turned[pl.ds(j * LANES + h * 64 + i, 16, stride=4), :] = part
    mirrored = [jnp.transpose(turned[j * LANES : (j + 1) * LANES, :]) for j in range(4)]
    near = iota((size, LANES), 1) < 64
    for y in range(4):
        for m in range(2):
            cut = []
            for h in range(2):
                at = (y * 2 + h) * 2 * size + m * size
                mine = ((y * 2 + h) * 2 + x) * 2 * size + m * size
                cut.append(summed[pl.ds(pl.multiple_of(mine, 8), size), :] + other[at : at + size, :])
            own = (
                jnp.where(near, cut[0], pltpu.roll(cut[1], 64, 1)),
                jnp.where(near, pltpu.roll(cut[0], 64, 1), cut[1]),
            )
            for e in range(2):
                j = 2 * m + e
                packed[pl.ds(y * 4 + j, size, stride=16), :] = own[e] - mirrored[j][y * size : (y + 1) * size]
    rows = []
    for y in range(4):
        for j in range(4):
            rows.append(orbital[y : y + 1, :] ^ orbital_s[block * 4 + j])
    entry = jnp.concatenate(rows, axis=0)

    def rows_of(p):
        return pl.ds(pl.multiple_of(p * 16, 16), 16)

    def store(p):
        values = packed[pl.ds(pl.multiple_of(slots[occ, p] * 16, 16), 16), :]
        filled[rows_of(p), :] = jnp.where(entry == labels[occ * LANES + p], values, 0.0)

    def part_of(part):
        share = 4 // len(outs)
        to = outs[part // share].at[pl.ds(part % share * 512, 512), :]
        return pltpu.make_async_copy(filled.at[pl.ds(part * 512, 512), :], to, done.at[part])

    def fill():
        def step(p, carry):
            store(p)
            return carry

        for part in range(4):
            lax.fori_loop(part * 32, part * 32 + 32, step, 0, unroll=8)
            part_of(part).start()

    def fill_in():
        for half in range(2):
            copy = pltpu.make_async_copy(held[half], filled.at[pl.ds(half * 1024, 1024), :], done.at[half])
            copy.start()
            copy.wait()

        def step(p, carry):
            pl.when(slots[occ, p] >= 0)(lambda: store(p))
            return carry

        lax.fori_loop(0, LANES, step, 0)
        for part in range(4):
            part_of(part).start()

    if held:
        pl.when(rounds[0] > 1)(fill_in)
        pl.when(rounds[0] <= 1)(fill)
    else:
        fill()
    for part in range(4):
        part_of(part).wait()


def call(kernel, name, scalars, out_shape, operands, scratch=(), cost=None, out_specs=None, vmem=8, any_last=0):
    return pl.pallas_call(
        kernel,
        out_shape=out_shape,
        in_specs=[SMEM] * scalars + [VMEM] * (len(operands) - scalars - any_last) + [HBM] * any_last,
        out_specs=out_specs or jax.tree.map(lambda _: VMEM, out_shape),
        scratch_shapes=list(scratch),
        compiler_params=pltpu.CompilerParams(vmem_limit_bytes=vmem * 1024 * 1024),
        cost_estimate=cost and pl.CostEstimate(flops=cost[0], bytes_accessed=cost[1], transcendentals=0),
        name=name,
    )(*operands)


def on_device(amplitudes, integrals, orbital_irrep, slab_irrep, pair_irrep):
    y, xh, z = lax.axis_index("y"), lax.axis_index("xh"), lax.axis_index("z")
    x, core = lax.axis_index("xl"), lax.axis_index("core")
    block, occ = (y * 2 + xh) * 16 + z, x * 2 + core
    place = jnp.stack([block, occ, core, 0, x, y, xh]).astype(jnp.int32)
    f32 = functools.partial(jax.ShapeDtypeStruct, dtype=jnp.float32)
    i32 = functools.partial(jax.ShapeDtypeStruct, dtype=jnp.int32)
    half = jax.ShapeDtypeStruct((DEPTH, 2048), jnp.bfloat16)

    mine = jnp.broadcast_to(amplitudes.reshape(1, 4, DEPTH), (16, 4, DEPTH))
    near = lax.all_to_all(mine, "z", 0, 0, tiled=True).reshape(GROUP, DEPTH)

    panel = integrals.reshape(3, LANES, 4, 4, LANES).transpose(0, 1, 3, 2, 4).reshape(DEPTH * 16, LANES)
    orbital = orbital_irrep.reshape(4, LANES)
    pair = pair_irrep.reshape(4, LANES)

    v_high, v_low = call(
        prepare_kernel,
        "prepare",
        3,
        [half, half],
        [place, slab_irrep, orbital_irrep, orbital, panel],
        [
            pltpu.VMEM((DEPTH * 16, LANES), jnp.float32),
            pltpu.VMEM((DEPTH, 2048), jnp.bfloat16),
            pltpu.VMEM((DEPTH, 2048), jnp.bfloat16),
            pltpu.SemaphoreType.DMA((9,)),
        ],
        cost=(8_000_000, 7_000_000),
        out_specs=[HBM, HBM],
        vmem=58,
        any_last=1,
    )

    def plan(turn):
        return call(
            plan_kernel,
            "plan",
            2,
            [i32((4, LANES)), i32((4, LANES)), i32((4, 2 * LANES)), i32((GROUP, LANES)), i32((2,))],
            [turn.reshape(1), place, pair],
            [pltpu.VMEM((LANES, LANES), jnp.int32)],
            out_specs=[VMEM, VMEM, VMEM, VMEM, SMEM],
        )

    def gather(sent, mates):
        packed = call(
            pack_kernel,
            "pack",
            2,
            f32((8 * KEPT, DEPTH)),
            [place, slab_irrep, orbital, mates, sent, near],
        )
        packed = packed.reshape(8, KEPT, DEPTH)
        return lax.all_to_all(packed, ("y", "xh"), 0, 0, tiled=True).reshape(8 * KEPT, DEPTH)

    def work(size, targets, gathered):
        keep, send = call(
            functools.partial(ladder_kernel, size),
            "ladder",
            2,
            [f32((32 * size, LANES))] * 2,
            [place, slab_irrep, orbital, targets, gathered, v_high, v_low],
            vmem=16,
        )
        arrived = lax.ppermute(send, "core", [(0, 1), (1, 0)])
        summed, other = call(
            functools.partial(add_kernel, size),
            "add",
            1,
            [f32((32 * size, LANES)), f32((16 * size, LANES))],
            [place, keep, arrived],
        )
        other = lax.ppermute(other, "xl", [(0, 1), (1, 0)])
        traded = lax.all_to_all(summed.reshape(16, 2 * size, LANES), ("y", "xh", "xl"), 0, 0, tiled=True)
        turned = call(
            functools.partial(turn_kernel, size),
            "turn",
            0,
            f32((16 * size, LANES)),
            [traded.reshape(32 * size, LANES)],
            [pltpu.VMEM((LANES, LANES), jnp.float32)],
        )
        swapped = lax.all_to_all(turned.reshape(16, size, LANES), "z", 0, 0, tiled=True).reshape(16 * size, LANES)
        return (summed, other, swapped), (keep, arrived)

    def spread(size, out_shape, rounds, slots, found, held=()):
        return call(
            functools.partial(spread_kernel, size),
            "spread",
            5,
            out_shape,
            [place, rounds, slots, pair_irrep, orbital_irrep, orbital, *found, *held],
            [
                pltpu.VMEM((512, LANES), jnp.float32),
                pltpu.VMEM((16 * size, LANES), jnp.float32),
                pltpu.VMEM((2048, LANES), jnp.float32),
                pltpu.SemaphoreType.DMA((4,)),
            ],
            out_specs=jax.tree.map(lambda _: HBM, out_shape),
            any_last=len(held),
        )

    sent, slots, targets, mates, rounds = plan(jnp.int32(0))
    near, v_high, v_low, sent, mates = lax.optimization_barrier((near, v_high, v_low, sent, mates))
    gathered = gather(sent, mates)

    def unpacked(filled):
        return filled.reshape(LANES, 4, 4, LANES).transpose(0, 2, 1, 3).reshape(LANES, 4, 512)

    def few(targets, gathered):
        found, _ = work(FEW, targets, gathered)
        return unpacked(spread(FEW, f32((2048, LANES)), rounds, slots, found))

    def many(targets, gathered):
        found, spare = work(SLOTS, targets, gathered)

        def later(state):
            turn, held = state
            sent, slots, targets, mates, _ = plan(turn)
            found, _ = work(SLOTS, targets, gather(sent, mates))
            return turn + 1, tuple(spread(SLOTS, [f32((1024, LANES))] * 2, rounds, slots, found, held))

        found, spare, turn = lax.optimization_barrier((found, spare, jnp.int32(1)))
        _, held = lax.while_loop(lambda state: state[0] < rounds[0], later, (turn, spare))
        return unpacked(spread(SLOTS, f32((2048, LANES)), rounds, slots, found, held))

    return lax.cond(rounds[1] > 0, few, many, targets, gathered)


def solution(mesh):
    devices = np.asarray(mesh.devices).reshape(4, 2, 16, 2, 2)
    fine = Mesh(devices, ("y", "xh", "z", "xl", "core"))
    blocks, groups = ("y", "xh", "z"), ("xl", "core")
    placed = (P(blocks, None, groups), P(None, groups, blocks, None), P(), P(), P())
    return jax.shard_map(
        on_device,
        mesh=fine,
        in_specs=placed,
        out_specs=P(groups, blocks, None),
        check_vma=False,
    )
```

time: 99.9 us -> 93.4 us (0.935)
  blocking collectives: 30.1 us -> 13.3 us
  waiting for transfers between devices: 21 us -> 28.2 us
  starting transfers between devices: 27.7 us -> 32.4 us
    all_to_all x2 -> x1, blocking collectives: 30.1 us -> 13.3 us  [work(): lax.all_to_all(summed.reshape(16, 2 * size, LANES), ('y', 'xh', 'xl'), 0,...]
    all_to_all x2 -> x3, waiting for transfers between devices: 13.5 us -> 21.4 us  [the longest x1 8.2 us: work(): lax.all_to_all(turned.reshape(16, size, LANES), 'z', 0, 0, tiled=True)]
    all_to_all x2 -> x3, starting transfers between devices: 23.2 us -> 28 us  [the longest x1 15.2 us: on_device(): near = lax.all_to_all(mine, 'z', 0, 0, tiled=True).reshape(GROUP, DEPTH)]
    slice x0 -> x1, local copies, waits for them, and re-layouts: none -> 1.29 us  [on_device(): return lax.cond(rounds[1] > 0, few, many, targets, gathered)]
    broadcast_in_dim x2 -> x1, local copies, waits for them, and re-layouts: 2.39 us -> 1.34 us  [on_device(): mine = jnp.broadcast_to(amplitudes.reshape(1, 4, DEPTH), (16, 4, DEPTH))]
  transfers between devices with their start and end apart: 4 -> 5, of which waited for: 4 -> 5; matrix products, arithmetic and copies ran while one was open for 0% -> 1% of each run, Pallas kernels for 7% -> 7%
where the time goes in v6:
time: 93.4 us; the launch traced here: 92.8 us
  starting transfers between devices  32.4 us (35%)
  waiting for transfers between devices  28.2 us (30%)
  Pallas kernels  14.5 us (16%)
  blocking collectives  13.3 us (14%)
  local copies, waits for them, and re-layouts  3.73 us (4%)
    all_to_all x1, starting transfers between devices, on_device(): near = lax.all_to_all(mine, 'z', 0, 0, tiled=True).reshape(GROUP, DEPTH)  15.2 us
    pallas_call x7, Pallas kernels, call(): pl.pallas_call(kernel, out_shape=out_shape, in_specs=[SMEM] * scalars + [...  14.5 us
    all_to_all x1, blocking collectives, work(): lax.all_to_all(summed.reshape(16, 2 * size, LANES), ('y', 'xh', 'xl'), 0,...  13.3 us
    all_to_all x1, waiting for transfers between devices, work(): lax.all_to_all(turned.reshape(16, size, LANES), 'z', 0, 0, tiled=True)  8.2 us
    all_to_all x1, waiting for transfers between devices, gather(): lax.all_to_all(packed, ('y', 'xh'), 0, 0, tiled=True)  7.03 us
    all_to_all x1, starting transfers between devices, gather(): lax.all_to_all(packed, ('y', 'xh'), 0, 0, tiled=True)  6.93 us
    all_to_all x1, waiting for transfers between devices, on_device(): near = lax.all_to_all(mine, 'z', 0, 0, tiled=True).reshape(GROUP, DEPTH)  6.19 us
    all_to_all x1, starting transfers between devices, work(): lax.all_to_all(turned.reshape(16, size, LANES), 'z', 0, 0, tiled=True)  5.83 us
  transfers between devices with their start and end apart: 5, of which 5 were waited for; matrix products, arithmetic and copies ran while one was open for 1% of the time, Pallas kernels for 7%

profile of v6, /device:TPU:32, one launch (start us, length us, event | category | flops | bytes accessed | tf_op | source)
XLA Modules:
  0.0 92.8 jit_solution(6133125201632937254)
XLA Ops:
  0.0 1.3 %broadcast_in_dim.8 = f32[16,4,384]{2,1,0:T(4,128)} broadcast(f32[4,384]{1,0:T(4,128)} %bitcast.94), dimensions={1,2} | broadcast | bytes 104448 | tf_op jit(solution)/shard_map/broadcast_in_dim | solution.py:296
  1.3 15.2 %all-to-all-start.7 = ((f32[16,4,384]{2,1,0:T(4,128)}), f32[16,4,384]{2,1,0:T(4,128)S(1)}, u32[]{:S(2)}, u32[]{:S(2)}) async-start(f32[16,4,384]{2,1,0:T(4,128)} %broadcast_in_dim.8), calls=%async_computation.7 | async-start | bytes 196608 | tf_op jit(solution)/shard_map/all_to_all | solution.py:297
  16.6 0.1 stack.27.place
  16.6 1.7 %plan.2 = (s32[4,128]{1,0:T(4,128)S(1)}, s32[4,128]{1,0:T(4,128)S(1)}, s32[4,256]{1,0:T(4,128)S(1)}, s32[64,128]{1,0:T(8,128)S(1)}, s32[2]{0:T(128)}) custom-call(s32[1]{0:T(128)} %constant.24.clone.1.turn, s32[7]{0:T(128)S(1)} %stack.27.place, s32[4,128]{1,0:T(4,128)} %bitcast.89), custom_call_target="tpu_custom_call" | custom-call | tf_op jit(solution)/shard_map/plan/pallas_call | solution.py:275
  18.3 0.0 copy-start
  18.3 0.0 copy-start.3
  18.3 0.0 copy-start.2
  18.4 5.0 %prepare.1 = (bf16[384,2048]{1,0:T(8,128)(2,1)}, bf16[384,2048]{1,0:T(8,128)(2,1)}) custom-call(s32[7]{0:T(128)S(1)} %stack.27.place, s32[3]{0:T(128)} %slab.3, s32[512]{0:T(512)} %orbital_s.1, s32[4,128]{1,0:T(4,128)} %bitcast.74, f32[6144,128]{1,0:T(8,128)} %bitcast.71), custom_call_target="tpu_custom_call" | custom-call | flops 8000000 | bytes 7000000 | tf_op jit(solution)/shard_map/prepare/pallas_call | solution.py:275
  23.4 6.2 %all-to-all-done.7 = f32[16,4,384]{2,1,0:T(4,128)S(1)} async-done(((f32[16,4,384]{2,1,0:T(4,128)}), f32[16,4,384]{2,1,0:T(4,128)S(1)}, u32[]{:S(2)}, u32[]{:S(2)}) %all-to-all-start.7) | async-done | bytes 98336 | tf_op jit(solution)/shard_map/all_to_all | solution.py:297
  29.6 0.0 copy-done
  29.6 0.0 copy-done.3
  29.6 1.5 %pack.2 = f32[192,384]{1,0:T(8,128)} custom-call(s32[7]{0:T(128)S(1)} %stack.27.place, s32[3]{0:T(128)S(1)} %copy-done.3, s32[4,128]{1,0:T(4,128)S(1)} %bitcast.75, s32[64,128]{1,0:T(8,128)S(1)} %get-tuple-element.191.mates, s32[4,128]{1,0:T(4,128)S(1)} %get-tuple-element.192.sent, f32[64,384]{1,0:T(8,128)S(1)} %reshape.86.near), custom_call_target="tpu_custom_call" | custom-call | tf_op jit(solution)/shard_map/pack/pallas_call | solution.py:275
  31.1 6.9 %all-to-all-start.8 = ((f32[8,24,384]{2,1,0:T(8,128)}), f32[8,24,384]{2,1,0:T(8,128)S(1)}, u32[]{:S(2)}, u32[]{:S(2)}) async-start(f32[8,24,384]{2,1,0:T(8,128)} %bitcast.39), calls=%async_computation.8 | async-start | bytes 589824 | tf_op jit(solution)/shard_map/all_to_all | solution.py:341
  38.0 1.3 %slice.6 = s32[1]{0:T(128)} slice(s32[2]{0:T(128)} %get-tuple-element.185), slice={[1:2]} | slice | bytes 8 | tf_op jit(solution)/shard_map/slice | solution.py:414
  40.0 7.0 %all-to-all-done.8 = f32[8,24,384]{2,1,0:T(8,128)S(1)} async-done(((f32[8,24,384]{2,1,0:T(8,128)}), f32[8,24,384]{2,1,0:T(8,128)S(1)}, u32[]{:S(2)}, u32[]{:S(2)}) %all-to-all-start.8) | async-done | bytes 294944 | tf_op jit(solution)/shard_map/all_to_all | solution.py:341
  47.0 0.0 copy-done.2
  47.0 44.9 %conditional.1 = (f32[128,4,512]{2,1,0:T(4,128)S(1)}) conditional(s32[]{:T(128)} %bitcast.33, (s32[7]{0:T(128)S(1)}, s32[3]{0:T(128)S(1)}, s32[4,128]{1,0:T(4,128)S(1)}, s32[4,256]{1,0:T(4,128)S(1)}, f32[192,384]{1,0:T(8,128)S(1)}, /*index=5*/bf16[384,2048]{1,0:T(8,128)(2,1)}, bf16[384,2048]{1,0:T(8,128)(2,1)}, s32[2]{0:T(128)}, ...), branch_computations={%region_0.0_spmd, %region_3.0_spmd} | conditional | flops 2 | bytes 12648933 | solution.py:414
  47.0 3.2 %ladder.4 = (f32[768,128]{1,0:T(8,128)S(1)}, f32[768,128]{1,0:T(8,128)S(1)}) custom-call(s32[7]{0:T(128)S(1)} %get-tuple-element.158.place, s32[3]{0:T(128)S(1)} %get-tuple-element.164.slab, s32[4,128]{1,0:T(4,128)S(1)} %bitcast.85, s32[4,256]{1,0:T(4,128)S(1)} %get-tuple-element.165.targets, f32[192,384]{1,0:T(8,128)S(1)} %get-tuple-element.166.gathered, ...), custom_call_target="tpu_custom_call" | custom-call | tf_op jit(solution)/shard_map/cond/branch_1_fun/ladder/pallas_call | solution.py:275
  50.2 1.9 %collective-permute-start = (f32[768,128]{1,0:T(8,128)S(1)}, f32[768,128]{1,0:T(8,128)S(1)}, u32[]{:S(2)}, u32[]{:S(2)}) collective-permute-start(f32[768,128]{1,0:T(8,128)S(1)} %get-tuple-element.170), channel_id=1, source_target_pairs={{0,1},{1,0},{2,3},{3,2},{4,5},{5,4},{6,7},{7,6},{8,9},{9,8},{10,11... | collective-permute-start | bytes 1179656 | tf_op jit(solution)/shard_map/cond/branch_1_fun/ppermute | solution.py:352
  52.1 1.7 %collective-permute-done.arrived = f32[768,128]{1,0:T(8,128)S(1)} collective-permute-done((f32[768,128]{1,0:T(8,128)S(1)}, f32[768,128]{1,0:T(8,128)S(1)}, u32[]{:S(2)}, u32[]{:S(2)}) %collective-permute-start) | collective-permute-done | bytes 393248 | tf_op jit(solution)/shard_map/cond/branch_1_fun/ppermute | solution.py:352
  53.8 0.6 add.21
  54.4 13.3 %all_to_all.45 = f32[16,48,128]{2,1,0:T(8,128)S(1)} all-to-all(f32[16,48,128]{2,1,0:T(8,128)S(1)} %bitcast.68), channel_id=1, replica_groups=mesh['y'=4,'xh'=2,'z'=16,'xl'=2,'core'=2] {'y','xh','xl'}, dimensions={0} | all-to-all | bytes 786432 | tf_op jit(solution)/shard_map/cond/branch_1_fun/all_to_all | solution.py:361
  67.7 0.9 %turn.4 = f32[384,128]{1,0:T(8,128)} custom-call(f32[768,128]{1,0:T(8,128)S(1)} %bitcast.67), custom_call_target="tpu_custom_call" | custom-call | tf_op jit(solution)/shard_map/cond/branch_1_fun/turn/pallas_call | solution.py:275
  68.6 5.8 %all-to-all-start.1 = ((f32[16,24,128]{2,1,0:T(8,128)}), f32[16,24,128]{2,1,0:T(8,128)S(1)}, u32[]{:S(2)}, u32[]{:S(2)}) async-start(f32[16,24,128]{2,1,0:T(8,128)} %bitcast.19), calls=%async_computation.1 | async-start | bytes 393216 | tf_op jit(solution)/shard_map/cond/branch_1_fun/all_to_all | solution.py:370
  74.4 2.5 %collective-permute-start.1 = (f32[384,128]{1,0:T(8,128)S(1)}, f32[384,128]{1,0:T(8,128)S(1)}, u32[]{:S(2)}, u32[]{:S(2)}) collective-permute-start(f32[384,128]{1,0:T(8,128)S(1)} %get-tuple-element.172), channel_id=1, source_target_pairs={{0,2},{2,0},{1,3},{3,1},{4,6},{6,4},{5,7},{7,5},{8,10},{10,8},{9,1... | collective-permute-start | bytes 589832 | tf_op jit(solution)/shard_map/cond/branch_1_fun/ppermute | solution.py:360
  76.9 5.1 %collective-permute-done.1.other = f32[384,128]{1,0:T(8,128)S(1)} collective-permute-done((f32[384,128]{1,0:T(8,128)S(1)}, f32[384,128]{1,0:T(8,128)S(1)}, u32[]{:S(2)}, u32[]{:S(2)}) %collective-permute-start.1) | collective-permute-done | bytes 196640 | tf_op jit(solution)/shard_map/cond/branch_1_fun/ppermute | solution.py:360
  82.0 8.2 %all-to-all-done.1 = f32[16,24,128]{2,1,0:T(8,128)S(1)} async-done(((f32[16,24,128]{2,1,0:T(8,128)}), f32[16,24,128]{2,1,0:T(8,128)S(1)}, u32[]{:S(2)}, u32[]{:S(2)}) %all-to-all-start.1) | async-done | bytes 196640 | tf_op jit(solution)/shard_map/cond/branch_1_fun/all_to_all | solution.py:370
  90.2 1.7 %spread.4 = f32[2048,128]{1,0:T(8,128)S(1)} custom-call(s32[7]{0:T(128)S(1)} %get-tuple-element.158.place, s32[2]{0:T(128)} %get-tuple-element.159.rounds, s32[4,128]{1,0:T(4,128)S(1)} %get-tuple-element.160.slots, s32[512]{0:T(512)S(1)} %get-tuple-element.161.labels, s32[512]{0:T(512)S(1)} %get-tuple-element.162.orbital_s, s32[4,128]{1,0:T(4,128)S(1)} %bitcast.86, ...), custom_call_target="tpu_custom_call" | custom-call | tf_op jit(solution)/shard_map/cond/branch_1_fun/spread/pallas_call | solution.py:275
  91.9 0.0 copy-start.1
  91.9 1.0 %copy-done.1 = f32[128,4,512]{2,1,0:T(4,128)} copy-done((f32[128,4,512]{2,1,0:T(4,128)}, f32[128,4,512]{2,1,0:T(4,128)S(1)}, u32[]{:S(2)}) %copy-start.1) | copy-done | bytes 1048600
  (1 shorter events, 0.0 us)
Async XLA Ops:
  1.3 28.2 %all-to-all-start.7 = ((f32[16,4,384]{2,1,0:T(4,128)}), f32[16,4,384]{2,1,0:T(4,128)S(1)}, u32[]{:S(2)}, u32[]{:S(2)}) async-start(f32[16,4,384]{2,1,0:T(4,128)} %broadcast_in_dim.8), calls=%async_computation.7 | async-start | bytes 196608 | tf_op jit(solution)/shard_map/all_to_all | solution.py:297
  18.3 11.3 %copy-start = (s32[512]{0:T(512)S(1)}, s32[512]{0:T(512)}, u32[]{:S(2)}) copy-start(s32[512]{0:T(512)} %orbital_s.1) | copy-start | bytes 6148
  18.3 11.3 %copy-start.3 = (s32[3]{0:T(128)S(1)}, s32[3]{0:T(128)}, u32[]{:S(2)}) copy-start(s32[3]{0:T(128)} %slab.3) | copy-start | bytes 40
  18.3 28.6 %copy-start.2 = (s32[512]{0:T(512)S(1)}, s32[512]{0:T(512)}, u32[]{:S(2)}) copy-start(s32[512]{0:T(512)} %param.13) | copy-start | bytes 6148
  31.1 15.9 %all-to-all-start.8 = ((f32[8,24,384]{2,1,0:T(8,128)}), f32[8,24,384]{2,1,0:T(8,128)S(1)}, u32[]{:S(2)}, u32[]{:S(2)}) async-start(f32[8,24,384]{2,1,0:T(8,128)} %bitcast.39), calls=%async_computation.8 | async-start | bytes 589824 | tf_op jit(solution)/shard_map/all_to_all | solution.py:341
  50.2 3.6 %collective-permute-start = (f32[768,128]{1,0:T(8,128)S(1)}, f32[768,128]{1,0:T(8,128)S(1)}, u32[]{:S(2)}, u32[]{:S(2)}) collective-permute-start(f32[768,128]{1,0:T(8,128)S(1)} %get-tuple-element.170), channel_id=1, source_target_pairs={{0,1},{1,0},{2,3},{3,2},{4,5},{5,4},{6,7},{7,6},{8,9},{9,8},{10,11... | collective-permute-start | bytes 1179656 | tf_op jit(solution)/shard_map/cond/branch_1_fun/ppermute | solution.py:352
  68.6 21.6 %all-to-all-start.1 = ((f32[16,24,128]{2,1,0:T(8,128)}), f32[16,24,128]{2,1,0:T(8,128)S(1)}, u32[]{:S(2)}, u32[]{:S(2)}) async-start(f32[16,24,128]{2,1,0:T(8,128)} %bitcast.19), calls=%async_computation.1 | async-start | bytes 393216 | tf_op jit(solution)/shard_map/cond/branch_1_fun/all_to_all | solution.py:370
  74.4 7.6 %collective-permute-start.1 = (f32[384,128]{1,0:T(8,128)S(1)}, f32[384,128]{1,0:T(8,128)S(1)}, u32[]{:S(2)}, u32[]{:S(2)}) collective-permute-start(f32[384,128]{1,0:T(8,128)S(1)} %get-tuple-element.172), channel_id=1, source_target_pairs={{0,2},{2,0},{1,3},{3,1},{4,6},{6,4},{5,7},{7,5},{8,10},{10,8},{9,1... | collective-permute-start | bytes 589832 | tf_op jit(solution)/shard_map/cond/branch_1_fun/ppermute | solution.py:360
  91.9 1.0 %copy-start.1 = (f32[128,4,512]{2,1,0:T(4,128)}, f32[128,4,512]{2,1,0:T(4,128)S(1)}, u32[]{:S(2)}) copy-start(f32[128,4,512]{2,1,0:T(4,128)S(1)} %get-tuple-element.384) | copy-start | bytes 3145732

commit v7 on v6

--- a/solution.py
+++ b/solution.py
@@ -12,7 +12,7 @@
 LANES = 128
 GROUP = 64
 SLOTS = 32
-FEW = 24
+FEWER = (24, 28)
 KEPT = 24
 HALF = 16
 DEPTH = 3 * LANES
@@ -42,7 +42,7 @@
     return jnp.transpose(jnp.broadcast_to(row, (LANES, LANES)))
 
 
-def plan_kernel(turn, place, pair, sent, slots, targets, mates, rounds, column_s):
+def plan_kernel(turn, place, pair, sent, slots, targets, mates, rounds, choice, column_s):
     source, lane = iota((LANES, LANES), 0), iota((LANES, LANES), 1)
     near = source < GROUP
     mate = near == (lane < GROUP)
@@ -61,7 +61,8 @@
         starts.append([count((column == (lane + t * LANES) // KEPT) & near) for t in range(2)])
     one = (most <= KEPT) & (total <= SLOTS)
     rounds[0] = jnp.where(one, 1, (most + HALF - 1) // HALF)
-    rounds[1] = jnp.where(total <= FEW, 1, 0)
+    fewer = jnp.where(total <= FEWER[0], 0, jnp.where(total <= FEWER[1], 1, 2))
+    choice[0] = jnp.where(one, fewer, 2)
     shift = turn[0] * HALF
     for q in range(4):
         window = ranks[q] - shift
@@ -130,7 +131,8 @@
     occ, core = place[1], place[2]
     depth_row = orbital[pl.ds(occ, 1), :]
     depth_row = jnp.concatenate([depth_row ^ slab[c] for c in range(3)], axis=1)
-    slot = iota((size, 8 * KEPT), 0)
+    width = -(-size // 8) * 8
+    slot = iota((width, 8 * KEPT), 0)
     highs, lows = [], []
     for half in range(2):
         for x in range(2):
@@ -139,17 +141,18 @@
             first = gathered[pl.ds(pl.multiple_of(quarter * 2 * KEPT, 8), KEPT), :]
             second = gathered[pl.ds(pl.multiple_of(quarter * 2 * KEPT + KEPT, 8), KEPT), :]
             second = jnp.concatenate([jnp.where(depth_row == l, second, 0.0) for l in range(8)], axis=0)
-            if size > KEPT:
-                first = jnp.concatenate([first, jnp.zeros((size - KEPT, DEPTH), jnp.float32)], axis=0)
+            if width > KEPT:
+                first = jnp.concatenate([first, jnp.zeros((width - KEPT, DEPTH), jnp.float32)], axis=0)
             for to, one, two in zip((highs, lows), split(first), split(second)):
                 to.append(one.astype(jnp.float32) + dot(pick, two))
+    rows = 4 * width
     t_both = jnp.concatenate(highs + lows, axis=0).astype(jnp.bfloat16)
     t_high = jnp.concatenate(highs, axis=0).astype(jnp.bfloat16)
-    near = iota((4 * size, LANES), 1) < 64
+    near = iota((rows, LANES), 1) < 64
     for y in range(4):
         panel = slice(y * 512, (y + 1) * 512)
         parts = dot(t_both, v_high[:, panel])
-        total = parts[: 4 * size] + parts[4 * size :] + dot(t_high, v_low[:, panel])
+        total = parts[:rows] + parts[rows:] + dot(t_high, v_low[:, panel])
         for m in range(2):
             even, odd = total[:, 2 * m * LANES : (2 * m + 1) * LANES], total[:, (2 * m + 1) * LANES : (2 * m + 2) * LANES]
             cut = (
@@ -158,7 +161,7 @@
             )
             for half, out in ((0, keep), (1, send)):
                 for x in range(2):
-                    at = (half * 2 + x) * size
+                    at = (half * 2 + x) * width
                     for h in range(2):
                         to = (((y * 2 + h) * 2 + x) * 2 + m) * size
                         out[to : to + size, :] = cut[h][at : at + size]
@@ -170,6 +173,12 @@
     for block in range(8):
         rows = pl.ds(pl.multiple_of((block * 2 + 1 - x) * 2 * size, 8), 2 * size)
         other[block * 2 * size : (block + 1) * 2 * size, :] = summed[rows, :]
+
+
+def folded(size):
+    spare, gap = LANES - 4 * size, SLOTS - size
+    for t in range(gap):
+        yield size + t, [(u * gap + t, spare * u) for u in range(size // gap)]
 
 
 def turn_kernel(size, arrived, out, turned):
@@ -182,14 +191,18 @@
                 rows.append(arrived[at : at + size, :] + arrived[2 * size + at : 2 * size + at + size, :])
             if size < SLOTS:
                 rows.append(jnp.zeros((LANES - 4 * size, LANES), jnp.float32))
-            turned[...] = jnp.transpose(jnp.concatenate(rows, axis=0))
-            for e in range(2):
-                parts = [turned[pl.ds(e * 64 + j, 16, stride=4), :] for j in range(4)]
-                if size < SLOTS:
-                    last = parts.pop()
-                    parts = [jnp.where(lane < 96, part, pltpu.roll(last, 96 - 32 * u, 1)) for u, part in enumerate(parts)]
-                for j, part in enumerate(parts):
-                    out[pl.ds(j * 8 + h * 4 + 2 * m + e, 16, stride=size), :] = part
+            at = (h * 2 + m) * LANES
+            turned[at : at + LANES, :] = jnp.transpose(jnp.concatenate(rows, axis=0))
+    parts = []
+    for j in range(4):
+        for h in range(2):
+            for i in range(4):
+                parts.append(turned[pl.ds((h * 2 + i // 2) * LANES + i % 2 * 64 + j, 16, stride=4), :])
+    for last, pieces in folded(size):
+        for row, at in pieces:
+            parts[row] = jnp.where(lane < 4 * size, parts[row], pltpu.roll(parts[last], 4 * size - at, 1))
+    for row in range(size):
+        out[pl.ds(row, 16, stride=size), :] = parts[row]
 
 
 def spread_kernel(size, place, rounds, slots, labels, orbital_s, orbital, summed, other, swapped, *rest):
@@ -197,14 +210,17 @@
     held, outs = (rest[:2], rest[2:]) if size == SLOTS else ((), rest)
     block, occ, x = place[0], place[1], place[4]
     lane = iota((16, LANES), 1)
-    for h in range(2):
-        for i in range(4):
-            parts = [swapped[pl.ds(j * 8 + h * 4 + i, 16, stride=size), :] for j in range(size // 8)]
-            if size < SLOTS:
-                low = jnp.where(lane < 32, pltpu.roll(parts[0], 32, 1), pltpu.roll(parts[1], 64, 1))
-                parts.append(jnp.where(lane < 64, low, pltpu.roll(parts[2], 96, 1)))
-            for j, part in enumerate(parts):
-                turned[pl.ds(j * LANES + h * 64 + i, 16, stride=4), :] = part
+    parts = [swapped[pl.ds(row, 16, stride=size), :] for row in range(size)]
+    for last, pieces in folded(size):
+        whole = None
+        for row, at in pieces:
+            piece = pltpu.roll(parts[row], (at - 4 * size) % LANES, 1)
+            whole = piece if whole is None else jnp.where(lane < at, whole, piece)
+        parts.append(whole)
+    for j in range(4):
+        for h in range(2):
+            for i in range(4):
+                turned[pl.ds(j * LANES + h * 64 + i, 16, stride=4), :] = parts[j * 8 + h * 4 + i]
     mirrored = [jnp.transpose(turned[j * LANES : (j + 1) * LANES, :]) for j in range(4)]
     near = iota((size, LANES), 1) < 64
     for y in range(4):
@@ -212,8 +228,8 @@
             cut = []
             for h in range(2):
                 at = (y * 2 + h) * 2 * size + m * size
-                mine = ((y * 2 + h) * 2 + x) * 2 * size + m * size
-                cut.append(summed[pl.ds(pl.multiple_of(mine, 8), size), :] + other[at : at + size, :])
+                mine = summed[pl.ds(pl.multiple_of(((y * 2 + h) * 2 + x) * 2 * size, 8), 2 * size), :]
+                cut.append(mine[m * size : (m + 1) * size] + other[at : at + size, :])
             own = (
                 jnp.where(near, cut[0], pltpu.roll(cut[1], 64, 1)),
                 jnp.where(near, pltpu.roll(cut[0], 64, 1), cut[1]),
@@ -323,10 +339,10 @@
             plan_kernel,
             "plan",
             2,
-            [i32((4, LANES)), i32((4, LANES)), i32((4, 2 * LANES)), i32((GROUP, LANES)), i32((2,))],
+            [i32((4, LANES)), i32((4, LANES)), i32((4, 2 * LANES)), i32((GROUP, LANES)), i32((1,)), i32((1,))],
             [turn.reshape(1), place, pair],
             [pltpu.VMEM((LANES, LANES), jnp.int32)],
-            out_specs=[VMEM, VMEM, VMEM, VMEM, SMEM],
+            out_specs=[VMEM, VMEM, VMEM, VMEM, SMEM, SMEM],
         )
 
     def gather(sent, mates):
@@ -365,9 +381,11 @@
             0,
             f32((16 * size, LANES)),
             [traded.reshape(32 * size, LANES)],
-            [pltpu.VMEM((LANES, LANES), jnp.float32)],
-        )
-        swapped = lax.all_to_all(turned.reshape(16, size, LANES), "z", 0, 0, tiled=True).reshape(16 * size, LANES)
+            [pltpu.VMEM((512, LANES), jnp.float32)],
+        )
+        tile = 4 if size % 8 else 8
+        swapped = lax.all_to_all(turned.reshape(16, size // tile, tile, LANES), "z", 0, 0, tiled=True)
+        swapped = swapped.reshape(16 * size, LANES)
         return (summed, other, swapped), (keep, arrived)
 
     def spread(size, out_shape, rounds, slots, found, held=()):
@@ -387,23 +405,23 @@
             any_last=len(held),
         )
 
-    sent, slots, targets, mates, rounds = plan(jnp.int32(0))
+    sent, slots, targets, mates, rounds, choice = plan(jnp.int32(0))
     near, v_high, v_low, sent, mates = lax.optimization_barrier((near, v_high, v_low, sent, mates))
     gathered = gather(sent, mates)
 
     def unpacked(filled):
         return filled.reshape(LANES, 4, 4, LANES).transpose(0, 2, 1, 3).reshape(LANES, 4, 512)
 
-    def few(targets, gathered):
-        found, _ = work(FEW, targets, gathered)
-        return unpacked(spread(FEW, f32((2048, LANES)), rounds, slots, found))
+    def few(size, targets, gathered):
+        found, _ = work(size, targets, gathered)
+        return unpacked(spread(size, f32((2048, LANES)), rounds, slots, found))
 
     def many(targets, gathered):
         found, spare = work(SLOTS, targets, gathered)
 
         def later(state):
             turn, held = state
-            sent, slots, targets, mates, _ = plan(turn)
+            sent, slots, targets, mates, _, _ = plan(turn)
             found, _ = work(SLOTS, targets, gather(sent, mates))
             return turn + 1, tuple(spread(SLOTS, [f32((1024, LANES))] * 2, rounds, slots, found, held))
 
@@ -411,7 +429,8 @@
         _, held = lax.while_loop(lambda state: state[0] < rounds[0], later, (turn, spare))
         return unpacked(spread(SLOTS, f32((2048, LANES)), rounds, slots, found, held))
 
-    return lax.cond(rounds[1] > 0, few, many, targets, gathered)
+    ways = [functools.partial(few, size) for size in FEWER] + [many]
+    return lax.switch(choice[0], ways, targets, gathered)
 
 
 def solution(mesh):

time: 93.4 us -> 96.2 us (1.030)
  waiting for transfers between devices: 28.2 us -> 30.7 us
  local copies, waits for them, and re-layouts: 3.73 us -> 1.48 us
  Pallas kernels: 14.5 us -> 15.9 us
    pallas_call x7, Pallas kernels: 14.5 us -> 15.9 us  [call(): pl.pallas_call(kernel, out_shape=out_shape, in_specs=[SMEM] * scalars + [...]
    all_to_all x1, waiting for transfers between devices: 7.03 us -> 8.34 us  [gather(): lax.all_to_all(packed, ('y', 'xh'), 0, 0, tiled=True)]
    slice x1 -> x0, local copies, waits for them, and re-layouts: 1.29 us -> none  [on_device(): return lax.cond(rounds[1] > 0, few, many, targets, gathered)]
    unnamed x8 -> x6, local copies, waits for them, and re-layouts: 0.98 us -> 0.02 us
  transfers between devices with their start and end apart: 5 -> 5, of which waited for: 5 -> 5; matrix products, arithmetic and copies ran while one was open for 1% -> 0% of each run, Pallas kernels for 7% -> 7%
where the time goes in v7:
time: 96.2 us; the launch traced here: 95.6 us
  starting transfers between devices  32.4 us (34%)
  waiting for transfers between devices  30.7 us (32%)
  Pallas kernels  15.9 us (17%)
  blocking collectives  14 us (15%)
  local copies, waits for them, and re-layouts  1.48 us (2%)
    pallas_call x7, Pallas kernels, call(): pl.pallas_call(kernel, out_shape=out_shape, in_specs=[SMEM] * scalars + [...  15.9 us
    all_to_all x1, starting transfers between devices, on_device(): near = lax.all_to_all(mine, 'z', 0, 0, tiled=True).reshape(GROUP, DEPTH)  15.2 us
    all_to_all x1, blocking collectives, work(): lax.all_to_all(summed.reshape(16, 2 * size, LANES), ('y', 'xh', 'xl'), 0,...  14 us
    all_to_all x1, waiting for transfers between devices, work(): lax.all_to_all(turned.reshape(16, size // tile, tile, LANES), 'z', 0, 0,...  8.97 us
    all_to_all x1, waiting for transfers between devices, gather(): lax.all_to_all(packed, ('y', 'xh'), 0, 0, tiled=True)  8.34 us
    all_to_all x1, starting transfers between devices, gather(): lax.all_to_all(packed, ('y', 'xh'), 0, 0, tiled=True)  6.93 us
    all_to_all x1, waiting for transfers between devices, on_device(): near = lax.all_to_all(mine, 'z', 0, 0, tiled=True).reshape(GROUP, DEPTH)  6.2 us
    all_to_all x1, starting transfers between devices, work(): lax.all_to_all(turned.reshape(16, size // tile, tile, LANES), 'z', 0, 0,...  5.84 us
  transfers between devices with their start and end apart: 5, of which 5 were waited for; matrix products, arithmetic and copies ran while one was open for 0% of the time, Pallas kernels for 7%

profile of v7, /device:TPU:32, one launch (start us, length us, event | category | flops | bytes accessed | tf_op | source)
XLA Modules:
  0.0 95.6 jit_solution(1445297803425946636)
XLA Ops:
  0.0 1.3 %broadcast_in_dim.8 = f32[16,4,384]{2,1,0:T(4,128)} broadcast(f32[4,384]{1,0:T(4,128)} %bitcast.106), dimensions={1,2} | broadcast | bytes 104448 | tf_op jit(solution)/shard_map/broadcast_in_dim | solution.py:312
  1.3 15.2 %all-to-all-start.9 = ((f32[16,4,384]{2,1,0:T(4,128)}), f32[16,4,384]{2,1,0:T(4,128)S(1)}, u32[]{:S(2)}, u32[]{:S(2)}) async-start(f32[16,4,384]{2,1,0:T(4,128)} %broadcast_in_dim.8), calls=%async_computation.9 | async-start | bytes 196608 | tf_op jit(solution)/shard_map/all_to_all | solution.py:313
  16.6 0.1 stack.27.place
  16.6 1.7 %plan.2 = (s32[4,128]{1,0:T(4,128)S(1)}, s32[4,128]{1,0:T(4,128)S(1)}, s32[4,256]{1,0:T(4,128)S(1)}, s32[64,128]{1,0:T(8,128)S(1)}, s32[1]{0:T(128)}, /*index=5*/s32[1]{0:T(128)}) custom-call(s32[1]{0:T(128)} %constant.25.clone.1.turn, s32[7]{0:T(128)S(1)} %stack.27.place, s32[4,128]{1,0:T(4,128)} %bitcast.101), custom_call_target="tpu_custom_call" | custom-call | tf_op jit(solution)/shard_map/plan/pallas_call | solution.py:291
  18.3 0.0 copy-start
  18.3 0.0 copy-start.2
  18.4 0.0 copy-start.1
  18.4 5.0 %prepare.1 = (bf16[384,2048]{1,0:T(8,128)(2,1)}, bf16[384,2048]{1,0:T(8,128)(2,1)}) custom-call(s32[7]{0:T(128)S(1)} %stack.27.place, s32[3]{0:T(128)} %slab.3, s32[512]{0:T(512)} %orbital_s.1, s32[4,128]{1,0:T(4,128)} %bitcast.85, f32[6144,128]{1,0:T(8,128)} %bitcast.84), custom_call_target="tpu_custom_call" | custom-call | flops 8000000 | bytes 7000000 | tf_op jit(solution)/shard_map/prepare/pallas_call | solution.py:291
  23.4 6.2 %all-to-all-done.9 = f32[16,4,384]{2,1,0:T(4,128)S(1)} async-done(((f32[16,4,384]{2,1,0:T(4,128)}), f32[16,4,384]{2,1,0:T(4,128)S(1)}, u32[]{:S(2)}, u32[]{:S(2)}) %all-to-all-start.9) | async-done | bytes 98336 | tf_op jit(solution)/shard_map/all_to_all | solution.py:313
  29.6 0.0 copy-done
  29.6 0.0 copy-done.2
  29.6 1.5 %pack.2 = f32[192,384]{1,0:T(8,128)} custom-call(s32[7]{0:T(128)S(1)} %stack.27.place, s32[3]{0:T(128)S(1)} %copy-done.2, s32[4,128]{1,0:T(4,128)S(1)} %bitcast.86, s32[64,128]{1,0:T(8,128)S(1)} %get-tuple-element.230.mates, s32[4,128]{1,0:T(4,128)S(1)} %get-tuple-element.231.sent, f32[64,384]{1,0:T(8,128)S(1)} %reshape.103.near), custom_call_target="tpu_custom_call" | custom-call | tf_op jit(solution)/shard_map/pack/pallas_call | solution.py:291
  31.1 6.9 %all-to-all-start.10 = ((f32[8,24,384]{2,1,0:T(8,128)}), f32[8,24,384]{2,1,0:T(8,128)S(1)}, u32[]{:S(2)}, u32[]{:S(2)}) async-start(f32[8,24,384]{2,1,0:T(8,128)} %bitcast.48), calls=%async_computation.10 | async-start | bytes 589824 | tf_op jit(solution)/shard_map/all_to_all | solution.py:357
  38.7 8.3 %all-to-all-done.10 = f32[8,24,384]{2,1,0:T(8,128)S(1)} async-done(((f32[8,24,384]{2,1,0:T(8,128)}), f32[8,24,384]{2,1,0:T(8,128)S(1)}, u32[]{:S(2)}, u32[]{:S(2)}) %all-to-all-start.10) | async-done | bytes 294944 | tf_op jit(solution)/shard_map/all_to_all | solution.py:357
  47.0 0.0 copy-done.1
  47.0 48.4 %conditional.1 = (f32[128,4,512]{2,1,0:T(4,128)}) conditional(s32[]{:T(128)} %bitcast.42, (s32[7]{0:T(128)S(1)}, s32[3]{0:T(128)S(1)}, s32[4,128]{1,0:T(4,128)S(1)}, s32[4,256]{1,0:T(4,128)S(1)}, f32[192,384]{1,0:T(8,128)S(1)}, /*index=5*/bf16[384,2048]{1,0:T(8,128)(2,1)}, bf16[384,2048]{1,0:T(8,128)(2,1)}, s32[1]{0:T(128)}, ...), branch_computations={%region_0.0_spmd, %region_1.0_spmd, %region_2.0_spmd} | conditional | flops 2 | bytes 12648933 | solution.py:433
  47.0 3.3 %ladder.5 = (f32[896,128]{1,0:T(8,128)S(1)}, f32[896,128]{1,0:T(8,128)S(1)}) custom-call(s32[7]{0:T(128)S(1)} %get-tuple-element.146.place, s32[3]{0:T(128)S(1)} %get-tuple-element.152.slab, s32[4,128]{1,0:T(4,128)S(1)} %bitcast.92, s32[4,256]{1,0:T(4,128)S(1)} %get-tuple-element.153.targets, f32[192,384]{1,0:T(8,128)S(1)} %get-tuple-element.154.gathered, ...), custom_call_target="tpu_custom_call" | custom-call | tf_op jit(solution)/shard_map/cond/branch_1_fun/ladder/pallas_call | solution.py:291
  50.3 1.9 %collective-permute-start.2 = (f32[896,128]{1,0:T(8,128)S(1)}, f32[896,128]{1,0:T(8,128)S(1)}, u32[]{:S(2)}, u32[]{:S(2)}) collective-permute-start(f32[896,128]{1,0:T(8,128)S(1)} %get-tuple-element.158), channel_id=1, source_target_pairs={{0,1},{1,0},{2,3},{3,2},{4,5},{5,4},{6,7},{7,6},{8,9},{9,8},{10,11... | collective-permute-start | bytes 1376264 | tf_op jit(solution)/shard_map/cond/branch_1_fun/ppermute | solution.py:368
  52.2 1.8 %collective-permute-done.2.arrived = f32[896,128]{1,0:T(8,128)S(1)} collective-permute-done((f32[896,128]{1,0:T(8,128)S(1)}, f32[896,128]{1,0:T(8,128)S(1)}, u32[]{:S(2)}, u32[]{:S(2)}) %collective-permute-start.2) | collective-permute-done | bytes 458784 | tf_op jit(solution)/shard_map/cond/branch_1_fun/ppermute | solution.py:368
  54.0 0.6 add.22
  54.6 14.0 %all_to_all.53 = f32[16,56,128]{2,1,0:T(8,128)S(1)} all-to-all(f32[16,56,128]{2,1,0:T(8,128)S(1)} %bitcast.74), channel_id=1, replica_groups=mesh['y'=4,'xh'=2,'z'=16,'xl'=2,'core'=2] {'y','xh','xl'}, dimensions={0} | all-to-all | bytes 917504 | tf_op jit(solution)/shard_map/cond/branch_1_fun/all_to_all | solution.py:377
  68.6 0.9 turn.5
  69.6 5.8 %all-to-all-start.3 = ((f32[16,7,4,128]{3,2,1,0:T(4,128)}), f32[16,7,4,128]{3,2,1,0:T(4,128)S(1)}, u32[]{:S(2)}, u32[]{:S(2)}) async-start(f32[16,7,4,128]{3,2,1,0:T(4,128)} %bitcast.11), calls=%async_computation.3 | async-start | bytes 458752 | tf_op jit(solution)/shard_map/cond/branch_1_fun/all_to_all | solution.py:387
  75.4 2.5 %collective-permute-start.3 = (f32[448,128]{1,0:T(8,128)S(1)}, f32[448,128]{1,0:T(8,128)S(1)}, u32[]{:S(2)}, u32[]{:S(2)}) collective-permute-start(f32[448,128]{1,0:T(8,128)S(1)} %get-tuple-element.160), channel_id=1, source_target_pairs={{0,2},{2,0},{1,3},{3,1},{4,6},{6,4},{5,7},{7,5},{8,10},{10,8},{9,1... | collective-permute-start | bytes 688136 | tf_op jit(solution)/shard_map/cond/branch_1_fun/ppermute | solution.py:376
  77.9 5.4 %collective-permute-done.3.other = f32[448,128]{1,0:T(8,128)S(1)} collective-permute-done((f32[448,128]{1,0:T(8,128)S(1)}, f32[448,128]{1,0:T(8,128)S(1)}, u32[]{:S(2)}, u32[]{:S(2)}) %collective-permute-start.3) | collective-permute-done | bytes 229408 | tf_op jit(solution)/shard_map/cond/branch_1_fun/ppermute | solution.py:376
  83.3 9.0 %all-to-all-done.3 = f32[16,7,4,128]{3,2,1,0:T(4,128)S(1)} async-done(((f32[16,7,4,128]{3,2,1,0:T(4,128)}), f32[16,7,4,128]{3,2,1,0:T(4,128)S(1)}, u32[]{:S(2)}, u32[]{:S(2)}) %all-to-all-start.3) | async-done | bytes 229408 | tf_op jit(solution)/shard_map/cond/branch_1_fun/all_to_all | solution.py:387
  92.3 2.9 %spread.5 = f32[2048,128]{1,0:T(8,128)} custom-call(s32[7]{0:T(128)S(1)} %get-tuple-element.146.place, s32[1]{0:T(128)} %get-tuple-element.147.rounds, s32[4,128]{1,0:T(4,128)S(1)} %get-tuple-element.148.slots, s32[512]{0:T(512)S(1)} %get-tuple-element.149.labels, s32[512]{0:T(512)S(1)} %get-tuple-element.150.orbital_s, s32[4,128]{1,0:T(4,128)S(1)} %bitcast.93, ...), custom_call_target="tpu_custom_call" | custom-call | tf_op jit(solution)/shard_map/cond/branch_1_fun/spread/pallas_call | solution.py:291
  (1 shorter events, 0.0 us)
Async XLA Ops:
  1.3 28.2 %all-to-all-start.9 = ((f32[16,4,384]{2,1,0:T(4,128)}), f32[16,4,384]{2,1,0:T(4,128)S(1)}, u32[]{:S(2)}, u32[]{:S(2)}) async-start(f32[16,4,384]{2,1,0:T(4,128)} %broadcast_in_dim.8), calls=%async_computation.9 | async-start | bytes 196608 | tf_op jit(solution)/shard_map/all_to_all | solution.py:313
  18.3 11.3 %copy-start = (s32[512]{0:T(512)S(1)}, s32[512]{0:T(512)}, u32[]{:S(2)}) copy-start(s32[512]{0:T(512)} %orbital_s.1) | copy-start | bytes 6148
  18.3 11.3 %copy-start.2 = (s32[3]{0:T(128)S(1)}, s32[3]{0:T(128)}, u32[]{:S(2)}) copy-start(s32[3]{0:T(128)} %slab.3) | copy-start | bytes 40
  18.4 28.6 %copy-start.1 = (s32[512]{0:T(512)S(1)}, s32[512]{0:T(512)}, u32[]{:S(2)}) copy-start(s32[512]{0:T(512)} %param.14) | copy-start | bytes 6148
  31.1 15.9 %all-to-all-start.10 = ((f32[8,24,384]{2,1,0:T(8,128)}), f32[8,24,384]{2,1,0:T(8,128)S(1)}, u32[]{:S(2)}, u32[]{:S(2)}) async-start(f32[8,24,384]{2,1,0:T(8,128)} %bitcast.48), calls=%async_computation.10 | async-start | bytes 589824 | tf_op jit(solution)/shard_map/all_to_all | solution.py:357
  50.3 3.7 %collective-permute-start.2 = (f32[896,128]{1,0:T(8,128)S(1)}, f32[896,128]{1,0:T(8,128)S(1)}, u32[]{:S(2)}, u32[]{:S(2)}) collective-permute-start(f32[896,128]{1,0:T(8,128)S(1)} %get-tuple-element.158), channel_id=1, source_target_pairs={{0,1},{1,0},{2,3},{3,2},{4,5},{5,4},{6,7},{7,6},{8,9},{9,8},{10,11... | collective-permute-start | bytes 1376264 | tf_op jit(solution)/shard_map/cond/branch_1_fun/ppermute | solution.py:368
  69.6 22.7 %all-to-all-start.3 = ((f32[16,7,4,128]{3,2,1,0:T(4,128)}), f32[16,7,4,128]{3,2,1,0:T(4,128)S(1)}, u32[]{:S(2)}, u32[]{:S(2)}) async-start(f32[16,7,4,128]{3,2,1,0:T(4,128)} %bitcast.11), calls=%async_computation.3 | async-start | bytes 458752 | tf_op jit(solution)/shard_map/cond/branch_1_fun/all_to_all | solution.py:387
  75.4 7.9 %collective-permute-start.3 = (f32[448,128]{1,0:T(8,128)S(1)}, f32[448,128]{1,0:T(8,128)S(1)}, u32[]{:S(2)}, u32[]{:S(2)}) collective-permute-start(f32[448,128]{1,0:T(8,128)S(1)} %get-tuple-element.160), channel_id=1, source_target_pairs={{0,2},{2,0},{1,3},{3,1},{4,6},{6,4},{5,7},{7,5},{8,10},{10,8},{9,1... | collective-permute-start | bytes 688136 | tf_op jit(solution)/shard_map/cond/branch_1_fun/ppermute | solution.py:376

commit v8 on v7

--- a/solution.py
+++ b/solution.py
@@ -193,16 +193,20 @@
                 rows.append(jnp.zeros((LANES - 4 * size, LANES), jnp.float32))
             at = (h * 2 + m) * LANES
             turned[at : at + LANES, :] = jnp.transpose(jnp.concatenate(rows, axis=0))
-    parts = []
-    for j in range(4):
-        for h in range(2):
-            for i in range(4):
-                parts.append(turned[pl.ds((h * 2 + i // 2) * LANES + i % 2 * 64 + j, 16, stride=4), :])
+
+    def part(row):
+        j, h, i = row // 8, row // 4 % 2, row % 4
+        return turned[pl.ds((h * 2 + i // 2) * LANES + i % 2 * 64 + j, 16, stride=4), :]
+
+    if size == SLOTS:
+        for row in range(size):
+            out[pl.ds(row, 16, stride=size), :] = part(row)
     for last, pieces in folded(size):
+        spread_out = part(last)
         for row, at in pieces:
-            parts[row] = jnp.where(lane < 4 * size, parts[row], pltpu.roll(parts[last], 4 * size - at, 1))
-    for row in range(size):
-        out[pl.ds(row, 16, stride=size), :] = parts[row]
+            out[pl.ds(row, 16, stride=size), :] = jnp.where(
+                lane < 4 * size, part(row), pltpu.roll(spread_out, 4 * size - at, 1)
+            )
 
 
 def spread_kernel(size, place, rounds, slots, labels, orbital_s, orbital, summed, other, swapped, *rest):
@@ -210,17 +214,22 @@
     held, outs = (rest[:2], rest[2:]) if size == SLOTS else ((), rest)
     block, occ, x = place[0], place[1], place[4]
     lane = iota((16, LANES), 1)
-    parts = [swapped[pl.ds(row, 16, stride=size), :] for row in range(size)]
+
+    def put(row, part):
+        j, h, i = row // 8, row // 4 % 2, row % 4
+        turned[pl.ds(j * LANES + h * 64 + i, 16, stride=4), :] = part
+
+    if size == SLOTS:
+        for row in range(size):
+            put(row, swapped[pl.ds(row, 16, stride=size), :])
     for last, pieces in folded(size):
         whole = None
         for row, at in pieces:
-            piece = pltpu.roll(parts[row], (at - 4 * size) % LANES, 1)
+            part = swapped[pl.ds(row, 16, stride=size), :]
+            put(row, part)
+            piece = pltpu.roll(part, (at - 4 * size) % LANES, 1)
             whole = piece if whole is None else jnp.where(lane < at, whole, piece)
-        parts.append(whole)
-    for j in range(4):
-        for h in range(2):
-            for i in range(4):
-                turned[pl.ds(j * LANES + h * 64 + i, 16, stride=4), :] = parts[j * 8 + h * 4 + i]
+        put(last, whole)
     mirrored = [jnp.transpose(turned[j * LANES : (j + 1) * LANES, :]) for j in range(4)]
     near = iota((size, LANES), 1) < 64
     for y in range(4):

time: 96.2 us -> 94 us (0.977)
  waiting for transfers between devices: 30.7 us -> 29.5 us
where the time goes in v8:
time: 94 us; the launch traced here: 93.4 us
  starting transfers between devices  32.4 us (34%)
  waiting for transfers between devices  29.5 us (31%)
  Pallas kernels  15.7 us (17%)
  blocking collectives  13.3 us (14%)
  local copies, waits for them, and re-layouts  1.48 us (2%)
    pallas_call x7, Pallas kernels, call(): pl.pallas_call(kernel, out_shape=out_shape, in_specs=[SMEM] * scalars + [...  15.7 us
    all_to_all x1, starting transfers between devices, on_device(): near = lax.all_to_all(mine, 'z', 0, 0, tiled=True).reshape(GROUP, DEPTH)  15.2 us
    all_to_all x1, blocking collectives, work(): lax.all_to_all(summed.reshape(16, 2 * size, LANES), ('y', 'xh', 'xl'), 0,...  13.3 us
    all_to_all x1, waiting for transfers between devices, gather(): lax.all_to_all(packed, ('y', 'xh'), 0, 0, tiled=True)  8.34 us
    all_to_all x1, waiting for transfers between devices, work(): lax.all_to_all(turned.reshape(16, size // tile, tile, LANES), 'z', 0, 0,...  8.21 us
    all_to_all x1, starting transfers between devices, gather(): lax.all_to_all(packed, ('y', 'xh'), 0, 0, tiled=True)  6.93 us
    all_to_all x1, waiting for transfers between devices, on_device(): near = lax.all_to_all(mine, 'z', 0, 0, tiled=True).reshape(GROUP, DEPTH)  6.2 us
    all_to_all x1, starting transfers between devices, work(): lax.all_to_all(turned.reshape(16, size // tile, tile, LANES), 'z', 0, 0,...  5.85 us
  transfers between devices with their start and end apart: 5, of which 5 were waited for; matrix products, arithmetic and copies ran while one was open for 0% of the time, Pallas kernels for 7%

profile of v8, /device:TPU:32, one launch (start us, length us, event | category | flops | bytes accessed | tf_op | source)
XLA Modules:
  0.0 93.4 jit_solution(11709275538572474515)
XLA Ops:
  0.0 1.3 %broadcast_in_dim.8 = f32[16,4,384]{2,1,0:T(4,128)} broadcast(f32[4,384]{1,0:T(4,128)} %bitcast.106), dimensions={1,2} | broadcast | bytes 104448 | tf_op jit(solution)/shard_map/broadcast_in_dim | solution.py:321
  1.3 15.2 %all-to-all-start.9 = ((f32[16,4,384]{2,1,0:T(4,128)}), f32[16,4,384]{2,1,0:T(4,128)S(1)}, u32[]{:S(2)}, u32[]{:S(2)}) async-start(f32[16,4,384]{2,1,0:T(4,128)} %broadcast_in_dim.8), calls=%async_computation.9 | async-start | bytes 196608 | tf_op jit(solution)/shard_map/all_to_all | solution.py:322
  16.6 0.1 stack.27.place
  16.6 1.7 %plan.2 = (s32[4,128]{1,0:T(4,128)S(1)}, s32[4,128]{1,0:T(4,128)S(1)}, s32[4,256]{1,0:T(4,128)S(1)}, s32[64,128]{1,0:T(8,128)S(1)}, s32[1]{0:T(128)}, /*index=5*/s32[1]{0:T(128)}) custom-call(s32[1]{0:T(128)} %constant.25.clone.1.turn, s32[7]{0:T(128)S(1)} %stack.27.place, s32[4,128]{1,0:T(4,128)} %bitcast.101), custom_call_target="tpu_custom_call" | custom-call | tf_op jit(solution)/shard_map/plan/pallas_call | solution.py:300
  18.3 0.0 copy-start
  18.3 0.0 copy-start.2
  18.4 0.0 copy-start.1
  18.4 5.0 %prepare.1 = (bf16[384,2048]{1,0:T(8,128)(2,1)}, bf16[384,2048]{1,0:T(8,128)(2,1)}) custom-call(s32[7]{0:T(128)S(1)} %stack.27.place, s32[3]{0:T(128)} %slab.3, s32[512]{0:T(512)} %orbital_s.1, s32[4,128]{1,0:T(4,128)} %bitcast.85, f32[6144,128]{1,0:T(8,128)} %bitcast.84), custom_call_target="tpu_custom_call" | custom-call | flops 8000000 | bytes 7000000 | tf_op jit(solution)/shard_map/prepare/pallas_call | solution.py:300
  23.4 6.2 %all-to-all-done.9 = f32[16,4,384]{2,1,0:T(4,128)S(1)} async-done(((f32[16,4,384]{2,1,0:T(4,128)}), f32[16,4,384]{2,1,0:T(4,128)S(1)}, u32[]{:S(2)}, u32[]{:S(2)}) %all-to-all-start.9) | async-done | bytes 98336 | tf_op jit(solution)/shard_map/all_to_all | solution.py:322
  29.6 0.0 copy-done
  29.6 0.0 copy-done.2
  29.6 1.5 %pack.2 = f32[192,384]{1,0:T(8,128)} custom-call(s32[7]{0:T(128)S(1)} %stack.27.place, s32[3]{0:T(128)S(1)} %copy-done.2, s32[4,128]{1,0:T(4,128)S(1)} %bitcast.86, s32[64,128]{1,0:T(8,128)S(1)} %get-tuple-element.230.mates, s32[4,128]{1,0:T(4,128)S(1)} %get-tuple-element.231.sent, f32[64,384]{1,0:T(8,128)S(1)} %reshape.103.near), custom_call_target="tpu_custom_call" | custom-call | tf_op jit(solution)/shard_map/pack/pallas_call | solution.py:300
  31.1 6.9 %all-to-all-start.10 = ((f32[8,24,384]{2,1,0:T(8,128)}), f32[8,24,384]{2,1,0:T(8,128)S(1)}, u32[]{:S(2)}, u32[]{:S(2)}) async-start(f32[8,24,384]{2,1,0:T(8,128)} %bitcast.48), calls=%async_computation.10 | async-start | bytes 589824 | tf_op jit(solution)/shard_map/all_to_all | solution.py:366
  38.7 8.3 %all-to-all-done.10 = f32[8,24,384]{2,1,0:T(8,128)S(1)} async-done(((f32[8,24,384]{2,1,0:T(8,128)}), f32[8,24,384]{2,1,0:T(8,128)S(1)}, u32[]{:S(2)}, u32[]{:S(2)}) %all-to-all-start.10) | async-done | bytes 294944 | tf_op jit(solution)/shard_map/all_to_all | solution.py:366
  47.0 0.0 copy-done.1
  47.0 46.3 %conditional.1 = (f32[128,4,512]{2,1,0:T(4,128)}) conditional(s32[]{:T(128)} %bitcast.42, (s32[7]{0:T(128)S(1)}, s32[3]{0:T(128)S(1)}, s32[4,128]{1,0:T(4,128)S(1)}, s32[4,256]{1,0:T(4,128)S(1)}, f32[192,384]{1,0:T(8,128)S(1)}, /*index=5*/bf16[384,2048]{1,0:T(8,128)(2,1)}, bf16[384,2048]{1,0:T(8,128)(2,1)}, s32[1]{0:T(128)}, ...), branch_computations={%region_0.0_spmd, %region_1.0_spmd, %region_2.0_spmd} | conditional | flops 2 | bytes 12648933 | solution.py:442
  47.0 3.1 %ladder.4 = (f32[768,128]{1,0:T(8,128)S(1)}, f32[768,128]{1,0:T(8,128)S(1)}) custom-call(s32[7]{0:T(128)S(1)} %get-tuple-element.130.place, s32[3]{0:T(128)S(1)} %get-tuple-element.137.slab, s32[4,128]{1,0:T(4,128)S(1)} %bitcast.90, s32[4,256]{1,0:T(4,128)S(1)} %get-tuple-element.138.targets, f32[192,384]{1,0:T(8,128)S(1)} %get-tuple-element.139.gathered, ...), custom_call_target="tpu_custom_call" | custom-call | tf_op jit(solution)/shard_map/cond/branch_0_fun/ladder/pallas_call | solution.py:300
  50.1 1.9 %collective-permute-start = (f32[768,128]{1,0:T(8,128)S(1)}, f32[768,128]{1,0:T(8,128)S(1)}, u32[]{:S(2)}, u32[]{:S(2)}) collective-permute-start(f32[768,128]{1,0:T(8,128)S(1)} %get-tuple-element.143), channel_id=1, source_target_pairs={{0,1},{1,0},{2,3},{3,2},{4,5},{5,4},{6,7},{7,6},{8,9},{9,8},{10,11... | collective-permute-start | bytes 1179656 | tf_op jit(solution)/shard_map/cond/branch_0_fun/ppermute | solution.py:377
  52.1 1.7 %collective-permute-done.arrived = f32[768,128]{1,0:T(8,128)S(1)} collective-permute-done((f32[768,128]{1,0:T(8,128)S(1)}, f32[768,128]{1,0:T(8,128)S(1)}, u32[]{:S(2)}, u32[]{:S(2)}) %collective-permute-start) | collective-permute-done | bytes 393248 | tf_op jit(solution)/shard_map/cond/branch_0_fun/ppermute | solution.py:377
  53.8 0.6 add.21
  54.4 13.3 %all_to_all.52 = f32[16,48,128]{2,1,0:T(8,128)S(1)} all-to-all(f32[16,48,128]{2,1,0:T(8,128)S(1)} %bitcast.77), channel_id=1, replica_groups=mesh['y'=4,'xh'=2,'z'=16,'xl'=2,'core'=2] {'y','xh','xl'}, dimensions={0} | all-to-all | bytes 786432 | tf_op jit(solution)/shard_map/cond/branch_0_fun/all_to_all | solution.py:386
  67.6 0.9 turn.4
  68.5 5.9 %all-to-all-start.1 = ((f32[16,3,8,128]{3,2,1,0:T(8,128)}), f32[16,3,8,128]{3,2,1,0:T(8,128)S(1)}, u32[]{:S(2)}, u32[]{:S(2)}) async-start(f32[16,3,8,128]{3,2,1,0:T(8,128)} %bitcast.2), calls=%async_computation.1 | async-start | bytes 393216 | tf_op jit(solution)/shard_map/cond/branch_0_fun/all_to_all | solution.py:396
  74.4 2.5 %collective-permute-start.1 = (f32[384,128]{1,0:T(8,128)S(1)}, f32[384,128]{1,0:T(8,128)S(1)}, u32[]{:S(2)}, u32[]{:S(2)}) collective-permute-start(f32[384,128]{1,0:T(8,128)S(1)} %get-tuple-element.145), channel_id=1, source_target_pairs={{0,2},{2,0},{1,3},{3,1},{4,6},{6,4},{5,7},{7,5},{8,10},{10,8},{9,1... | collective-permute-start | bytes 589832 | tf_op jit(solution)/shard_map/cond/branch_0_fun/ppermute | solution.py:385
  76.9 5.1 %collective-permute-done.1.other = f32[384,128]{1,0:T(8,128)S(1)} collective-permute-done((f32[384,128]{1,0:T(8,128)S(1)}, f32[384,128]{1,0:T(8,128)S(1)}, u32[]{:S(2)}, u32[]{:S(2)}) %collective-permute-start.1) | collective-permute-done | bytes 196640 | tf_op jit(solution)/shard_map/cond/branch_0_fun/ppermute | solution.py:385
  82.0 8.2 %all-to-all-done.1 = f32[16,3,8,128]{3,2,1,0:T(8,128)S(1)} async-done(((f32[16,3,8,128]{3,2,1,0:T(8,128)}), f32[16,3,8,128]{3,2,1,0:T(8,128)S(1)}, u32[]{:S(2)}, u32[]{:S(2)}) %all-to-all-start.1) | async-done | bytes 196640 | tf_op jit(solution)/shard_map/cond/branch_0_fun/all_to_all | solution.py:396
  90.2 2.9 %spread.4 = f32[2048,128]{1,0:T(8,128)} custom-call(s32[7]{0:T(128)S(1)} %get-tuple-element.130.place, s32[1]{0:T(128)} %get-tuple-element.132.rounds, s32[4,128]{1,0:T(4,128)S(1)} %get-tuple-element.133.slots, s32[512]{0:T(512)S(1)} %get-tuple-element.134.labels, s32[512]{0:T(512)S(1)} %get-tuple-element.135.orbital_s, s32[4,128]{1,0:T(4,128)S(1)} %bitcast.91, ...), custom_call_target="tpu_custom_call" | custom-call | tf_op jit(solution)/shard_map/cond/branch_0_fun/spread/pallas_call | solution.py:300
  (1 shorter events, 0.0 us)
Async XLA Ops:
  1.3 28.2 %all-to-all-start.9 = ((f32[16,4,384]{2,1,0:T(4,128)}), f32[16,4,384]{2,1,0:T(4,128)S(1)}, u32[]{:S(2)}, u32[]{:S(2)}) async-start(f32[16,4,384]{2,1,0:T(4,128)} %broadcast_in_dim.8), calls=%async_computation.9 | async-start | bytes 196608 | tf_op jit(solution)/shard_map/all_to_all | solution.py:322
  18.3 11.3 %copy-start = (s32[512]{0:T(512)S(1)}, s32[512]{0:T(512)}, u32[]{:S(2)}) copy-start(s32[512]{0:T(512)} %orbital_s.1) | copy-start | bytes 6148
  18.3 11.3 %copy-start.2 = (s32[3]{0:T(128)S(1)}, s32[3]{0:T(128)}, u32[]{:S(2)}) copy-start(s32[3]{0:T(128)} %slab.3) | copy-start | bytes 40
  18.4 28.6 %copy-start.1 = (s32[512]{0:T(512)S(1)}, s32[512]{0:T(512)}, u32[]{:S(2)}) copy-start(s32[512]{0:T(512)} %param.14) | copy-start | bytes 6148
  31.1 15.9 %all-to-all-start.10 = ((f32[8,24,384]{2,1,0:T(8,128)}), f32[8,24,384]{2,1,0:T(8,128)S(1)}, u32[]{:S(2)}, u32[]{:S(2)}) async-start(f32[8,24,384]{2,1,0:T(8,128)} %bitcast.48), calls=%async_computation.10 | async-start | bytes 589824 | tf_op jit(solution)/shard_map/all_to_all | solution.py:366
  50.1 3.6 %collective-permute-start = (f32[768,128]{1,0:T(8,128)S(1)}, f32[768,128]{1,0:T(8,128)S(1)}, u32[]{:S(2)}, u32[]{:S(2)}) collective-permute-start(f32[768,128]{1,0:T(8,128)S(1)} %get-tuple-element.143), channel_id=1, source_target_pairs={{0,1},{1,0},{2,3},{3,2},{4,5},{5,4},{6,7},{7,6},{8,9},{9,8},{10,11... | collective-permute-start | bytes 1179656 | tf_op jit(solution)/shard_map/cond/branch_0_fun/ppermute | solution.py:377
  68.5 21.6 %all-to-all-start.1 = ((f32[16,3,8,128]{3,2,1,0:T(8,128)}), f32[16,3,8,128]{3,2,1,0:T(8,128)S(1)}, u32[]{:S(2)}, u32[]{:S(2)}) async-start(f32[16,3,8,128]{3,2,1,0:T(8,128)} %bitcast.2), calls=%async_computation.1 | async-start | bytes 393216 | tf_op jit(solution)/shard_map/cond/branch_0_fun/all_to_all | solution.py:396
  74.4 7.6 %collective-permute-start.1 = (f32[384,128]{1,0:T(8,128)S(1)}, f32[384,128]{1,0:T(8,128)S(1)}, u32[]{:S(2)}, u32[]{:S(2)}) collective-permute-start(f32[384,128]{1,0:T(8,128)S(1)} %get-tuple-element.145), channel_id=1, source_target_pairs={{0,2},{2,0},{1,3},{3,1},{4,6},{6,4},{5,7},{7,5},{8,10},{10,8},{9,1... | collective-permute-start | bytes 589832 | tf_op jit(solution)/shard_map/cond/branch_0_fun/ppermute | solution.py:385

commit v9 on v8

--- a/solution.py
+++ b/solution.py
@@ -138,8 +138,8 @@
         for x in range(2):
             quarter = 2 * x + (core ^ half)
             pick = jnp.where(slot == targets[pl.ds(quarter, 1), : 8 * KEPT], 1.0, 0.0).astype(jnp.bfloat16)
-            first = gathered[pl.ds(pl.multiple_of(quarter * 2 * KEPT, 8), KEPT), :]
-            second = gathered[pl.ds(pl.multiple_of(quarter * 2 * KEPT + KEPT, 8), KEPT), :]
+            first = gathered[pl.ds(pl.multiple_of(quarter * KEPT, 8), KEPT), :]
+            second = gathered[pl.ds(pl.multiple_of((4 + quarter) * KEPT, 8), KEPT), :]
             second = jnp.concatenate([jnp.where(depth_row == l, second, 0.0) for l in range(8)], axis=0)
             if width > KEPT:
                 first = jnp.concatenate([first, jnp.zeros((width - KEPT, DEPTH), jnp.float32)], axis=0)
@@ -163,16 +163,16 @@
                 for x in range(2):
                     at = (half * 2 + x) * width
                     for h in range(2):
-                        to = (((y * 2 + h) * 2 + x) * 2 + m) * size
+                        to = (((h * 2 + x) * 4 + y) * 2 + m) * size
                         out[to : to + size, :] = cut[h][at : at + size]
 
 
 def add_kernel(size, place, keep, arrived, summed, other):
     x = place[4]
     summed[...] = keep[...] + arrived[...]
-    for block in range(8):
-        rows = pl.ds(pl.multiple_of((block * 2 + 1 - x) * 2 * size, 8), 2 * size)
-        other[block * 2 * size : (block + 1) * 2 * size, :] = summed[rows, :]
+    for h in range(2):
+        rows = pl.ds(pl.multiple_of((h * 2 + 1 - x) * 8 * size, 8), 8 * size)
+        other[h * 8 * size : (h + 1) * 8 * size, :] = summed[rows, :]
 
 
 def folded(size):
@@ -187,8 +187,8 @@
         for m in range(2):
             rows = []
             for y in range(4):
-                at = (y * 2 + h) * 4 * size + m * size
-                rows.append(arrived[at : at + size, :] + arrived[2 * size + at : 2 * size + at + size, :])
+                at = (h * 8 + y) * 2 * size + m * size
+                rows.append(arrived[at : at + size, :] + arrived[8 * size + at : 8 * size + at + size, :])
             if size < SLOTS:
                 rows.append(jnp.zeros((LANES - 4 * size, LANES), jnp.float32))
             at = (h * 2 + m) * LANES
@@ -236,8 +236,8 @@
         for m in range(2):
             cut = []
             for h in range(2):
-                at = (y * 2 + h) * 2 * size + m * size
-                mine = summed[pl.ds(pl.multiple_of(((y * 2 + h) * 2 + x) * 2 * size, 8), 2 * size), :]
+                at = (h * 4 + y) * 2 * size + m * size
+                mine = summed[pl.ds(pl.multiple_of(((h * 2 + x) * 4 + y) * 2 * size, 8), 2 * size), :]
                 cut.append(mine[m * size : (m + 1) * size] + other[at : at + size, :])
             own = (
                 jnp.where(near, cut[0], pltpu.roll(cut[1], 64, 1)),
@@ -270,7 +270,7 @@
             return carry
 
         for part in range(4):
-            lax.fori_loop(part * 32, part * 32 + 32, step, 0, unroll=8)
+            lax.fori_loop(part * 32, part * 32 + 32, step, 0, unroll=32)
             part_of(part).start()
 
     def fill_in():
@@ -363,7 +363,7 @@
             [place, slab_irrep, orbital, mates, sent, near],
         )
         packed = packed.reshape(8, KEPT, DEPTH)
-        return lax.all_to_all(packed, ("y", "xh"), 0, 0, tiled=True).reshape(8 * KEPT, DEPTH)
+        return lax.all_to_all(packed, ("xh", "y"), 0, 0, tiled=True).reshape(8 * KEPT, DEPTH)
 
     def work(size, targets, gathered):
         keep, send = call(
@@ -383,7 +383,7 @@
             [place, keep, arrived],
         )
         other = lax.ppermute(other, "xl", [(0, 1), (1, 0)])
-        traded = lax.all_to_all(summed.reshape(16, 2 * size, LANES), ("y", "xh", "xl"), 0, 0, tiled=True)
+        traded = lax.all_to_all(summed.reshape(16, 2 * size, LANES), ("xh", "xl", "y"), 0, 0, tiled=True)
         turned = call(
             functools.partial(turn_kernel, size),
             "turn",

time: 94 us -> 95.7 us (1.018)
  waiting for transfers between devices: 29.5 us -> 31 us
where the time goes in v9:
time: 95.7 us; the launch traced here: 95.2 us
  starting transfers between devices  31.8 us (33%)
  waiting for transfers between devices  31 us (32%)
  Pallas kernels  15.8 us (17%)
  blocking collectives  14 us (15%)
  local copies, waits for them, and re-layouts  1.48 us (2%)
    pallas_call x7, Pallas kernels, call(): pl.pallas_call(kernel, out_shape=out_shape, in_specs=[SMEM] * scalars + [...  15.8 us
    all_to_all x1, starting transfers between devices, on_device(): near = lax.all_to_all(mine, 'z', 0, 0, tiled=True).reshape(GROUP, DEPTH)  15.2 us
    all_to_all x1, blocking collectives, work(): lax.all_to_all(summed.reshape(16, 2 * size, LANES), ('xh', 'xl', 'y'), 0,...  14 us
    all_to_all x1, waiting for transfers between devices, work(): lax.all_to_all(turned.reshape(16, size // tile, tile, LANES), 'z', 0, 0,...  8.78 us
    all_to_all x1, waiting for transfers between devices, gather(): lax.all_to_all(packed, ('xh', 'y'), 0, 0, tiled=True)  8.24 us
    all_to_all x1, starting transfers between devices, gather(): lax.all_to_all(packed, ('xh', 'y'), 0, 0, tiled=True)  6.93 us
    all_to_all x1, waiting for transfers between devices, on_device(): near = lax.all_to_all(mine, 'z', 0, 0, tiled=True).reshape(GROUP, DEPTH)  6.2 us
    ppermute x1, waiting for transfers between devices, work(): other = lax.ppermute(other, 'xl', [(0, 1), (1, 0)])  5.99 us
  transfers between devices with their start and end apart: 5, of which 5 were waited for; matrix products, arithmetic and copies ran while one was open for 0% of the time, Pallas kernels for 7%

profile of v9, /device:TPU:32, one launch (start us, length us, event | category | flops | bytes accessed | tf_op | source)
XLA Modules:
  0.0 95.2 jit_solution(7295271146219244683)
XLA Ops:
  0.0 1.3 %broadcast_in_dim.8 = f32[16,4,384]{2,1,0:T(4,128)} broadcast(f32[4,384]{1,0:T(4,128)} %bitcast.106), dimensions={1,2} | broadcast | bytes 104448 | tf_op jit(solution)/shard_map/broadcast_in_dim | solution.py:321
  1.3 15.2 %all-to-all-start.9 = ((f32[16,4,384]{2,1,0:T(4,128)}), f32[16,4,384]{2,1,0:T(4,128)S(1)}, u32[]{:S(2)}, u32[]{:S(2)}) async-start(f32[16,4,384]{2,1,0:T(4,128)} %broadcast_in_dim.8), calls=%async_computation.9 | async-start | bytes 196608 | tf_op jit(solution)/shard_map/all_to_all | solution.py:322
  16.6 0.1 stack.27.place
  16.6 1.7 %plan.2 = (s32[4,128]{1,0:T(4,128)S(1)}, s32[4,128]{1,0:T(4,128)S(1)}, s32[4,256]{1,0:T(4,128)S(1)}, s32[64,128]{1,0:T(8,128)S(1)}, s32[1]{0:T(128)}, /*index=5*/s32[1]{0:T(128)}) custom-call(s32[1]{0:T(128)} %constant.25.clone.1.turn, s32[7]{0:T(128)S(1)} %stack.27.place, s32[4,128]{1,0:T(4,128)} %bitcast.101), custom_call_target="tpu_custom_call" | custom-call | tf_op jit(solution)/shard_map/plan/pallas_call | solution.py:300
  18.3 0.0 copy-start
  18.3 0.0 copy-start.2
  18.4 0.0 copy-start.1
  18.4 5.0 %prepare.1 = (bf16[384,2048]{1,0:T(8,128)(2,1)}, bf16[384,2048]{1,0:T(8,128)(2,1)}) custom-call(s32[7]{0:T(128)S(1)} %stack.27.place, s32[3]{0:T(128)} %slab.3, s32[512]{0:T(512)} %orbital_s.1, s32[4,128]{1,0:T(4,128)} %bitcast.85, f32[6144,128]{1,0:T(8,128)} %bitcast.84), custom_call_target="tpu_custom_call" | custom-call | flops 8000000 | bytes 7000000 | tf_op jit(solution)/shard_map/prepare/pallas_call | solution.py:300
  23.4 6.2 %all-to-all-done.9 = f32[16,4,384]{2,1,0:T(4,128)S(1)} async-done(((f32[16,4,384]{2,1,0:T(4,128)}), f32[16,4,384]{2,1,0:T(4,128)S(1)}, u32[]{:S(2)}, u32[]{:S(2)}) %all-to-all-start.9) | async-done | bytes 98336 | tf_op jit(solution)/shard_map/all_to_all | solution.py:322
  29.6 0.0 copy-done
  29.6 0.0 copy-done.2
  29.6 1.5 %pack.2 = f32[192,384]{1,0:T(8,128)} custom-call(s32[7]{0:T(128)S(1)} %stack.27.place, s32[3]{0:T(128)S(1)} %copy-done.2, s32[4,128]{1,0:T(4,128)S(1)} %bitcast.86, s32[64,128]{1,0:T(8,128)S(1)} %get-tuple-element.230.mates, s32[4,128]{1,0:T(4,128)S(1)} %get-tuple-element.231.sent, f32[64,384]{1,0:T(8,128)S(1)} %reshape.103.near), custom_call_target="tpu_custom_call" | custom-call | tf_op jit(solution)/shard_map/pack/pallas_call | solution.py:300
  31.1 6.9 %all-to-all-start.10 = ((f32[8,24,384]{2,1,0:T(8,128)}), f32[8,24,384]{2,1,0:T(8,128)S(1)}, u32[]{:S(2)}, u32[]{:S(2)}) async-start(f32[8,24,384]{2,1,0:T(8,128)} %bitcast.48), calls=%async_computation.10 | async-start | bytes 589824 | tf_op jit(solution)/shard_map/all_to_all | solution.py:366
  38.7 8.2 %all-to-all-done.10 = f32[8,24,384]{2,1,0:T(8,128)S(1)} async-done(((f32[8,24,384]{2,1,0:T(8,128)}), f32[8,24,384]{2,1,0:T(8,128)S(1)}, u32[]{:S(2)}, u32[]{:S(2)}) %all-to-all-start.10) | async-done | bytes 294944 | tf_op jit(solution)/shard_map/all_to_all | solution.py:366
  46.9 0.0 copy-done.1
  46.9 48.1 %conditional.1 = (f32[128,4,512]{2,1,0:T(4,128)}) conditional(s32[]{:T(128)} %bitcast.42, (s32[7]{0:T(128)S(1)}, s32[3]{0:T(128)S(1)}, s32[4,128]{1,0:T(4,128)S(1)}, s32[4,256]{1,0:T(4,128)S(1)}, f32[192,384]{1,0:T(8,128)S(1)}, /*index=5*/bf16[384,2048]{1,0:T(8,128)(2,1)}, bf16[384,2048]{1,0:T(8,128)(2,1)}, s32[1]{0:T(128)}, ...), branch_computations={%region_0.0_spmd, %region_1.0_spmd, %region_2.0_spmd} | conditional | flops 2 | bytes 12648933 | solution.py:442
  46.9 3.3 %ladder.5 = (f32[896,128]{1,0:T(8,128)S(1)}, f32[896,128]{1,0:T(8,128)S(1)}) custom-call(s32[7]{0:T(128)S(1)} %get-tuple-element.146.place, s32[3]{0:T(128)S(1)} %get-tuple-element.152.slab, s32[4,128]{1,0:T(4,128)S(1)} %bitcast.92, s32[4,256]{1,0:T(4,128)S(1)} %get-tuple-element.153.targets, f32[192,384]{1,0:T(8,128)S(1)} %get-tuple-element.154.gathered, ...), custom_call_target="tpu_custom_call" | custom-call | tf_op jit(solution)/shard_map/cond/branch_1_fun/ladder/pallas_call | solution.py:300
  50.2 1.9 %collective-permute-start.2 = (f32[896,128]{1,0:T(8,128)S(1)}, f32[896,128]{1,0:T(8,128)S(1)}, u32[]{:S(2)}, u32[]{:S(2)}) collective-permute-start(f32[896,128]{1,0:T(8,128)S(1)} %get-tuple-element.158), channel_id=1, source_target_pairs={{0,1},{1,0},{2,3},{3,2},{4,5},{5,4},{6,7},{7,6},{8,9},{9,8},{10,11... | collective-permute-start | bytes 1376264 | tf_op jit(solution)/shard_map/cond/branch_1_fun/ppermute | solution.py:377
  52.1 1.8 %collective-permute-done.2.arrived = f32[896,128]{1,0:T(8,128)S(1)} collective-permute-done((f32[896,128]{1,0:T(8,128)S(1)}, f32[896,128]{1,0:T(8,128)S(1)}, u32[]{:S(2)}, u32[]{:S(2)}) %collective-permute-start.2) | collective-permute-done | bytes 458784 | tf_op jit(solution)/shard_map/cond/branch_1_fun/ppermute | solution.py:377
  53.9 0.6 add.22
  54.5 14.0 %all_to_all.53 = f32[16,56,128]{2,1,0:T(8,128)S(1)} all-to-all(f32[16,56,128]{2,1,0:T(8,128)S(1)} %bitcast.74), channel_id=1, replica_groups=mesh['y'=4,'xh'=2,'z'=16,'xl'=2,'core'=2] {'xh','xl','y'}, dimensions={0} | all-to-all | bytes 917504 | tf_op jit(solution)/shard_map/cond/branch_1_fun/all_to_all | solution.py:386
  68.5 0.9 turn.5
  69.4 5.9 %all-to-all-start.3 = ((f32[16,7,4,128]{3,2,1,0:T(4,128)}), f32[16,7,4,128]{3,2,1,0:T(4,128)S(1)}, u32[]{:S(2)}, u32[]{:S(2)}) async-start(f32[16,7,4,128]{3,2,1,0:T(4,128)} %bitcast.11), calls=%async_computation.3 | async-start | bytes 458752 | tf_op jit(solution)/shard_map/cond/branch_1_fun/all_to_all | solution.py:396
  75.3 1.9 %collective-permute-start.3 = (f32[448,128]{1,0:T(8,128)S(1)}, f32[448,128]{1,0:T(8,128)S(1)}, u32[]{:S(2)}, u32[]{:S(2)}) collective-permute-start(f32[448,128]{1,0:T(8,128)S(1)} %get-tuple-element.160), channel_id=1, source_target_pairs={{0,2},{2,0},{1,3},{3,1},{4,6},{6,4},{5,7},{7,5},{8,10},{10,8},{9,1... | collective-permute-start | bytes 688136 | tf_op jit(solution)/shard_map/cond/branch_1_fun/ppermute | solution.py:385
  77.2 6.0 %collective-permute-done.3.other = f32[448,128]{1,0:T(8,128)S(1)} collective-permute-done((f32[448,128]{1,0:T(8,128)S(1)}, f32[448,128]{1,0:T(8,128)S(1)}, u32[]{:S(2)}, u32[]{:S(2)}) %collective-permute-start.3) | collective-permute-done | bytes 229408 | tf_op jit(solution)/shard_map/cond/branch_1_fun/ppermute | solution.py:385
  83.2 8.8 %all-to-all-done.3 = f32[16,7,4,128]{3,2,1,0:T(4,128)S(1)} async-done(((f32[16,7,4,128]{3,2,1,0:T(4,128)}), f32[16,7,4,128]{3,2,1,0:T(4,128)S(1)}, u32[]{:S(2)}, u32[]{:S(2)}) %all-to-all-start.3) | async-done | bytes 229408 | tf_op jit(solution)/shard_map/cond/branch_1_fun/all_to_all | solution.py:396
  92.0 2.8 %spread.5 = f32[2048,128]{1,0:T(8,128)} custom-call(s32[7]{0:T(128)S(1)} %get-tuple-element.146.place, s32[1]{0:T(128)} %get-tuple-element.147.rounds, s32[4,128]{1,0:T(4,128)S(1)} %get-tuple-element.148.slots, s32[512]{0:T(512)S(1)} %get-tuple-element.149.labels, s32[512]{0:T(512)S(1)} %get-tuple-element.150.orbital_s, s32[4,128]{1,0:T(4,128)S(1)} %bitcast.93, ...), custom_call_target="tpu_custom_call" | custom-call | tf_op jit(solution)/shard_map/cond/branch_1_fun/spread/pallas_call | solution.py:300
  (1 shorter events, 0.0 us)
Async XLA Ops:
  1.3 28.2 %all-to-all-start.9 = ((f32[16,4,384]{2,1,0:T(4,128)}), f32[16,4,384]{2,1,0:T(4,128)S(1)}, u32[]{:S(2)}, u32[]{:S(2)}) async-start(f32[16,4,384]{2,1,0:T(4,128)} %broadcast_in_dim.8), calls=%async_computation.9 | async-start | bytes 196608 | tf_op jit(solution)/shard_map/all_to_all | solution.py:322
  18.3 11.3 %copy-start = (s32[512]{0:T(512)S(1)}, s32[512]{0:T(512)}, u32[]{:S(2)}) copy-start(s32[512]{0:T(512)} %orbital_s.1) | copy-start | bytes 6148
  18.3 11.3 %copy-start.2 = (s32[3]{0:T(128)S(1)}, s32[3]{0:T(128)}, u32[]{:S(2)}) copy-start(s32[3]{0:T(128)} %slab.3) | copy-start | bytes 40
  18.4 28.5 %copy-start.1 = (s32[512]{0:T(512)S(1)}, s32[512]{0:T(512)}, u32[]{:S(2)}) copy-start(s32[512]{0:T(512)} %param.14) | copy-start | bytes 6148
  31.1 15.8 %all-to-all-start.10 = ((f32[8,24,384]{2,1,0:T(8,128)}), f32[8,24,384]{2,1,0:T(8,128)S(1)}, u32[]{:S(2)}, u32[]{:S(2)}) async-start(f32[8,24,384]{2,1,0:T(8,128)} %bitcast.48), calls=%async_computation.10 | async-start | bytes 589824 | tf_op jit(solution)/shard_map/all_to_all | solution.py:366
  50.2 3.7 %collective-permute-start.2 = (f32[896,128]{1,0:T(8,128)S(1)}, f32[896,128]{1,0:T(8,128)S(1)}, u32[]{:S(2)}, u32[]{:S(2)}) collective-permute-start(f32[896,128]{1,0:T(8,128)S(1)} %get-tuple-element.158), channel_id=1, source_target_pairs={{0,1},{1,0},{2,3},{3,2},{4,5},{5,4},{6,7},{7,6},{8,9},{9,8},{10,11... | collective-permute-start | bytes 1376264 | tf_op jit(solution)/shard_map/cond/branch_1_fun/ppermute | solution.py:377
  69.4 22.5 %all-to-all-start.3 = ((f32[16,7,4,128]{3,2,1,0:T(4,128)}), f32[16,7,4,128]{3,2,1,0:T(4,128)S(1)}, u32[]{:S(2)}, u32[]{:S(2)}) async-start(f32[16,7,4,128]{3,2,1,0:T(4,128)} %bitcast.11), calls=%async_computation.3 | async-start | bytes 458752 | tf_op jit(solution)/shard_map/cond/branch_1_fun/all_to_all | solution.py:396
  75.3 7.9 %collective-permute-start.3 = (f32[448,128]{1,0:T(8,128)S(1)}, f32[448,128]{1,0:T(8,128)S(1)}, u32[]{:S(2)}, u32[]{:S(2)}) collective-permute-start(f32[448,128]{1,0:T(8,128)S(1)} %get-tuple-element.160), channel_id=1, source_target_pairs={{0,2},{2,0},{1,3},{3,1},{4,6},{6,4},{5,7},{7,5},{8,10},{10,8},{9,1... | collective-permute-start | bytes 688136 | tf_op jit(solution)/shard_map/cond/branch_1_fun/ppermute | solution.py:385
